TPU v7x, 32 devices: a whole 2x2x4 slice. The times are simulated.
32 devices in a mesh: vol: 2 (over x), row: 4 (over y, core), col: 4 (over z).
Axes of the slice: x: 2, y: 2, z: 4, core: 2. Of those that a mesh axis runs over, the one named last changes fastest.
Arguments:
- source: float32 [16, 16, 32, 512], P(None, 'vol', 'row', 'col'), may hold values from -8 to 8
- labels: int32 [16, 32, 512], P('vol', 'row', 'col'), may hold values from 0 to 7
- region_coeff: float32 [8], replicated, may hold values from 0.3 to 3
- node_cell: int32 [4096], P(('vol', 'row', 'col')), may hold values from 0 to 8191
- node_pos: float32 [3, 4096], P(None, ('vol', 'row', 'col')), may hold values from 0 to 1
- incident: float32 [16, 4096], P(None, ('vol', 'row', 'col')), may hold values from -6 to 6
Outputs:
- field: float32 [16, 16, 32, 512], P(None, 'vol', 'row', 'col')
- flux: float32 [16, 4096], P(None, ('vol', 'row', 'col'))
Inputs may be any that keep to these rules, and one draw needn't show every extreme that they name: `node_cell`: cell of node j inside its volume block, several nodes may share a cell.
All inputs are finite; a program needn't handle non-finite values.
Results may differ from a plain program's by a relative error of at most 0.0029.
Values may be sent and summed in bfloat16 or wider, within the bound.
No kernel may reach another device: no remote copies, remote signals or barrier semaphores. Data moves between devices by JAX's collectives and lax.ppermute only.
A program may use at most 64 MiB of HBM per device.

v0:
```python
import functools
import math

import jax
import jax.numpy as jnp
from jax import lax
from jax.experimental import pallas as pl
from jax.experimental.pallas import tpu as pltpu
from jax.sharding import PartitionSpec as P

SWEEPS = 4
ITERS = 2

MASS_TERM = 0.05
SOFTENING = 0.05
KERNEL_GAIN = 2.0

HALO = SWEEPS
RHS_HALO = SWEEPS - 1
STRIP = 2 * HALO
AXES = ("vol", "row", "col")
F32, BF16 = jnp.float32, jnp.bfloat16
NT = (((1,), (1,)), ((), ()))


def sweep_weights(count):
    return [
        1.0 / (1.05 - 0.95 * math.cos(math.pi * (2 * sweep + 1) / (2 * count)))
        for sweep in range(count)
    ]


def iota(shape, dim):
    return lax.broadcasted_iota(jnp.int32, shape, dim)


def kernel_call(body, out_shape, scratch=(), smem=0, operands=(), name=None):
    specs = [pl.BlockSpec(memory_space=pltpu.SMEM)] * smem
    specs += [pl.BlockSpec(memory_space=pltpu.VMEM)] * (len(operands) - smem)
    return pl.pallas_call(
        body,
        out_shape=out_shape,
        in_specs=specs,
        out_specs=jax.tree.map(lambda _: pl.BlockSpec(memory_space=pltpu.VMEM), out_shape),
        scratch_shapes=list(scratch),
        compiler_params=pltpu.CompilerParams(vmem_limit_bytes=56 * 1024 * 1024),
        name=name,
    )(*operands)


def pick(refs, low, even, rows, size):
    first = refs[0][pl.ds(rows, size), :]
    second = refs[1][pl.ds(rows, size), :] if len(refs) > 1 else jnp.zeros_like(first)
    flag = jnp.full(first.shape, even, jnp.int32).astype(first.dtype)
    mine, other = (1 - flag, flag) if low else (flag, 1 - flag)
    return first * mine + second * other


def exchange(array, axis, arrays=None):
    count = lax.axis_size(axis)
    arrays = arrays or [array] * 2
    out = []
    for which in range(2 if count > 2 else 1):
        pairs = []
        for i in range(which, count - 1, 2):
            pairs += [(i, i + 1), (i + 1, i)]
        out.append(lax.ppermute(arrays[which], axis, pairs))
    return out


def edge_picker(cz, lanes):
    z, lane = iota((cz, lanes), 0), iota((cz, lanes), 1)
    k = lane % STRIP
    wanted = jnp.where(k < HALO, HALO - 1 - k, cz - 1 - k + HALO)
    return (z == wanted).astype(F32), lane // STRIP - HALO


def strip_rows(read, cx, cy, cz):
    base, lane_y = edge_picker(cz, cz)
    total = None
    for y in range(cy):
        rows = jnp.concatenate([read(x, y).astype(BF16) for x in range(cx)], axis=0)
        picked = jnp.where(lane_y == y, base, 0.0).astype(BF16)
        part = jnp.dot(rows, picked, preferred_element_type=F32)
        total = part if total is None else total + part
    return total.astype(BF16)


def first_kernel(dims, source, labels, incident, cells, rhs_out, send_out, left):
    cx, cy, cz, ch, nodes = dims
    cell = cells[...]
    row, z = cell // cz, cell % cz
    hits = (iota((cz, nodes), 0) == z).astype(BF16)
    flux = incident[...]
    top = flux.astype(BF16).astype(F32)
    rest = flux - top
    for r in range(cx * cy):
        here = jnp.broadcast_to(row == r, (ch, nodes))
        left[r * ch:(r + 1) * ch, :nodes] = jnp.where(here, top, 0.0).astype(BF16)
        left[r * ch:(r + 1) * ch, nodes:] = jnp.where(here, rest, 0.0).astype(BF16)
    added = lax.dot_general(
        left[...], jnp.concatenate([hits, hits], axis=1), NT, preferred_element_type=F32
    )
    rhs_out[...] = added
    for r in range(cx * cy):
        rhs_out[r * ch:(r + 1) * ch, :] += source[pl.ds(r, ch, stride=cx * cy), :]

    def read(x, y):
        start = (x * cy + y) * ch
        return rhs_out[start:start + ch, :]

    send_out[:cx * ch, :] = strip_rows(read, cx, cy, cz)
    base, lane_y = edge_picker(cz, cz)
    codes = (labels[...] + 1).astype(F32).astype(BF16)
    strips = jnp.dot(codes, base.astype(BF16), preferred_element_type=F32)
    own = (iota(strips.shape, 0) % cy) == lane_y[:1, :]
    strips = jnp.where(own, strips, 0.0).reshape(cx, cy, cz).sum(axis=1)
    send_out[cx * ch:, :] = jnp.concatenate(
        [strips, jnp.zeros((16 - cx, cz), F32)], axis=0
    ).astype(BF16)


def second_kernel(dims, width, with_labels, nz, nx, place, *refs):
    cx, cy, cz, ch, nodes = dims
    main, refs = refs[0], refs[1:]
    if with_labels:
        labels, refs = refs[0], refs[1:]
    zrecv, refs = refs[:nz], refs[nz:]
    strip_out, sends, refs = refs[0], refs[1:1 + nx], refs[1 + nx:]
    even_x = 1 - place[0] % 2
    even_z = 1 - place[2] % 2
    rows = cx * ch + (16 if with_labels else 0)
    lane = iota((rows, cz), 1)
    upper = pick(zrecv, False, even_z, 0, rows)
    lower = pick(zrecv, True, even_z, 0, rows)
    strip_out[...] = jnp.where(
        lane % STRIP < HALO, upper.astype(F32), lower.astype(F32)
    ).astype(BF16)
    if with_labels:
        (codes,) = refs
        codes[...] = jnp.zeros_like(codes)
        codes[:16, :] = strip_out[cx * ch:, :].astype(F32)
    slab = width * cy * ch
    for which in range(nx):
        upward = even_x if which == 0 else 1 - even_x
        x0 = upward * (cx - width)
        send = sends[which]
        send[:slab, :] = main[pl.ds(pl.multiple_of(x0 * (cy * ch), 16), slab), :].astype(BF16)
        send[slab:slab + width * ch, :] = strip_out[
            pl.ds(pl.multiple_of(x0 * ch, 16), width * ch), :
        ]
        if with_labels:
            start = slab + width * ch
            x0 = upward * (cx - HALO)
            send[start:start + HALO * cy, :] = (
                labels[pl.ds(pl.multiple_of(x0 * cy, 8), HALO * cy), :] + 1
            ).astype(F32).astype(BF16)
            send[start + HALO * cy:, :] = codes[pl.ds(x0, 16), :].astype(BF16)


def third_kernel(dims, width, with_labels, nx, ny, place, *refs):
    cx, cy, cz, ch, nodes = dims
    main, refs = refs[0], refs[1:]
    if with_labels:
        labels, refs = refs[0], refs[1:]
    strip, refs = refs[0], refs[1:]
    xrecv, refs = refs[:nx], refs[nx:]
    sends, refs = refs[:ny], refs[ny:]
    even_x = 1 - place[0] % 2
    even_y = 1 - place[1] % 2
    ex = cx + 2 * width
    slab = width * cy * ch
    if with_labels:
        codes, strip_codes, picked = refs
        fill_codes(dims, labels, strip, xrecv, slab + width * ch, even_x, codes, strip_codes)
    for which in range(ny):
        send = sends[which]
        upward = even_y if which == 0 else 1 - even_y
        y0 = upward * (cy - width)
        size = width * ch
        for x in range(ex):
            if width <= x < width + cx:
                start = pl.multiple_of(((x - width) * cy + y0) * ch, 16)
                piece = main[pl.ds(start, size), :].astype(BF16)
            else:
                low = x < width
                start = pl.multiple_of(((x if low else x - width - cx) * cy + y0) * ch, 16)
                piece = pick(xrecv, low, even_x, start, size)
            send[x * size:(x + 1) * size, :] = piece
        start = ex * size
        send[start:start + width * ch, :] = pick(xrecv, True, even_x, slab, width * ch)
        send[start + width * ch:start + (width + cx) * ch, :] = strip[:cx * ch, :]
        send[start + (width + cx) * ch:start + ex * ch, :] = pick(
            xrecv, False, even_x, slab, width * ch
        )
        if with_labels:
            start += ex * ch
            y0 = upward * (cy - HALO)
            tall = cx + 2 * HALO
            for x in range(tall):
                picked[x * HALO:(x + 1) * HALO, :] = codes[pl.ds(x * cy + y0, HALO), :]
            send[start:start + tall * HALO, :] = picked[...].astype(BF16)
            send[start + tall * HALO:, :] = strip_codes[...].astype(BF16)


def fill_codes(dims, labels, strip, xrecv, start, even_x, codes, strip_codes):
    cx, cy, cz, ch, nodes = dims
    side = HALO * cy
    codes[:side, :] = pick(xrecv, True, even_x, start, side).astype(F32)
    codes[side:side + cx * cy, :] = (labels[...] + 1).astype(F32)
    codes[side + cx * cy:, :] = pick(xrecv, False, even_x, start, side).astype(F32)
    strip_codes[:HALO, :] = pick(xrecv, True, even_x, start + side, 16).astype(F32)[:HALO]
    strip_codes[HALO:HALO + cx, :] = strip[cx * ch:cx * ch + 16, :].astype(F32)[:cx]
    strip_codes[HALO + cx:, :] = pick(xrecv, False, even_x, start + side, 16).astype(F32)[:HALO]


def assemble(dims, width, main, strip, xrecv, yrecv, even_x, even_y, out, out_strip):
    cx, cy, cz, ch, nodes = dims
    ex = cx + 2 * width
    out[HALO:HALO + cx, HALO:HALO + cy] = main[...].reshape(cx, cy, ch, cz)
    slab = width * cy * ch
    low = pick(xrecv, True, even_x, 0, slab).astype(F32)
    out[HALO - width:HALO, HALO:HALO + cy] = low.reshape(width, cy, ch, cz)
    high = pick(xrecv, False, even_x, 0, slab).astype(F32)
    out[HALO + cx:HALO + cx + width, HALO:HALO + cy] = high.reshape(width, cy, ch, cz)
    size = ex * width * ch
    low = pick(yrecv, True, even_y, 0, size).astype(F32)
    out[HALO - width:HALO + cx + width, HALO - width:HALO] = low.reshape(ex, width, ch, cz)
    high = pick(yrecv, False, even_y, 0, size).astype(F32)
    out[HALO - width:HALO + cx + width, HALO + cy:HALO + cy + width] = high.reshape(
        ex, width, ch, cz
    )
    own = jnp.concatenate(
        [
            pick(xrecv, True, even_x, slab, width * ch),
            strip[:cx * ch, :],
            pick(xrecv, False, even_x, slab, width * ch),
        ],
        axis=0,
    ).astype(F32)
    low = pick(yrecv, True, even_y, size, ex * ch).astype(F32)
    high = pick(yrecv, False, even_y, size, ex * ch).astype(F32)
    full = join_strips(own, low, high, cy)
    out_strip[HALO - width:HALO + cx + width] = full.reshape(ex, ch, cz)


def join_strips(own, low, high, cy):
    lane = iota(own.shape, 1)
    shift = cy * STRIP
    lanes = own.shape[1]
    low = pltpu.roll(low, lanes - shift, 1)
    high = pltpu.roll(high, shift, 1)
    return jnp.where(
        lane < HALO * STRIP, low, jnp.where(lane < (HALO + cy) * STRIP, own, high)
    )


def sweep(dims, reach, weight, src, src_strip, dst, dst_strip, r, r_strip, c, c_strip):
    cx, cy, cz, ch, nodes = dims
    lane = iota((ch, cz), 1)
    first, last = lane == 0, lane == cz - 1

    def spread(ref, k, x, y):
        return jnp.broadcast_to(ref[k, x, y:y + 1, :], (ch, cz))

    def column(x, _):
        beyond = src_strip[x]
        for y in range(HALO - reach, HALO + cy + reach):
            here = src[x, y]
            ends = pltpu.roll(beyond, (2 * cz - (y * STRIP + HALO)) % cz, 1)
            above = jnp.where(last, ends, pltpu.roll(here, cz - 1, 1))
            below = jnp.where(first, ends, pltpu.roll(here, 1, 1))
            total = r[x, y] - here
            total += spread(c, 0, x, y) * src[x + 1, y]
            total += spread(c, 1, x, y) * src[x - 1, y]
            total += spread(c, 2, x, y) * src[x, y + 1]
            total += spread(c, 3, x, y) * src[x, y - 1]
            total += spread(c, 4, x, y) * above
            total += spread(c, 5, x, y) * below
            dst[x, y] = here + weight * total
        return _

    lax.fori_loop(HALO - reach, HALO + cx + reach, column, 0)
    if reach == 0:
        return

    k = lane % STRIP
    group = lane // STRIP
    touching = (k == HALO) | (k == HALO - 1)

    def strip_column(x, _):
        here = src_strip[x]
        ends = jnp.zeros_like(here)
        for y in range(HALO - reach + 1, HALO + cy + reach - 1):
            moved = pltpu.roll(src[x, y], (y * STRIP + HALO) % cz, 1)
            ends = jnp.where(touching & (group == y), moved, ends)

        def spread_strip(k):
            return jnp.broadcast_to(c_strip[k, pl.ds(x, 1), :], (ch, cz))

        above = jnp.where(k == HALO, ends, pltpu.roll(here, 1, 1))
        below = jnp.where(k == HALO - 1, ends, pltpu.roll(here, cz - 1, 1))
        total = r_strip[x] - here
        total += spread_strip(0) * src_strip[x + 1]
        total += spread_strip(1) * src_strip[x - 1]
        total += spread_strip(2) * pltpu.roll(here, cz - STRIP, 1)
        total += spread_strip(3) * pltpu.roll(here, STRIP, 1)
        total += spread_strip(4) * above
        total += spread_strip(5) * below
        dst_strip[x] = here + weight * total
        return _

    lax.fori_loop(HALO - reach + 1, HALO + cx + reach - 1, strip_column, 0)


def coefficients(dims, kc, kc_strip, c, c_strip):
    cx, cy, cz, ch, nodes = dims
    tx, ty = cx + 2 * HALO, cy + 2 * HALO
    lane = iota((ty, cz), 1)
    y = iota((ty, cz), 0)
    here = kc_strip[8:8 + tx, :]
    group = lane // STRIP
    k = lane % STRIP
    touching = ((k == HALO) | (k == HALO - 1)) & (group == y)
    ends = []
    for x in range(tx):
        own = kc[x + 1, 8:8 + ty, :]
        moved = pltpu.roll(own, HALO, 1, stride=STRIP, stride_axis=0)
        ends.append(jnp.sum(jnp.where(touching, moved, 0.0), axis=0, keepdims=True))
        beyond = jnp.broadcast_to(kc_strip[8 + x:9 + x, :], (ty, cz))
        upper = jnp.where((group == y) & (k == HALO - 1), beyond, 0.0).sum(axis=1, keepdims=True)
        lower = jnp.where((group == y) & (k == HALO), beyond, 0.0).sum(axis=1, keepdims=True)
        others = [
            kc[x + 2, 8:8 + ty, :],
            kc[x, 8:8 + ty, :],
            kc[x + 1, 9:9 + ty, :],
            kc[x + 1, 7:7 + ty, :],
            jnp.where(lane == cz - 1, upper, pltpu.roll(own, cz - 1, 1)),
            jnp.where(lane == 0, lower, pltpu.roll(own, 1, 1)),
        ]
        finish(own, others, [c.at[i, x] for i in range(7)])
    ends = jnp.concatenate(ends, axis=0)
    lane = iota((tx, cz), 1)
    k = lane % STRIP
    others = [
        kc_strip[9:9 + tx, :],
        kc_strip[7:7 + tx, :],
        pltpu.roll(here, cz - STRIP, 1),
        pltpu.roll(here, STRIP, 1),
        jnp.where(k == HALO, ends, pltpu.roll(here, 1, 1)),
        jnp.where(k == HALO - 1, ends, pltpu.roll(here, cz - 1, 1)),
    ]
    finish(here, others, [c_strip.at[i] for i in range(7)])


def finish(own, others, outs):
    faces = [0.5 * (own + other) for other in others]
    diag = MASS_TERM + faces[0]
    for face in faces[1:]:
        diag = diag + face
    inverse = jnp.where(own > 0.0, 1.0 / diag, 0.0)
    for face, out in zip(faces, outs[:6], strict=True):
        out[...] = face * inverse
    outs[6][...] = inverse


def smooth(dims, start, fields, strips, r, r_strip, c, c_strip):
    weights = sweep_weights(SWEEPS)
    now = 0
    for number in range(start, SWEEPS):
        sweep(
            dims, SWEEPS - 1 - number, weights[number], fields[now], strips[now],
            fields[1 - now], strips[1 - now], r, r_strip, c, c_strip,
        )
        now = 1 - now
    return fields[now]


def gather_nodes(dims, field, row, z):
    cx, cy, cz, ch, nodes = dims
    hits = (iota((cz, nodes), 0) == z).astype(BF16)
    rows = field[HALO:HALO + cx, HALO:HALO + cy].reshape(cx * cy * ch, cz).astype(BF16)
    at_z = jnp.dot(rows, hits, preferred_element_type=F32)
    total = jnp.zeros((ch, nodes), F32)
    for r in range(cx * cy):
        here = jnp.broadcast_to(row == r, (ch, nodes))
        total = jnp.where(here, at_z[r * ch:(r + 1) * ch], total)
    return total.astype(BF16)


def fourth_kernel(dims, nx, ny, place, region_coeff, main, labels, cells, pos, strip, *refs):
    cx, cy, cz, ch, nodes = dims
    xrecv, yrecv, refs = refs[:nx], refs[nx:nx + ny], refs[nx + ny:]
    field_out, block_out, send_out, r, r_strip, c, c_strip, refs = *refs[:7], refs[7:]
    fa, fb, sa, sb, kc, kc_strip, codes, strip_codes, side_codes = refs
    even_x = 1 - place[0] % 2
    even_y = 1 - place[1] % 2
    tx, ty = cx + 2 * HALO, cy + 2 * HALO
    width = RHS_HALO
    ex = cx + 2 * width

    fill_codes(
        dims, labels, strip, xrecv, width * cy * ch + width * ch, even_x, codes, strip_codes
    )
    kc[...] = jnp.zeros_like(kc)
    kc_strip[...] = jnp.zeros_like(kc_strip)

    def conductivity(code):
        value = jnp.zeros_like(code)
        for region in range(region_coeff.shape[0]):
            value = jnp.where(code == region + 1, region_coeff[region], value)
        return value

    kc[1:1 + tx, 8 + HALO:8 + HALO + cy] = conductivity(codes[...]).reshape(tx, cy, cz)
    start = ex * width * ch + ex * ch
    for low in (True, False):
        got = pick(yrecv, low, even_y, start, tx * HALO).astype(F32)
        side_codes[...] = conductivity(got)
        y0 = 8 if low else 8 + HALO + cy
        for x in range(tx):
            kc[1 + x, y0:y0 + HALO, :] = side_codes[x * HALO:(x + 1) * HALO, :]
    start += tx * HALO
    low = pick(yrecv, True, even_y, start, 16).astype(F32)
    high = pick(yrecv, False, even_y, start, 16).astype(F32)
    kc_strip[8:8 + tx, :] = conductivity(join_strips(strip_codes[...], low, high, cy))
    coefficients(dims, kc, kc_strip, c, c_strip)

    r[...] = jnp.zeros_like(r)
    r_strip[...] = jnp.zeros_like(r_strip)
    assemble(dims, width, main, strip, xrecv, yrecv, even_x, even_y, r, r_strip)
    weight = sweep_weights(SWEEPS)[0]

    def column(x, _):
        for y in range(HALO - width, HALO + cy + width):
            value = r[x, y] * jnp.broadcast_to(c[6, x, y:y + 1, :], (ch, cz))
            r[x, y] = value
            fa[x, y] = weight * value
        value = r_strip[x] * jnp.broadcast_to(c_strip[6, pl.ds(x, 1), :], (ch, cz))
        r_strip[x] = value
        sa[x] = weight * value
        return _

    lax.fori_loop(HALO - width, HALO + cx + width, column, 0)
    field = smooth(dims, 1, (fa, fb), (sa, sb), r, r_strip, c, c_strip)

    field_out[...] = field[HALO:HALO + cx, HALO:HALO + cy].reshape(cx * cy * ch, cz)
    send_out[...] = strip_rows(lambda x, y: field[HALO + x, HALO + y], cx, cy, cz)
    cell = cells[...]
    row, z = cell // cz, cell % cz
    block_out[:ch, :] = gather_nodes(dims, field, row, z)
    rows = []
    for axis in range(3):
        value = pos[axis:axis + 1, :]
        for _ in range(3):
            part = value.astype(BF16).astype(F32)
            rows.append(part)
            value = value - part
    rows += [row.astype(F32), z.astype(F32), jnp.zeros((5, nodes), F32)]
    block_out[ch:, :] = jnp.concatenate(rows, axis=0).astype(BF16)


def boundary_kernel(dims, count, scale, pos, recv, kernel_out, sum_out, half_out):
    cx, cy, cz, ch, nodes = dims
    own = [jnp.broadcast_to(pos[k:k + 1, :], (nodes, nodes)).T for k in range(3)]

    def block(b, total):
        parts = recv[b, ch:ch + 16, :].astype(F32)
        squared = None
        for k in range(3):
            other = parts[3 * k:3 * k + 1] + parts[3 * k + 1:3 * k + 2] + parts[3 * k + 2:3 * k + 3]
            delta = own[k] - jnp.broadcast_to(other, (nodes, nodes))
            squared = delta * delta if squared is None else squared + delta * delta
        tile = (scale * lax.rsqrt(squared + SOFTENING * SOFTENING)).astype(BF16)
        kernel_out[b] = tile
        return total + lax.dot_general(recv[b, :ch, :], tile, NT, preferred_element_type=F32)

    total = lax.fori_loop(0, count, block, jnp.zeros((ch, nodes), F32))
    sum_out[...] = total
    half_out[...] = total.astype(BF16)


def last_kernel(dims, count, incident, recv, tiles, flux_out):
    cx, cy, cz, ch, nodes = dims

    def block(b, total):
        return total + lax.dot_general(recv[b], tiles[b], NT, preferred_element_type=F32)

    flux_out[...] = incident[...] + lax.fori_loop(0, count, block, jnp.zeros((ch, nodes), F32))


def fifth_kernel(dims, sizes, nx, ny, place, main, sums, cells, recv, blocks, strip, *refs):
    cx, cy, cz, ch, nodes = dims
    xrecv, yrecv, refs = refs[:nx], refs[nx:nx + ny], refs[nx + ny:]
    r_in, rs_in, c, c_strip, refs = *refs[:4], refs[4:]
    field_out, block_out, refs = *refs[:2], refs[2:]
    r, r_strip, fa, fb, sa, sb, left = refs
    even_x = 1 - place[0] % 2
    even_y = 1 - place[1] % 2
    width = RHS_HALO
    r[...] = r_in[...]
    r_strip[...] = rs_in[...]
    fa[...] = jnp.zeros_like(fa)
    sa[...] = jnp.zeros_like(sa)
    assemble(dims, HALO, main, strip, xrecv, yrecv, even_x, even_y, fa, sa)

    def neighbour(dx, dy, dz):
        at = [place[i] + d for i, d in enumerate((dx, dy, dz))]
        good = None
        for i, size in enumerate(sizes):
            ok = (at[i] >= 0) & (at[i] < size)
            good = ok if good is None else good & ok
            at[i] = jnp.clip(at[i], 0, size - 1)
        index = (at[0] * sizes[1] + at[1]) * sizes[2] + at[2]
        info = blocks[index, ch:ch + 16, :].astype(F32)
        good = jnp.full((1, nodes), good.astype(jnp.int32), jnp.int32) > 0
        row = jnp.where(good, info[9:10].astype(jnp.int32), -1)
        return recv[index].astype(F32), row, info[10:11].astype(jnp.int32)

    spans = {
        -1: (HALO - width, HALO, cx), 0: (HALO, HALO + cx, 0), 1: (HALO + cx, HALO + cx + width, -cx),
    }
    cell = cells[...]
    own_row, own_z = cell // cz, cell % cz
    strip_lane = iota((cz, nodes), 0)
    for dx in (-1, 0, 1):
        x0, x1, back_x = spans[dx]
        edge = []
        hits_edge = []
        for dy in (-1, 0, 1):
            y0, y1, back_y = spans[dy]
            parts = []
            if dx == 0 and dy == 0:
                top = sums[...].astype(BF16).astype(F32)
                row, z = own_row, own_z
                parts = [top, sums[...] - top]
            else:
                value, row, z = neighbour(dx, dy, 0)
                parts = [value]
            hits = (iota((cz, nodes), 0) == z).astype(BF16)
            hits = jnp.concatenate([hits] * len(parts), axis=1)
            count = (x1 - x0) * (y1 - y0)
            at = 0
            for x in range(x0, x1):
                for y in range(y0, y1):
                    wanted = (x - HALO + back_x) * cy + (y - HALO + back_y)
                    here = jnp.broadcast_to(row == wanted, (ch, nodes))
                    for i, value in enumerate(parts):
                        left[at:at + ch, i * nodes:(i + 1) * nodes] = jnp.where(
                            here, value, 0.0
                        ).astype(BF16)
                    at += ch
            added = lax.dot_general(
                left[:at, :len(parts) * nodes], hits, NT, preferred_element_type=F32
            )
            at = 0
            for x in range(x0, x1):
                for y in range(y0, y1):
                    inverse = jnp.broadcast_to(c[6, x, y:y + 1, :], (ch, cz))
                    r[x, y] += added[at:at + ch] * inverse
                    at += ch
            for dz in (-1, 1):
                value, row, z = neighbour(dx, dy, dz)
                y = row % cy + cy * dy + HALO
                k = HALO - 1 - z if dz > 0 else HALO + cz - 1 - z
                good = (row >= 0) & (y >= 0) & (y < cy + 2 * HALO) & (k >= 0) & (k < STRIP)
                good = good & ((k < HALO) if dz > 0 else (k >= HALO))
                lane = jnp.where(good, y * STRIP + k, -1)
                hits_edge.append((strip_lane == lane).astype(BF16))
                edge.append((value, jnp.where(row >= 0, row // cy, -1)))
        for x in range(x0, x1):
            at = (x - x0) * ch
            for i, (value, node_x) in enumerate(edge):
                here = jnp.broadcast_to(node_x == x - HALO + back_x, (ch, nodes))
                left[at:at + ch, i * nodes:(i + 1) * nodes] = jnp.where(here, value, 0.0).astype(BF16)
        added = lax.dot_general(
            left[:(x1 - x0) * ch, :len(edge) * nodes], jnp.concatenate(hits_edge, axis=1), NT,
            preferred_element_type=F32,
        )
        for x in range(x0, x1):
            inverse = jnp.broadcast_to(c_strip[6, x:x + 1, :], (ch, cz))
            r_strip[x] += added[(x - x0) * ch:(x - x0 + 1) * ch] * inverse

    field = smooth(dims, 0, (fa, fb), (sa, sb), r, r_strip, c, c_strip)
    for x in range(cx):
        for y in range(cy):
            field_out[pl.ds(x * cy + y, ch, stride=cx * cy), :] = field[HALO + x, HALO + y]
    block_out[...] = gather_nodes(dims, field, own_row, own_z)


def per_device(source, labels, region_coeff, node_cell, node_pos, incident):
    ch, cx, cy, cz = source.shape
    nodes = node_cell.shape[0]
    dims = (cx, cy, cz, ch, nodes)
    sizes = tuple(lax.axis_size(axis) for axis in AXES)
    count = math.prod(sizes)
    nx, ny, nz = (2 if size > 2 else 1 for size in sizes)
    scale = KERNEL_GAIN / math.sqrt(nodes * count)
    tx, ty = cx + 2 * HALO, cy + 2 * HALO
    place = jnp.stack([lax.axis_index(axis) for axis in AXES]).astype(jnp.int32)
    rows = cx * cy * ch
    flat = source.reshape(ch * cx * cy, cz)
    marks = labels.reshape(cx * cy, cz)
    cells = node_cell.reshape(1, nodes)
    shape = jax.ShapeDtypeStruct
    vmem = pltpu.VMEM

    rhs, send = kernel_call(
        functools.partial(first_kernel, dims),
        (shape((rows, cz), F32), shape((cx * ch + 16, cz), BF16)),
        [vmem((rows, 2 * nodes), BF16)],
        operands=(flat, marks, incident, cells),
        name="scatter_first",
    )

    def halo(main, send, width, with_labels, between=(lambda x: x, lambda x: x)):
        zrecv = exchange(send, "col")
        zrecv = between[0](zrecv)
        extra = HALO * cy + 16 if with_labels else 0
        strip_rows_ = cx * ch + (16 if with_labels else 0)
        own = (main, marks) if with_labels else (main,)
        strip, *sends = kernel_call(
            functools.partial(second_kernel, dims, width, with_labels, nz, nx),
            (shape((strip_rows_, cz), BF16),)
            + (shape((width * cy * ch + width * ch + extra, cz), BF16),) * nx,
            [vmem((32, cz), F32)] if with_labels else [],
            smem=1,
            operands=(place, *own, *zrecv),
            name="pack_x",
        )
        xrecv = exchange(None, "vol", sends)
        xrecv = between[1](xrecv)
        ex = cx + 2 * width
        extra = tx * HALO + 16 if with_labels else 0
        sends = kernel_call(
            functools.partial(third_kernel, dims, width, with_labels, nx, ny),
            (shape((ex * width * ch + ex * ch + extra, cz), BF16),) * ny,
            [vmem((tx * cy, cz), F32), vmem((tx, cz), F32), vmem((tx * HALO, cz), F32)]
            if with_labels else [],
            smem=1,
            operands=(place, *own, strip, *xrecv),
            name="pack_y",
        )
        yrecv = exchange(None, "row", sends)
        return strip, xrecv, yrecv

    strip, xrecv, yrecv = halo(rhs, send, RHS_HALO, True)
    field, block, send, r, r_strip, c, c_strip = kernel_call(
        functools.partial(fourth_kernel, dims, nx, ny),
        (
            shape((rows, cz), F32),
            shape((ch + 16, nodes), BF16),
            shape((cx * ch, cz), BF16),
            shape((tx, ty, ch, cz), F32),
            shape((tx, ch, cz), F32),
            shape((7, tx, ty, cz), F32),
            shape((7, tx, cz), F32),
        ),
        [
            vmem((tx, ty, ch, cz), F32),
            vmem((tx, ty, ch, cz), F32),
            vmem((tx, ch, cz), F32),
            vmem((tx, ch, cz), F32),
            vmem((tx + 2, ty + 16, cz), F32),
            vmem((tx + 16, cz), F32),
            vmem((tx * cy, cz), F32),
            vmem((tx, cz), F32),
            vmem((tx * HALO, cz), F32),
        ],
        smem=2,
        operands=(place, region_coeff, rhs, marks, cells, node_pos, strip, *xrecv, *yrecv),
        name="sweeps_first",
    )

    def to_all(value):
        spread = jnp.broadcast_to(value[None], (count,) + value.shape)
        return lax.all_to_all(spread, AXES, 0, 0, tiled=True)

    blocks = to_all(block)
    tiles, sums, half = kernel_call(
        functools.partial(boundary_kernel, dims, count, scale),
        (
            shape((count, nodes, nodes), BF16),
            shape((ch, nodes), F32),
            shape((ch, nodes), BF16),
        ),
        operands=(node_pos, blocks),
        name="boundary",
    )
    recv = to_all(half)
    strip, xrecv, yrecv = halo(field, send, HALO, False)
    field, block = kernel_call(
        functools.partial(fifth_kernel, dims, sizes, nx, ny),
        (shape((ch * cx * cy, cz), F32), shape((ch, nodes), BF16)),
        [
            vmem((tx, ty, ch, cz), F32),
            vmem((tx, ch, cz), F32),
            vmem((tx, ty, ch, cz), F32),
            vmem((tx, ty, ch, cz), F32),
            vmem((tx, ch, cz), F32),
            vmem((tx, ch, cz), F32),
            vmem((rows, 6 * nodes), BF16),
        ],
        smem=1,
        operands=(
            place, field, sums, cells, recv, blocks, strip, *xrecv, *yrecv, r, r_strip, c, c_strip
        ),
        name="sweeps_last",
    )
    flux = kernel_call(
        functools.partial(last_kernel, dims, count),
        shape((ch, nodes), F32),
        operands=(incident, to_all(block), tiles),
        name="flux_last",
    )
    return field.reshape(source.shape), flux


def solution(mesh):
    placed = (
        P(None, "vol", "row", "col"),
        P("vol", "row", "col"),
        P(),
        P(("vol", "row", "col")),
        P(None, ("vol", "row", "col")),
        P(None, ("vol", "row", "col")),
    )
    return jax.shard_map(
        per_device,
        mesh=mesh,
        in_specs=placed,
        out_specs=(P(None, "vol", "row", "col"), P(None, ("vol", "row", "col"))),
        check_vma=False,
    )
```

profile of v0, /device:TPU:0, one launch (start us, length us, event | category | flops | bytes accessed | tf_op | source)
XLA Modules:
  0.0 124.5 jit_solution(11089791793625434352)
XLA Ops:
  0.6 2.4 %scatter_first.1 = (f32[1024,128]{1,0:T(8,128)}, bf16[144,128]{1,0:T(8,128)(2,1)}) custom-call(f32[1024,128]{1,0:T(8,128)} %bitcast.11, s32[64,128]{1,0:T(8,128)} %bitcast.7, f32[16,128]{1,0:T(8,128)} %incident.3, s32[1,128]{1,0:T(1,128)} %bitcast.12), custom_call_target="tpu_custom_call" | custom-call | tf_op jit(solution)/shard_map/scatter_first/pallas_call | solution.py:40
  3.0 0.7 collective-permute-start.1
  3.7 5.9 %collective-permute-start = (bf16[144,128]{1,0:T(8,128)(2,1)}, bf16[144,128]{1,0:T(8,128)(2,1)S(1)}, u32[]{:S(2)}, u32[]{:S(2)}) collective-permute-start(bf16[144,128]{1,0:T(8,128)(2,1)} %get-tuple-element.25), channel_id=1, source_target_pairs={{0,1},{1,0},{2,3},{3,2},{4,5},{5,4},{6,7},{7,6},{8,9},{9,8},{10,11... | collective-permute-start | bytes 110600 | tf_op jit(solution)/shard_map/ppermute | solution.py:67
  9.6 0.6 pad_add_fusion.place
  10.2 0.0 collective-permute-done.1.refs_3_
  10.2 0.0 copy-start.8
  10.2 1.5 %collective-permute-done.refs_2_ = bf16[144,128]{1,0:T(8,128)(2,1)S(1)} collective-permute-done((bf16[144,128]{1,0:T(8,128)(2,1)}, bf16[144,128]{1,0:T(8,128)(2,1)S(1)}, u32[]{:S(2)}, u32[]{:S(2)}) %collective-permute-start) | collective-permute-done | bytes 36896 | tf_op jit(solution)/shard_map/ppermute | solution.py:67
  11.8 0.0 copy-start.9
  11.8 0.0 copy-done.8
  11.8 0.6 copy-done.9
  12.4 1.8 %pack_x.2 = (bf16[144,128]{1,0:T(8,128)(2,1)}, bf16[480,128]{1,0:T(8,128)(2,1)}) custom-call(s32[3]{0:T(128)} %pad_add_fusion.place, f32[1024,128]{1,0:T(8,128)} %get-tuple-element.24.refs_0_.main, s32[64,128]{1,0:T(8,128)} %bitcast.8, bf16[144,128]{1,0:T(8,128)(2,1)} %copy-done.9, bf16[144,128]{1,0:T(8,128)(2,1)} %copy-done.8), custom_call_target="tpu_custom_call" | custom-call | tf_op jit(solution)/shard_map/pack_x/pallas_call | solution.py:40
  14.2 1.5 %collective-permute-start.2 = (bf16[480,128]{1,0:T(8,128)(2,1)}, bf16[480,128]{1,0:T(8,128)(2,1)S(1)}, u32[]{:S(2)}, u32[]{:S(2)}) collective-permute-start(bf16[480,128]{1,0:T(8,128)(2,1)} %get-tuple-element.27), channel_id=1, source_target_pairs={{0,16},{16,0},{1,17},{17,1},{2,18},{18,2},{3,19},{19,3},{4,20},{20... | collective-permute-start | bytes 368648 | tf_op jit(solution)/shard_map/ppermute | solution.py:67
  15.6 3.6 %collective-permute-done.2.refs_3_.refs_0_ = bf16[480,128]{1,0:T(8,128)(2,1)S(1)} collective-permute-done((bf16[480,128]{1,0:T(8,128)(2,1)}, bf16[480,128]{1,0:T(8,128)(2,1)S(1)}, u32[]{:S(2)}, u32[]{:S(2)}) %collective-permute-start.2) | collective-permute-done | bytes 122912 | tf_op jit(solution)/shard_map/ppermute | solution.py:67
  19.2 0.0 copy-start.3
  19.2 0.6 copy-done.3
  19.9 2.0 %pack_y.2 = (bf16[976,128]{1,0:T(8,128)(2,1)}, bf16[976,128]{1,0:T(8,128)(2,1)}) custom-call(s32[3]{0:T(128)} %pad_add_fusion.place, f32[1024,128]{1,0:T(8,128)} %get-tuple-element.24.refs_0_.main, s32[64,128]{1,0:T(8,128)} %bitcast.9, bf16[144,128]{1,0:T(8,128)(2,1)} %get-tuple-element.26.refs_2_.strip, bf16[480,128]{1,0:T(8,128)(2,1)} %copy-done.3), custom_call_target="tpu_custom_call" | custom-call | tf_op jit(solution)/shard_map/pack_y/pallas_call | solution.py:40
  21.9 0.0 collective-permute-start.3
  21.9 0.7 collective-permute-start.4
  22.5 1.1 collective-permute-done.3.refs_1_
  23.6 0.0 copy-start.6
  23.6 0.0 collective-permute-done.4.refs_2_
  23.6 0.7 copy-done.6
  24.3 0.0 copy-start.7
  24.3 0.7 copy-done.7
  25.0 10.5 %sweeps_first.1 = (f32[1024,128]{1,0:T(8,128)}, bf16[32,128]{1,0:T(8,128)(2,1)}, bf16[128,128]{1,0:T(8,128)(2,1)}, f32[16,16,16,128]{3,2,1,0:T(8,128)}, f32[16,1...) custom-call(s32[3]{0:T(128)} %pad_add_fusion.place, f32[8]{0:T(128)} %region_coeff.1, ...), custom_call_target="tpu_custom_call" | custom-call | tf_op jit(solution)/shard_map/sweeps_first/pallas_call | solution.py:40
  35.5 1.4 %broadcast_in_dim.6 = bf16[32,32,128]{2,1,0:T(8,128)(2,1)} broadcast(bf16[32,128]{1,0:T(8,128)(2,1)} %get-tuple-element.31), dimensions={1,2} | broadcast | bytes 270336 | tf_op jit(solution)/shard_map/broadcast_in_dim | solution.py:675
  36.9 9.6 %all-to-all-start = ((bf16[32,32,128]{2,1,0:T(8,128)(2,1)}), bf16[32,32,128]{2,1,0:T(8,128)(2,1)S(1)}, u32[]{:S(2)}, u32[]{:S(2)}) async-start(bf16[32,32,128]{2,1,0:T(8,128)(2,1)} %broadcast_in_dim.6), calls=%async_computation | async-start | bytes 524288 | tf_op jit(solution)/shard_map/all_to_all | solution.py:676
  46.5 0.7 collective-permute-start.6
  47.2 4.5 %collective-permute-start.5 = (bf16[128,128]{1,0:T(8,128)(2,1)}, bf16[128,128]{1,0:T(8,128)(2,1)S(1)}, u32[]{:S(2)}, u32[]{:S(2)}) collective-permute-start(bf16[128,128]{1,0:T(8,128)(2,1)} %get-tuple-element.34), channel_id=1, source_target_pairs={{0,1},{1,0},{2,3},{3,2},{4,5},{5,4},{6,7},{7,6},{8,9},{9,8},{10,11... | collective-permute-start | bytes 98312 | tf_op jit(solution)/shard_map/ppermute | solution.py:67
  51.8 0.0 collective-permute-done.6.refs_2_
  51.8 0.0 copy-start.10
  51.8 2.4 %collective-permute-done.5.refs_1_ = bf16[128,128]{1,0:T(8,128)(2,1)S(1)} collective-permute-done((bf16[128,128]{1,0:T(8,128)(2,1)}, bf16[128,128]{1,0:T(8,128)(2,1)S(1)}, u32[]{:S(2)}, u32[]{:S(2)}) %collective-permute-start.5) | collective-permute-done | bytes 32800 | tf_op jit(solution)/shard_map/ppermute | solution.py:67
  54.1 0.0 copy-start.11
  54.1 0.0 copy-done.10
  54.1 0.6 copy-done.11
  54.8 1.8 %pack_x.3 = (bf16[128,128]{1,0:T(8,128)(2,1)}, bf16[576,128]{1,0:T(8,128)(2,1)}) custom-call(s32[3]{0:T(128)} %pad_add_fusion.place, f32[1024,128]{1,0:T(8,128)} %get-tuple-element.30.refs_0_.main, bf16[128,128]{1,0:T(8,128)(2,1)} %copy-done.11, bf16[128,128]{1,0:T(8,128)(2,1)} %copy-done.10), custom_call_target="tpu_custom_call" | custom-call | tf_op jit(solution)/shard_map/pack_x/pallas_call | solution.py:40
  56.5 1.4 %collective-permute-start.7 = (bf16[576,128]{1,0:T(8,128)(2,1)}, bf16[576,128]{1,0:T(8,128)(2,1)S(1)}, u32[]{:S(2)}, u32[]{:S(2)}) collective-permute-start(bf16[576,128]{1,0:T(8,128)(2,1)} %get-tuple-element.36), channel_id=1, source_target_pairs={{0,16},{16,0},{1,17},{17,1},{2,18},{18,2},{3,19},{19,3},{4,20},{20... | collective-permute-start | bytes 442376 | tf_op jit(solution)/shard_map/ppermute | solution.py:67
  58.0 4.0 %collective-permute-done.7.refs_2_.refs_0_ = bf16[576,128]{1,0:T(8,128)(2,1)S(1)} collective-permute-done((bf16[576,128]{1,0:T(8,128)(2,1)}, bf16[576,128]{1,0:T(8,128)(2,1)S(1)}, u32[]{:S(2)}, u32[]{:S(2)}) %collective-permute-start.7) | collective-permute-done | bytes 147488 | tf_op jit(solution)/shard_map/ppermute | solution.py:67
  61.9 0.0 copy-start.1
  61.9 0.7 copy-done.1
  62.6 2.0 %pack_y.3 = (bf16[1280,128]{1,0:T(8,128)(2,1)}, bf16[1280,128]{1,0:T(8,128)(2,1)}) custom-call(s32[3]{0:T(128)} %pad_add_fusion.place, f32[1024,128]{1,0:T(8,128)} %get-tuple-element.30.refs_0_.main, bf16[128,128]{1,0:T(8,128)(2,1)} %get-tuple-element.35.refs_1_.strip, bf16[576,128]{1,0:T(8,128)(2,1)} %copy-done.1), custom_call_target="tpu_custom_call" | custom-call | tf_op jit(solution)/shard_map/pack_y/pallas_call | solution.py:40
  64.6 0.0 collective-permute-start.8
  64.6 0.7 collective-permute-start.9
  65.3 0.0 all-to-all-done.recv.blocks
  65.3 0.0 copy-start
  65.3 0.7 copy-done
  66.0 7.4 %boundary.1 = (bf16[32,128,128]{2,1,0:T(8,128)(2,1)}, f32[16,128]{1,0:T(8,128)}, bf16[16,128]{1,0:T(8,128)(2,1)}) custom-call(f32[3,128]{1,0:T(4,128)} %pos.3, bf16[32,32,128]{2,1,0:T(8,128)(2,1)} %copy-done), custom_call_target="tpu_custom_call" | custom-call | tf_op jit(solution)/shard_map/boundary/pallas_call | solution.py:40
  73.4 1.4 %broadcast_in_dim.7 = bf16[32,16,128]{2,1,0:T(8,128)(2,1)} broadcast(bf16[16,128]{1,0:T(8,128)(2,1)} %get-tuple-element.33), dimensions={1,2} | broadcast | bytes 135168 | tf_op jit(solution)/shard_map/broadcast_in_dim | solution.py:675
  74.8 7.6 %all-to-all-start.1 = ((bf16[32,16,128]{2,1,0:T(8,128)(2,1)}), bf16[32,16,128]{2,1,0:T(8,128)(2,1)S(1)}, u32[]{:S(2)}, u32[]{:S(2)}) async-start(bf16[32,16,128]{2,1,0:T(8,128)(2,1)} %broadcast_in_dim.7), calls=%async_computation.1 | async-start | bytes 262144 | tf_op jit(solution)/shard_map/all_to_all | solution.py:676
  82.4 0.0 collective-permute-done.8.refs_1_
  82.4 0.0 copy-start.4
  82.4 0.0 collective-permute-done.9.refs_2_
  82.4 0.0 copy-start.5
  82.4 8.4 %all-to-all-done.1.recv = bf16[32,16,128]{2,1,0:T(8,128)(2,1)S(1)} async-done(((bf16[32,16,128]{2,1,0:T(8,128)(2,1)}), bf16[32,16,128]{2,1,0:T(8,128)(2,1)S(1)}, u32[]{:S(2)}, u32[]{:S(2)}) %all-to-all-start.1) | async-done | bytes 131104 | tf_op jit(solution)/shard_map/all_to_all | solution.py:676
  90.8 0.0 copy-start.2
  90.8 0.0 copy-done.4
  90.8 0.0 copy-done.5
  90.8 0.6 copy-done.2
  91.4 14.9 %sweeps_last.1 = (f32[1024,128]{1,0:T(8,128)}, bf16[16,128]{1,0:T(8,128)(2,1)}) custom-call(s32[3]{0:T(128)} %pad_add_fusion.place, f32[1024,128]{1,0:T(8,128)} %get-tuple-element.30.refs_0_.main, f32[16,128]{1,0:T(8,128)} %get-tuple-element.32.sums, s32[1,128]{1,0:T(1,128)} %bitcast.14, bf16[32,16,128]{2,1,0:T(8,128)(2,1)} %copy-done.2, ...), custom_call_target="tpu_custom_call" | custom-call | tf_op jit(solution)/shard_map/sweeps_last/pallas_call | solution.py:40
  106.3 0.7 broadcast_in_dim.8
  107.0 10.8 %all_to_all.15.recv = bf16[32,16,128]{2,1,0:T(8,128)(2,1)} all-to-all(bf16[32,16,128]{2,1,0:T(8,128)(2,1)S(1)} %broadcast_in_dim.8), channel_id=1, replica_groups=mesh['vol'=2,'row'=4,'col'=4] {'vol','row','col'}, dimensions={0} | all-to-all | bytes 262144 | tf_op jit(solution)/shard_map/all_to_all | solution.py:676
  117.8 6.7 %flux_last.1 = f32[16,128]{1,0:T(8,128)} custom-call(f32[16,128]{1,0:T(8,128)} %incident.3, bf16[32,16,128]{2,1,0:T(8,128)(2,1)} %all_to_all.15.recv, bf16[32,128,128]{2,1,0:T(8,128)(2,1)} %get-tuple-element.45.tiles), custom_call_target="tpu_custom_call" | custom-call | tf_op jit(solution)/shard_map/flux_last/pallas_call | solution.py:40
Async XLA Ops:
  3.0 7.2 %collective-permute-start.1 = (bf16[144,128]{1,0:T(8,128)(2,1)}, bf16[144,128]{1,0:T(8,128)(2,1)S(1)}, u32[]{:S(2)}, u32[]{:S(2)}) collective-permute-start(bf16[144,128]{1,0:T(8,128)(2,1)} %get-tuple-element.25), channel_id=1, source_target_pairs={{1,2},{2,1},{5,6},{6,5},{9,10},{10,9},{13,14},{14,13},{17,18},{18,... | collective-permute-start | bytes 110600 | tf_op jit(solution)/shard_map/ppermute | solution.py:67
  3.7 8.1 %collective-permute-start = (bf16[144,128]{1,0:T(8,128)(2,1)}, bf16[144,128]{1,0:T(8,128)(2,1)S(1)}, u32[]{:S(2)}, u32[]{:S(2)}) collective-permute-start(bf16[144,128]{1,0:T(8,128)(2,1)} %get-tuple-element.25), channel_id=1, source_target_pairs={{0,1},{1,0},{2,3},{3,2},{4,5},{5,4},{6,7},{7,6},{8,9},{9,8},{10,11... | collective-permute-start | bytes 110600 | tf_op jit(solution)/shard_map/ppermute | solution.py:67
  10.2 1.6 %copy-start.8 = (bf16[144,128]{1,0:T(8,128)(2,1)}, bf16[144,128]{1,0:T(8,128)(2,1)S(1)}, u32[]{:S(2)}) copy-start(bf16[144,128]{1,0:T(8,128)(2,1)S(1)} %collective-permute-done.1.refs_3_) | copy-start | bytes 110596
  11.8 0.6 copy-start.9
  14.2 5.1 %collective-permute-start.2 = (bf16[480,128]{1,0:T(8,128)(2,1)}, bf16[480,128]{1,0:T(8,128)(2,1)S(1)}, u32[]{:S(2)}, u32[]{:S(2)}) collective-permute-start(bf16[480,128]{1,0:T(8,128)(2,1)} %get-tuple-element.27), channel_id=1, source_target_pairs={{0,16},{16,0},{1,17},{17,1},{2,18},{18,2},{3,19},{19,3},{4,20},{20... | collective-permute-start | bytes 368648 | tf_op jit(solution)/shard_map/ppermute | solution.py:67
  19.2 0.6 copy-start.3
  21.9 1.7 %collective-permute-start.3 = (bf16[976,128]{1,0:T(8,128)(2,1)}, bf16[976,128]{1,0:T(8,128)(2,1)S(1)}, u32[]{:S(2)}, u32[]{:S(2)}) collective-permute-start(bf16[976,128]{1,0:T(8,128)(2,1)} %get-tuple-element.28), channel_id=1, source_target_pairs={{0,4},{4,0},{8,12},{12,8},{1,5},{5,1},{9,13},{13,9},{2,6},{6,2},{1... | collective-permute-start | bytes 749576 | tf_op jit(solution)/shard_map/ppermute | solution.py:67
  21.9 1.7 %collective-permute-start.4 = (bf16[976,128]{1,0:T(8,128)(2,1)}, bf16[976,128]{1,0:T(8,128)(2,1)S(1)}, u32[]{:S(2)}, u32[]{:S(2)}) collective-permute-start(bf16[976,128]{1,0:T(8,128)(2,1)} %get-tuple-element.29), channel_id=1, source_target_pairs={{4,8},{8,4},{5,9},{9,5},{6,10},{10,6},{7,11},{11,7},{20,24},{24,20... | collective-permute-start | bytes 749576 | tf_op jit(solution)/shard_map/ppermute | solution.py:67
  23.6 0.7 copy-start.6
  24.3 0.7 copy-start.7
  36.9 28.4 %all-to-all-start = ((bf16[32,32,128]{2,1,0:T(8,128)(2,1)}), bf16[32,32,128]{2,1,0:T(8,128)(2,1)S(1)}, u32[]{:S(2)}, u32[]{:S(2)}) async-start(bf16[32,32,128]{2,1,0:T(8,128)(2,1)} %broadcast_in_dim.6), calls=%async_computation | async-start | bytes 524288 | tf_op jit(solution)/shard_map/all_to_all | solution.py:676
  46.5 5.2 %collective-permute-start.6 = (bf16[128,128]{1,0:T(8,128)(2,1)}, bf16[128,128]{1,0:T(8,128)(2,1)S(1)}, u32[]{:S(2)}, u32[]{:S(2)}) collective-permute-start(bf16[128,128]{1,0:T(8,128)(2,1)} %get-tuple-element.34), channel_id=1, source_target_pairs={{1,2},{2,1},{5,6},{6,5},{9,10},{10,9},{13,14},{14,13},{17,18},{18,... | collective-permute-start | bytes 98312 | tf_op jit(solution)/shard_map/ppermute | solution.py:67
  47.2 6.9 %collective-permute-start.5 = (bf16[128,128]{1,0:T(8,128)(2,1)}, bf16[128,128]{1,0:T(8,128)(2,1)S(1)}, u32[]{:S(2)}, u32[]{:S(2)}) collective-permute-start(bf16[128,128]{1,0:T(8,128)(2,1)} %get-tuple-element.34), channel_id=1, source_target_pairs={{0,1},{1,0},{2,3},{3,2},{4,5},{5,4},{6,7},{7,6},{8,9},{9,8},{10,11... | collective-permute-start | bytes 98312 | tf_op jit(solution)/shard_map/ppermute | solution.py:67
  51.8 2.4 %copy-start.10 = (bf16[128,128]{1,0:T(8,128)(2,1)}, bf16[128,128]{1,0:T(8,128)(2,1)S(1)}, u32[]{:S(2)}) copy-start(bf16[128,128]{1,0:T(8,128)(2,1)S(1)} %collective-permute-done.6.refs_2_) | copy-start | bytes 98308
  54.1 0.6 copy-start.11
  56.5 5.4 %collective-permute-start.7 = (bf16[576,128]{1,0:T(8,128)(2,1)}, bf16[576,128]{1,0:T(8,128)(2,1)S(1)}, u32[]{:S(2)}, u32[]{:S(2)}) collective-permute-start(bf16[576,128]{1,0:T(8,128)(2,1)} %get-tuple-element.36), channel_id=1, source_target_pairs={{0,16},{16,0},{1,17},{17,1},{2,18},{18,2},{3,19},{19,3},{4,20},{20... | collective-permute-start | bytes 442376 | tf_op jit(solution)/shard_map/ppermute | solution.py:67
  61.9 0.7 copy-start.1
  64.6 17.8 %collective-permute-start.8 = (bf16[1280,128]{1,0:T(8,128)(2,1)}, bf16[1280,128]{1,0:T(8,128)(2,1)S(1)}, u32[]{:S(2)}, u32[]{:S(2)}) collective-permute-start(bf16[1280,128]{1,0:T(8,128)(2,1)} %get-tuple-element.37), channel_id=1, source_target_pairs={{0,4},{4,0},{8,12},{12,8},{1,5},{5,1},{9,13},{13,9},{2,6},{6,2},{1... | collective-permute-start | bytes 983048 | tf_op jit(solution)/shard_map/ppermute | solution.py:67
  64.6 17.8 %collective-permute-start.9 = (bf16[1280,128]{1,0:T(8,128)(2,1)}, bf16[1280,128]{1,0:T(8,128)(2,1)S(1)}, u32[]{:S(2)}, u32[]{:S(2)}) collective-permute-start(bf16[1280,128]{1,0:T(8,128)(2,1)} %get-tuple-element.38), channel_id=1, source_target_pairs={{4,8},{8,4},{5,9},{9,5},{6,10},{10,6},{7,11},{11,7},{20,24},{24,20... | collective-permute-start | bytes 983048 | tf_op jit(solution)/shard_map/ppermute | solution.py:67
  65.3 0.7 copy-start
  74.8 16.0 %all-to-all-start.1 = ((bf16[32,16,128]{2,1,0:T(8,128)(2,1)}), bf16[32,16,128]{2,1,0:T(8,128)(2,1)S(1)}, u32[]{:S(2)}, u32[]{:S(2)}) async-start(bf16[32,16,128]{2,1,0:T(8,128)(2,1)} %broadcast_in_dim.7), calls=%async_computation.1 | async-start | bytes 262144 | tf_op jit(solution)/shard_map/all_to_all | solution.py:676
  82.4 8.4 %copy-start.4 = (bf16[1280,128]{1,0:T(8,128)(2,1)}, bf16[1280,128]{1,0:T(8,128)(2,1)S(1)}, u32[]{:S(2)}) copy-start(bf16[1280,128]{1,0:T(8,128)(2,1)S(1)} %collective-permute-done.8.refs_1_) | copy-start | bytes 983044
  82.4 8.4 %copy-start.5 = (bf16[1280,128]{1,0:T(8,128)(2,1)}, bf16[1280,128]{1,0:T(8,128)(2,1)S(1)}, u32[]{:S(2)}) copy-start(bf16[1280,128]{1,0:T(8,128)(2,1)S(1)} %collective-permute-done.9.refs_2_) | copy-start | bytes 983044
  90.8 0.7 copy-start.2
where the time goes:
time: 125 us
  Pallas kernels  49.4 us (40%)
  starting transfers between devices  33.2 us (27%)
  waiting for transfers between devices  20.9 us (17%)
  blocking collectives  10.8 us (9%)
  local copies, waits for them, and re-layouts  8.82 us (7%)
    pallas_call x9, Pallas kernels, kernel_call(): pl.pallas_call(body, out_shape=out_shape, in_specs=specs, out_specs=jax.t...  49.4 us
    all_to_all x2, starting transfers between devices, to_all(): return lax.all_to_all(spread, AXES, 0, 0, tiled=True)  17.2 us
    ppermute x10, starting transfers between devices, exchange(): out.append(lax.ppermute(arrays[which], axis, pairs))  16 us
    ppermute x10, waiting for transfers between devices, exchange(): out.append(lax.ppermute(arrays[which], axis, pairs))  12.5 us
    all_to_all x1, blocking collectives, to_all(): return lax.all_to_all(spread, AXES, 0, 0, tiled=True)  10.8 us
    all_to_all x2, waiting for transfers between devices, to_all(): return lax.all_to_all(spread, AXES, 0, 0, tiled=True)  8.37 us
    unnamed x24, local copies, waits for them, and re-layouts  5.35 us
    broadcast_in_dim x3, local copies, waits for them, and re-layouts, to_all(): spread = jnp.broadcast_to(value[None], (count,) + value.shape)  3.47 us
  transfers between devices with their start and end apart: 12, of which 6 were waited for; matrix products, arithmetic and copies ran while one was open for 2% of the time, Pallas kernels for 9%

commit v1 on v0

--- a/solution.py
+++ b/solution.py
@@ -20,6 +20,8 @@
 STRIP = 2 * HALO
 AXES = ("vol", "row", "col")
 F32, BF16 = jnp.float32, jnp.bfloat16
+ROW, LAYER, REGION, INCIDENT = 3, 4, 5, 8
+SPARE = 4 * 1024 * 1024
 NT = (((1,), (1,)), ((), ()))
 
 
@@ -35,6 +37,9 @@
 
 
 def kernel_call(body, out_shape, scratch=(), smem=0, operands=(), name=None):
+    held = [jnp.shape(leaf) + (leaf.dtype,) for leaf in jax.tree.leaves((out_shape, operands))]
+    held += [ref.shape + (ref.dtype,) for ref in scratch]
+    need = sum(math.prod(entry[:-1]) * jnp.dtype(entry[-1]).itemsize for entry in held)
     specs = [pl.BlockSpec(memory_space=pltpu.SMEM)] * smem
     specs += [pl.BlockSpec(memory_space=pltpu.VMEM)] * (len(operands) - smem)
     return pl.pallas_call(
@@ -43,7 +48,7 @@
         in_specs=specs,
         out_specs=jax.tree.map(lambda _: pl.BlockSpec(memory_space=pltpu.VMEM), out_shape),
         scratch_shapes=list(scratch),
-        compiler_params=pltpu.CompilerParams(vmem_limit_bytes=56 * 1024 * 1024),
+        compiler_params=pltpu.CompilerParams(vmem_limit_bytes=need + SPARE),
         name=name,
     )(*operands)
 
@@ -86,12 +91,15 @@
     return total.astype(BF16)
 
 
-def first_kernel(dims, source, labels, incident, cells, rhs_out, send_out, left):
-    cx, cy, cz, ch, nodes = dims
-    cell = cells[...]
-    row, z = cell // cz, cell % cz
+def node_places(small):
+    return (small[at:at + 1, :].astype(jnp.int32) for at in (ROW, LAYER))
+
+
+def first_kernel(dims, source, small, rhs_out, send_out, left):
+    cx, cy, cz, ch, nodes = dims
+    row, z = node_places(small)
     hits = (iota((cz, nodes), 0) == z).astype(BF16)
-    flux = incident[...]
+    flux = small[INCIDENT:INCIDENT + ch, :]
     top = flux.astype(BF16).astype(F32)
     rest = flux - top
     for r in range(cx * cy):
@@ -111,7 +119,7 @@
 
     send_out[:cx * ch, :] = strip_rows(read, cx, cy, cz)
     base, lane_y = edge_picker(cz, cz)
-    codes = (labels[...] + 1).astype(F32).astype(BF16)
+    codes = small[INCIDENT + ch:, :].astype(BF16)
     strips = jnp.dot(codes, base.astype(BF16), preferred_element_type=F32)
     own = (iota(strips.shape, 0) % cy) == lane_y[:1, :]
     strips = jnp.where(own, strips, 0.0).reshape(cx, cy, cz).sum(axis=1)
@@ -124,7 +132,7 @@
     cx, cy, cz, ch, nodes = dims
     main, refs = refs[0], refs[1:]
     if with_labels:
-        labels, refs = refs[0], refs[1:]
+        small, refs = refs[0], refs[1:]
     zrecv, refs = refs[:nz], refs[nz:]
     strip_out, sends, refs = refs[0], refs[1:1 + nx], refs[1 + nx:]
     even_x = 1 - place[0] % 2
@@ -153,8 +161,8 @@
             start = slab + width * ch
             x0 = upward * (cx - HALO)
             send[start:start + HALO * cy, :] = (
-                labels[pl.ds(pl.multiple_of(x0 * cy, 8), HALO * cy), :] + 1
-            ).astype(F32).astype(BF16)
+                small[pl.ds(pl.multiple_of(INCIDENT + ch + x0 * cy, 8), HALO * cy), :]
+            ).astype(BF16)
             send[start + HALO * cy:, :] = codes[pl.ds(x0, 16), :].astype(BF16)
 
 
@@ -162,7 +170,7 @@
     cx, cy, cz, ch, nodes = dims
     main, refs = refs[0], refs[1:]
     if with_labels:
-        labels, refs = refs[0], refs[1:]
+        small, refs = refs[0], refs[1:]
     strip, refs = refs[0], refs[1:]
     xrecv, refs = refs[:nx], refs[nx:]
     sends, refs = refs[:ny], refs[ny:]
@@ -172,7 +180,7 @@
     slab = width * cy * ch
     if with_labels:
         codes, strip_codes, picked = refs
-        fill_codes(dims, labels, strip, xrecv, slab + width * ch, even_x, codes, strip_codes)
+        fill_codes(dims, small, strip, xrecv, slab + width * ch, even_x, codes, strip_codes)
     for which in range(ny):
         send = sends[which]
         upward = even_y if which == 0 else 1 - even_y
@@ -203,11 +211,11 @@
             send[start + tall * HALO:, :] = strip_codes[...].astype(BF16)
 
 
-def fill_codes(dims, labels, strip, xrecv, start, even_x, codes, strip_codes):
+def fill_codes(dims, small, strip, xrecv, start, even_x, codes, strip_codes):
     cx, cy, cz, ch, nodes = dims
     side = HALO * cy
     codes[:side, :] = pick(xrecv, True, even_x, start, side).astype(F32)
-    codes[side:side + cx * cy, :] = (labels[...] + 1).astype(F32)
+    codes[side:side + cx * cy, :] = small[INCIDENT + ch:, :]
     codes[side + cx * cy:, :] = pick(xrecv, False, even_x, start, side).astype(F32)
     strip_codes[:HALO, :] = pick(xrecv, True, even_x, start + side, 16).astype(F32)[:HALO]
     strip_codes[HALO:HALO + cx, :] = strip[cx * ch:cx * ch + 16, :].astype(F32)[:cx]
@@ -388,7 +396,7 @@
     return total.astype(BF16)
 
 
-def fourth_kernel(dims, nx, ny, place, region_coeff, main, labels, cells, pos, strip, *refs):
+def fourth_kernel(dims, regions, nx, ny, place, main, small, strip, *refs):
     cx, cy, cz, ch, nodes = dims
     xrecv, yrecv, refs = refs[:nx], refs[nx:nx + ny], refs[nx + ny:]
     field_out, block_out, send_out, r, r_strip, c, c_strip, refs = *refs[:7], refs[7:]
@@ -400,15 +408,16 @@
     ex = cx + 2 * width
 
     fill_codes(
-        dims, labels, strip, xrecv, width * cy * ch + width * ch, even_x, codes, strip_codes
+        dims, small, strip, xrecv, width * cy * ch + width * ch, even_x, codes, strip_codes
     )
     kc[...] = jnp.zeros_like(kc)
     kc_strip[...] = jnp.zeros_like(kc_strip)
 
     def conductivity(code):
         value = jnp.zeros_like(code)
-        for region in range(region_coeff.shape[0]):
-            value = jnp.where(code == region + 1, region_coeff[region], value)
+        for region in range(regions):
+            coeff = jnp.broadcast_to(small[REGION:REGION + 1, region:region + 1], code.shape)
+            value = jnp.where(code == region + 1, coeff, value)
         return value
 
     kc[1:1 + tx, 8 + HALO:8 + HALO + cy] = conductivity(codes[...]).reshape(tx, cy, cz)
@@ -445,12 +454,11 @@
 
     field_out[...] = field[HALO:HALO + cx, HALO:HALO + cy].reshape(cx * cy * ch, cz)
     send_out[...] = strip_rows(lambda x, y: field[HALO + x, HALO + y], cx, cy, cz)
-    cell = cells[...]
-    row, z = cell // cz, cell % cz
+    row, z = node_places(small)
     block_out[:ch, :] = gather_nodes(dims, field, row, z)
     rows = []
     for axis in range(3):
-        value = pos[axis:axis + 1, :]
+        value = small[axis:axis + 1, :]
         for _ in range(3):
             part = value.astype(BF16).astype(F32)
             rows.append(part)
@@ -459,11 +467,11 @@
     block_out[ch:, :] = jnp.concatenate(rows, axis=0).astype(BF16)
 
 
-def boundary_kernel(dims, count, scale, pos, recv, kernel_out, sum_out, half_out):
-    cx, cy, cz, ch, nodes = dims
-    own = [jnp.broadcast_to(pos[k:k + 1, :], (nodes, nodes)).T for k in range(3)]
-
-    def block(b, total):
+def boundary_kernel(dims, count, scale, small, recv, kernel_out, sum_out, half_out):
+    cx, cy, cz, ch, nodes = dims
+    own = [jnp.broadcast_to(small[k:k + 1, :], (nodes, nodes)).T for k in range(3)]
+
+    def block(b, _):
         parts = recv[b, ch:ch + 16, :].astype(F32)
         squared = None
         for k in range(3):
@@ -471,24 +479,42 @@
             delta = own[k] - jnp.broadcast_to(other, (nodes, nodes))
             squared = delta * delta if squared is None else squared + delta * delta
         tile = (scale * lax.rsqrt(squared + SOFTENING * SOFTENING)).astype(BF16)
-        kernel_out[b] = tile
-        return total + lax.dot_general(recv[b, :ch, :], tile, NT, preferred_element_type=F32)
-
-    total = lax.fori_loop(0, count, block, jnp.zeros((ch, nodes), F32))
+        kernel_out[:, pl.ds(pl.multiple_of(b * nodes, nodes), nodes)] = tile
+        return _
+
+    lax.fori_loop(0, count, block, 0)
+    total = product(recv, kernel_out, count, dims)
     sum_out[...] = total
     half_out[...] = total.astype(BF16)
 
 
-def last_kernel(dims, count, incident, recv, tiles, flux_out):
-    cx, cy, cz, ch, nodes = dims
-
-    def block(b, total):
-        return total + lax.dot_general(recv[b], tiles[b], NT, preferred_element_type=F32)
-
-    flux_out[...] = incident[...] + lax.fori_loop(0, count, block, jnp.zeros((ch, nodes), F32))
-
-
-def fifth_kernel(dims, sizes, nx, ny, place, main, sums, cells, recv, blocks, strip, *refs):
+def product(recv, tiles, count, dims):
+    cx, cy, cz, ch, nodes = dims
+    group = math.gcd(count, 32)
+
+    def part(at):
+        traces = jnp.concatenate([recv[at + i, :ch, :] for i in range(group)], axis=1)
+        start = at * nodes
+        if not isinstance(at, int):
+            start = pl.multiple_of(start, nodes)
+        return lax.dot_general(
+            traces, tiles[:, pl.ds(start, group * nodes)], NT, preferred_element_type=F32
+        )
+
+    if group == count:
+        return part(0)
+    return lax.fori_loop(
+        0, count // group, lambda i, total: total + part(i * group), jnp.zeros((ch, nodes), F32)
+    )
+
+
+def last_kernel(dims, count, small, recv, tiles, flux_out):
+    cx, cy, cz, ch, nodes = dims
+    incident = small[INCIDENT:INCIDENT + ch, :]
+    flux_out[...] = incident + product(recv, tiles, count, dims)
+
+
+def fifth_kernel(dims, sizes, nx, ny, place, main, sums, small, recv, blocks, strip, *refs):
     cx, cy, cz, ch, nodes = dims
     xrecv, yrecv, refs = refs[:nx], refs[nx:nx + ny], refs[nx + ny:]
     r_in, rs_in, c, c_strip, refs = *refs[:4], refs[4:]
@@ -519,8 +545,7 @@
     spans = {
         -1: (HALO - width, HALO, cx), 0: (HALO, HALO + cx, 0), 1: (HALO + cx, HALO + cx + width, -cx),
     }
-    cell = cells[...]
-    own_row, own_z = cell // cz, cell % cz
+    own_row, own_z = node_places(small)
     strip_lane = iota((cz, nodes), 0)
     for dx in (-1, 0, 1):
         x0, x1, back_x = spans[dx]
@@ -604,11 +629,23 @@
     shape = jax.ShapeDtypeStruct
     vmem = pltpu.VMEM
 
+    height = INCIDENT + ch + cx * cy
+    small = jnp.zeros((height, cz), F32)
+    for value, row in (
+        (node_pos, 0),
+        ((cells // cz).astype(F32), ROW),
+        ((cells % cz).astype(F32), LAYER),
+        (region_coeff[None], REGION),
+        (incident, INCIDENT),
+        ((marks + 1).astype(F32), INCIDENT + ch),
+    ):
+        sides = ((row, height - row - value.shape[0], 0), (0, cz - value.shape[1], 0))
+        small += lax.pad(value, jnp.float32(0), sides)
     rhs, send = kernel_call(
         functools.partial(first_kernel, dims),
         (shape((rows, cz), F32), shape((cx * ch + 16, cz), BF16)),
         [vmem((rows, 2 * nodes), BF16)],
-        operands=(flat, marks, incident, cells),
+        operands=(flat, small),
         name="scatter_first",
     )
 
@@ -617,7 +654,7 @@
         zrecv = between[0](zrecv)
         extra = HALO * cy + 16 if with_labels else 0
         strip_rows_ = cx * ch + (16 if with_labels else 0)
-        own = (main, marks) if with_labels else (main,)
+        own = (main, small) if with_labels else (main,)
         strip, *sends = kernel_call(
             functools.partial(second_kernel, dims, width, with_labels, nz, nx),
             (shape((strip_rows_, cz), BF16),)
@@ -645,7 +682,7 @@
 
     strip, xrecv, yrecv = halo(rhs, send, RHS_HALO, True)
     field, block, send, r, r_strip, c, c_strip = kernel_call(
-        functools.partial(fourth_kernel, dims, nx, ny),
+        functools.partial(fourth_kernel, dims, region_coeff.shape[0], nx, ny),
         (
             shape((rows, cz), F32),
             shape((ch + 16, nodes), BF16),
@@ -666,8 +703,8 @@
             vmem((tx, cz), F32),
             vmem((tx * HALO, cz), F32),
         ],
-        smem=2,
-        operands=(place, region_coeff, rhs, marks, cells, node_pos, strip, *xrecv, *yrecv),
+        smem=1,
+        operands=(place, rhs, small, strip, *xrecv, *yrecv),
         name="sweeps_first",
     )
 
@@ -679,15 +716,19 @@
     tiles, sums, half = kernel_call(
         functools.partial(boundary_kernel, dims, count, scale),
         (
-            shape((count, nodes, nodes), BF16),
+            shape((nodes, count * nodes), BF16),
             shape((ch, nodes), F32),
             shape((ch, nodes), BF16),
         ),
-        operands=(node_pos, blocks),
+        operands=(small, blocks),
         name="boundary",
     )
+
+    def after_boundary(arrays):
+        return lax.optimization_barrier((arrays, half))[0]
+
+    strip, xrecv, yrecv = halo(field, send, HALO, False, (lambda x: x, after_boundary))
     recv = to_all(half)
-    strip, xrecv, yrecv = halo(field, send, HALO, False)
     field, block = kernel_call(
         functools.partial(fifth_kernel, dims, sizes, nx, ny),
         (shape((ch * cx * cy, cz), F32), shape((ch, nodes), BF16)),
@@ -702,14 +743,14 @@
         ],
         smem=1,
         operands=(
-            place, field, sums, cells, recv, blocks, strip, *xrecv, *yrecv, r, r_strip, c, c_strip
+            place, field, sums, small, recv, blocks, strip, *xrecv, *yrecv, r, r_strip, c, c_strip
         ),
         name="sweeps_last",
     )
     flux = kernel_call(
         functools.partial(last_kernel, dims, count),
         shape((ch, nodes), F32),
-        operands=(incident, to_all(block), tiles),
+        operands=(small, to_all(block), tiles),
         name="flux_last",
     )
     return field.reshape(source.shape), flux

time: 125 us -> 97.7 us (0.78)
  Pallas kernels: 49.4 us -> 27.4 us
  blocking collectives: 10.8 us -> 25.9 us
  waiting for transfers between devices: 20.9 us -> 10.3 us
  starting transfers between devices: 33.2 us -> 26.7 us
  local copies, waits for them, and re-layouts: 8.82 us -> 3.92 us
  other arithmetic: 0.59 us -> 2.23 us
    pallas_call x9, Pallas kernels: 49.4 us -> 27.4 us  [kernel_call(): pl.pallas_call(body, out_shape=out_shape, in_specs=specs, out_specs=jax.t...]
    all_to_all x1 -> x2, blocking collectives: 10.8 us -> 25.9 us  [to_all(): return lax.all_to_all(spread, AXES, 0, 0, tiled=True)]
    all_to_all x2 -> x1, waiting for transfers between devices: 8.37 us -> 0.56 us  [to_all(): return lax.all_to_all(spread, AXES, 0, 0, tiled=True)]
    all_to_all x2 -> x1, starting transfers between devices: 17.2 us -> 10.3 us  [to_all(): return lax.all_to_all(spread, AXES, 0, 0, tiled=True)]
    ppermute x10, waiting for transfers between devices: 12.5 us -> 9.75 us  [exchange(): out.append(lax.ppermute(arrays[which], axis, pairs))]
    broadcast_in_dim x3, local copies, waits for them, and re-layouts: 3.47 us -> 0.77 us  [to_all(): spread = jnp.broadcast_to(value[None], (count,) + value.shape)]
    unnamed x24 -> x6, local copies, waits for them, and re-layouts: 5.35 us -> 3.15 us
    convert_element_type x0 -> x2, other arithmetic: none -> 1.43 us  [the longest x1 0.76 us: per_device(): (marks + 1).astype(F32)]
  transfers between devices with their start and end apart: 12 -> 11, of which waited for: 6 -> 6; matrix products, arithmetic and copies ran while one was open for 2% -> 0% of each run, Pallas kernels for 9% -> 2%
where the time goes in v1:
time: 97.7 us; the launch traced here: 97.2 us
  Pallas kernels  27.4 us (28%)
  starting transfers between devices  26.7 us (27%)
  blocking collectives  25.9 us (27%)
  waiting for transfers between devices  10.3 us (11%)
  local copies, waits for them, and re-layouts  3.92 us (4%)
  other arithmetic  2.23 us (2%)
    pallas_call x9, Pallas kernels, kernel_call(): pl.pallas_call(body, out_shape=out_shape, in_specs=specs, out_specs=jax.t...  27.4 us
    all_to_all x2, blocking collectives, to_all(): return lax.all_to_all(spread, AXES, 0, 0, tiled=True)  25.9 us
    ppermute x10, starting transfers between devices, exchange(): out.append(lax.ppermute(arrays[which], axis, pairs))  16.4 us
    all_to_all x1, starting transfers between devices, to_all(): return lax.all_to_all(spread, AXES, 0, 0, tiled=True)  10.3 us
    ppermute x10, waiting for transfers between devices, exchange(): out.append(lax.ppermute(arrays[which], axis, pairs))  9.75 us
    unnamed x6, local copies, waits for them, and re-layouts  3.15 us
  transfers between devices with their start and end apart: 11, of which 6 were waited for; matrix products, arithmetic and copies ran while one was open for 0% of the time, Pallas kernels for 2%

profile of v1, /device:TPU:0, one launch (start us, length us, event | category | flops | bytes accessed | tf_op | source)
XLA Modules:
  0.0 97.2 jit_solution(7680628065470258433)
XLA Ops:
  0.6 0.7 convert_bitcast_fusion.1
  1.3 0.8 convert_bitcast_fusion
  2.1 0.7 pad_add_fusion.small.refs_1_
  2.8 0.0 copy-start.2
  2.8 1.0 %copy-done.2 = f32[16,8,8,128]{3,2,1,0:T(8,128)S(1)} copy-done((f32[16,8,8,128]{3,2,1,0:T(8,128)S(1)}, f32[16,8,8,128]{3,2,1,0:T(8,128)}, u32[]{:S(2)}) %copy-start.2) | copy-done | bytes 524312
  3.8 0.7 scatter_first.1
  4.6 0.7 collective-permute-start.1
  5.2 5.9 %collective-permute-start = (bf16[144,128]{1,0:T(8,128)(2,1)S(1)}, bf16[144,128]{1,0:T(8,128)(2,1)S(1)}, u32[]{:S(2)}, u32[]{:S(2)}) collective-permute-start(bf16[144,128]{1,0:T(8,128)(2,1)S(1)} %get-tuple-element.26), channel_id=1, source_target_pairs={{0,1},{1,0},{2,3},{3,2},{4,5},{5,4},{6,7},{7,6},{8,9},{9,8},{10,11... | collective-permute-start | bytes 110600 | tf_op jit(solution)/shard_map/ppermute | solution.py:72
  11.1 0.1 pad_add_fusion.1.place
  11.2 0.0 collective-permute-done.1.refs_3_
  11.2 1.9 %collective-permute-done.refs_2_ = bf16[144,128]{1,0:T(8,128)(2,1)S(1)} collective-permute-done((bf16[144,128]{1,0:T(8,128)(2,1)S(1)}, bf16[144,128]{1,0:T(8,128)(2,1)S(1)}, u32[]{:S(2)}, u32[]{:S(2)}) %collective-permute-start) | collective-permute-done | bytes 36896 | tf_op jit(solution)/shard_map/ppermute | solution.py:72
  13.1 0.6 pack_x.2
  13.7 1.6 %collective-permute-start.2 = (bf16[480,128]{1,0:T(8,128)(2,1)S(1)}, bf16[480,128]{1,0:T(8,128)(2,1)S(1)}, u32[]{:S(2)}, u32[]{:S(2)}) collective-permute-start(bf16[480,128]{1,0:T(8,128)(2,1)S(1)} %get-tuple-element.28), channel_id=1, source_target_pairs={{0,16},{16,0},{1,17},{17,1},{2,18},{18,2},{3,19},{19,3},{4,20},{20... | collective-permute-start | bytes 368648 | tf_op jit(solution)/shard_map/ppermute | solution.py:72
  15.2 3.4 %collective-permute-done.2.refs_3_.refs_0_ = bf16[480,128]{1,0:T(8,128)(2,1)S(1)} collective-permute-done((bf16[480,128]{1,0:T(8,128)(2,1)S(1)}, bf16[480,128]{1,0:T(8,128)(2,1)S(1)}, u32[]{:S(2)}, u32[]{:S(2)}) %collective-permute-start.2) | collective-permute-done | bytes 122912 | tf_op jit(solution)/shard_map/ppermute | solution.py:72
  18.6 0.6 pack_y.2
  19.2 0.1 collective-permute-start.3
  19.3 0.7 collective-permute-start.4
  20.0 0.8 collective-permute-done.3.refs_1_
  20.8 0.0 collective-permute-done.4.refs_2_
  20.8 8.3 %sweeps_first.1 = (f32[1024,128]{1,0:T(8,128)S(1)}, bf16[32,128]{1,0:T(8,128)(2,1)S(1)}, bf16[128,128]{1,0:T(8,128)(2,1)S(1)}, f32[16,16,16,128]{3,2,1,0:T(8,128...) custom-call(s32[3]{0:T(128)S(1)} %pad_add_fusion.1.place, ...), custom_call_target="tpu_custom_call" | custom-call | tf_op jit(solution)/shard_map/sweeps_first/pallas_call | solution.py:45
  29.1 0.0 copy-start
  29.1 0.9 copy-done
  30.1 0.7 broadcast_in_dim.9
  30.8 10.3 %all-to-all-start = ((bf16[32,32,128]{2,1,0:T(8,128)(2,1)}), bf16[32,32,128]{2,1,0:T(8,128)(2,1)S(1)}, u32[]{:S(2)}, u32[]{:S(2)}) async-start(bf16[32,32,128]{2,1,0:T(8,128)(2,1)} %broadcast_in_dim.9), calls=%async_computation | async-start | bytes 524288 | tf_op jit(solution)/shard_map/all_to_all | solution.py:713
  41.1 0.7 collective-permute-start.6
  41.8 4.5 %collective-permute-start.5 = (bf16[128,128]{1,0:T(8,128)(2,1)S(1)}, bf16[128,128]{1,0:T(8,128)(2,1)S(1)}, u32[]{:S(2)}, u32[]{:S(2)}) collective-permute-start(bf16[128,128]{1,0:T(8,128)(2,1)S(1)} %get-tuple-element.35), channel_id=1, source_target_pairs={{0,1},{1,0},{2,3},{3,2},{4,5},{5,4},{6,7},{7,6},{8,9},{9,8},{10,11... | collective-permute-start | bytes 98312 | tf_op jit(solution)/shard_map/ppermute | solution.py:72
  46.3 0.0 collective-permute-done.6.refs_2_
  46.3 2.3 %collective-permute-done.5.refs_1_ = bf16[128,128]{1,0:T(8,128)(2,1)S(1)} collective-permute-done((bf16[128,128]{1,0:T(8,128)(2,1)S(1)}, bf16[128,128]{1,0:T(8,128)(2,1)S(1)}, u32[]{:S(2)}, u32[]{:S(2)}) %collective-permute-start.5) | collective-permute-done | bytes 32800 | tf_op jit(solution)/shard_map/ppermute | solution.py:72
  48.6 0.6 pack_x.3
  49.2 1.5 %collective-permute-start.7 = (bf16[576,128]{1,0:T(8,128)(2,1)S(1)}, bf16[576,128]{1,0:T(8,128)(2,1)S(1)}, u32[]{:S(2)}, u32[]{:S(2)}) collective-permute-start(bf16[576,128]{1,0:T(8,128)(2,1)S(1)} %get-tuple-element.37), channel_id=1, source_target_pairs={{0,16},{16,0},{1,17},{17,1},{2,18},{18,2},{3,19},{19,3},{4,20},{20... | collective-permute-start | bytes 442376 | tf_op jit(solution)/shard_map/ppermute | solution.py:72
  50.8 0.6 all-to-all-done.recv.blocks
  51.3 1.8 %boundary.1 = (bf16[128,4096]{1,0:T(8,128)(2,1)S(1)}, f32[16,128]{1,0:T(8,128)S(1)}, bf16[16,128]{1,0:T(8,128)(2,1)S(1)}) custom-call(f32[88,128]{1,0:T(8,128)S(1)} %pad_add_fusion.small.refs_1_, bf16[32,32,128]{2,1,0:T(8,128)(2,1)S(1)} %all-to-all-done.recv.blocks), custom_call_target="tpu_custom_call" | custom-call | tf_op jit(solution)/shard_map/boundary/pallas_call | solution.py:45
  53.2 1.4 %collective-permute-done.7.refs_2_.refs_0_ = bf16[576,128]{1,0:T(8,128)(2,1)S(1)} collective-permute-done((bf16[576,128]{1,0:T(8,128)(2,1)S(1)}, bf16[576,128]{1,0:T(8,128)(2,1)S(1)}, u32[]{:S(2)}, u32[]{:S(2)}) %collective-permute-start.7) | collective-permute-done | bytes 147488 | tf_op jit(solution)/shard_map/ppermute | solution.py:72
  54.5 0.6 pack_y.3
  55.2 0.1 collective-permute-start.8
  55.2 0.7 collective-permute-start.9
  56.0 15.8 %all_to_all.15.recv = bf16[32,16,128]{2,1,0:T(8,128)(2,1)S(1)} all-to-all(bf16[32,16,128]{2,1,0:T(8,128)(2,1)S(1)} %broadcast_in_dim.10), channel_id=1, replica_groups=mesh['vol'=2,'row'=4,'col'=4] {'vol','row','col'}, dimensions={0} | all-to-all | bytes 262144 | tf_op jit(solution)/shard_map/all_to_all | solution.py:713
  71.8 0.0 collective-permute-done.8.refs_1_
  71.8 0.0 collective-permute-done.9.refs_2_
  71.8 0.0 copy-start.1
  71.8 1.2 %copy-done.1 = f32[7,16,16,128]{3,2,1,0:T(8,128)S(1)} copy-done((f32[7,16,16,128]{3,2,1,0:T(8,128)S(1)}, f32[7,16,16,128]{3,2,1,0:T(8,128)}, u32[]{:S(2)}) %copy-start.1) | copy-done | bytes 917528
  73.0 13.1 %sweeps_last.1 = (f32[1024,128]{1,0:T(8,128)}, bf16[16,128]{1,0:T(8,128)(2,1)S(1)}) custom-call(s32[3]{0:T(128)S(1)} %pad_add_fusion.1.place, f32[1024,128]{1,0:T(8,128)S(1)} %get-tuple-element.31.refs_0_.main, f32[16,128]{1,0:T(8,128)S(1)} %get-tuple-element.33.sums, f32[88,128]{1,0:T(8,128)S(1)} %pad_add_fusion.small.refs_1_, ...), custom_call_target="tpu_custom_call" | custom-call | tf_op jit(solution)/shard_map/sweeps_last/pallas_call | solution.py:45
  86.1 10.1 %all_to_all.16.recv = bf16[32,16,128]{2,1,0:T(8,128)(2,1)S(1)} all-to-all(bf16[32,16,128]{2,1,0:T(8,128)(2,1)S(1)} %broadcast_in_dim.11), channel_id=1, replica_groups=mesh['vol'=2,'row'=4,'col'=4] {'vol','row','col'}, dimensions={0} | all-to-all | bytes 262144 | tf_op jit(solution)/shard_map/all_to_all | solution.py:713
  96.3 1.0 %flux_last.1 = f32[16,128]{1,0:T(8,128)} custom-call(f32[88,128]{1,0:T(8,128)S(1)} %pad_add_fusion.small.refs_1_, bf16[32,16,128]{2,1,0:T(8,128)(2,1)S(1)} %all_to_all.16.recv, bf16[128,4096]{1,0:T(8,128)(2,1)S(1)} %get-tuple-element.47.tiles), custom_call_target="tpu_custom_call" | custom-call | tf_op jit(solution)/shard_map/flux_last/pallas_call | solution.py:45
  (2 shorter events, 0.0 us)
Async XLA Ops:
  2.8 1.0 %copy-start.2 = (f32[16,8,8,128]{3,2,1,0:T(8,128)S(1)}, f32[16,8,8,128]{3,2,1,0:T(8,128)}, u32[]{:S(2)}) copy-start(f32[16,8,8,128]{3,2,1,0:T(8,128)} %param.6) | copy-start | bytes 1572868
  4.6 6.7 %collective-permute-start.1 = (bf16[144,128]{1,0:T(8,128)(2,1)S(1)}, bf16[144,128]{1,0:T(8,128)(2,1)S(1)}, u32[]{:S(2)}, u32[]{:S(2)}) collective-permute-start(bf16[144,128]{1,0:T(8,128)(2,1)S(1)} %get-tuple-element.26), channel_id=1, source_target_pairs={{1,2},{2,1},{5,6},{6,5},{9,10},{10,9},{13,14},{14,13},{17,18},{18,... | collective-permute-start | bytes 110600 | tf_op jit(solution)/shard_map/ppermute | solution.py:72
  5.2 7.8 %collective-permute-start = (bf16[144,128]{1,0:T(8,128)(2,1)S(1)}, bf16[144,128]{1,0:T(8,128)(2,1)S(1)}, u32[]{:S(2)}, u32[]{:S(2)}) collective-permute-start(bf16[144,128]{1,0:T(8,128)(2,1)S(1)} %get-tuple-element.26), channel_id=1, source_target_pairs={{0,1},{1,0},{2,3},{3,2},{4,5},{5,4},{6,7},{7,6},{8,9},{9,8},{10,11... | collective-permute-start | bytes 110600 | tf_op jit(solution)/shard_map/ppermute | solution.py:72
  13.7 4.9 %collective-permute-start.2 = (bf16[480,128]{1,0:T(8,128)(2,1)S(1)}, bf16[480,128]{1,0:T(8,128)(2,1)S(1)}, u32[]{:S(2)}, u32[]{:S(2)}) collective-permute-start(bf16[480,128]{1,0:T(8,128)(2,1)S(1)} %get-tuple-element.28), channel_id=1, source_target_pairs={{0,16},{16,0},{1,17},{17,1},{2,18},{18,2},{3,19},{19,3},{4,20},{20... | collective-permute-start | bytes 368648 | tf_op jit(solution)/shard_map/ppermute | solution.py:72
  19.2 1.6 %collective-permute-start.3 = (bf16[976,128]{1,0:T(8,128)(2,1)S(1)}, bf16[976,128]{1,0:T(8,128)(2,1)S(1)}, u32[]{:S(2)}, u32[]{:S(2)}) collective-permute-start(bf16[976,128]{1,0:T(8,128)(2,1)S(1)} %get-tuple-element.29), channel_id=1, source_target_pairs={{0,4},{4,0},{8,12},{12,8},{1,5},{5,1},{9,13},{13,9},{2,6},{6,2},{1... | collective-permute-start | bytes 749576 | tf_op jit(solution)/shard_map/ppermute | solution.py:72
  19.3 1.5 %collective-permute-start.4 = (bf16[976,128]{1,0:T(8,128)(2,1)S(1)}, bf16[976,128]{1,0:T(8,128)(2,1)S(1)}, u32[]{:S(2)}, u32[]{:S(2)}) collective-permute-start(bf16[976,128]{1,0:T(8,128)(2,1)S(1)} %get-tuple-element.30), channel_id=1, source_target_pairs={{4,8},{8,4},{5,9},{9,5},{6,10},{10,6},{7,11},{11,7},{20,24},{24,20... | collective-permute-start | bytes 749576 | tf_op jit(solution)/shard_map/ppermute | solution.py:72
  29.1 0.9 copy-start
  30.8 20.5 %all-to-all-start = ((bf16[32,32,128]{2,1,0:T(8,128)(2,1)}), bf16[32,32,128]{2,1,0:T(8,128)(2,1)S(1)}, u32[]{:S(2)}, u32[]{:S(2)}) async-start(bf16[32,32,128]{2,1,0:T(8,128)(2,1)} %broadcast_in_dim.9), calls=%async_computation | async-start | bytes 524288 | tf_op jit(solution)/shard_map/all_to_all | solution.py:713
  41.1 5.2 %collective-permute-start.6 = (bf16[128,128]{1,0:T(8,128)(2,1)S(1)}, bf16[128,128]{1,0:T(8,128)(2,1)S(1)}, u32[]{:S(2)}, u32[]{:S(2)}) collective-permute-start(bf16[128,128]{1,0:T(8,128)(2,1)S(1)} %get-tuple-element.35), channel_id=1, source_target_pairs={{1,2},{2,1},{5,6},{6,5},{9,10},{10,9},{13,14},{14,13},{17,18},{18,... | collective-permute-start | bytes 98312 | tf_op jit(solution)/shard_map/ppermute | solution.py:72
  41.8 6.8 %collective-permute-start.5 = (bf16[128,128]{1,0:T(8,128)(2,1)S(1)}, bf16[128,128]{1,0:T(8,128)(2,1)S(1)}, u32[]{:S(2)}, u32[]{:S(2)}) collective-permute-start(bf16[128,128]{1,0:T(8,128)(2,1)S(1)} %get-tuple-element.35), channel_id=1, source_target_pairs={{0,1},{1,0},{2,3},{3,2},{4,5},{5,4},{6,7},{7,6},{8,9},{9,8},{10,11... | collective-permute-start | bytes 98312 | tf_op jit(solution)/shard_map/ppermute | solution.py:72
  49.2 5.3 %collective-permute-start.7 = (bf16[576,128]{1,0:T(8,128)(2,1)S(1)}, bf16[576,128]{1,0:T(8,128)(2,1)S(1)}, u32[]{:S(2)}, u32[]{:S(2)}) collective-permute-start(bf16[576,128]{1,0:T(8,128)(2,1)S(1)} %get-tuple-element.37), channel_id=1, source_target_pairs={{0,16},{16,0},{1,17},{17,1},{2,18},{18,2},{3,19},{19,3},{4,20},{20... | collective-permute-start | bytes 442376 | tf_op jit(solution)/shard_map/ppermute | solution.py:72
  55.2 16.6 %collective-permute-start.8 = (bf16[1280,128]{1,0:T(8,128)(2,1)S(1)}, bf16[1280,128]{1,0:T(8,128)(2,1)S(1)}, u32[]{:S(2)}, u32[]{:S(2)}) collective-permute-start(bf16[1280,128]{1,0:T(8,128)(2,1)S(1)} %get-tuple-element.39), channel_id=1, source_target_pairs={{0,4},{4,0},{8,12},{12,8},{1,5},{5,1},{9,13},{13,9},{2,6},{6,2},{1... | collective-permute-start | bytes 983048 | tf_op jit(solution)/shard_map/ppermute | solution.py:72
  55.2 16.5 %collective-permute-start.9 = (bf16[1280,128]{1,0:T(8,128)(2,1)S(1)}, bf16[1280,128]{1,0:T(8,128)(2,1)S(1)}, u32[]{:S(2)}, u32[]{:S(2)}) collective-permute-start(bf16[1280,128]{1,0:T(8,128)(2,1)S(1)} %get-tuple-element.40), channel_id=1, source_target_pairs={{4,8},{8,4},{5,9},{9,5},{6,10},{10,6},{7,11},{11,7},{20,24},{24,20... | collective-permute-start | bytes 983048 | tf_op jit(solution)/shard_map/ppermute | solution.py:72
  71.8 1.2 %copy-start.1 = (f32[7,16,16,128]{3,2,1,0:T(8,128)S(1)}, f32[7,16,16,128]{3,2,1,0:T(8,128)}, u32[]{:S(2)}) copy-start(f32[7,16,16,128]{3,2,1,0:T(8,128)} %copy-done) | copy-start | bytes 2752516

commit v2 on v1

--- a/solution.py
+++ b/solution.py
@@ -267,44 +267,42 @@
     cx, cy, cz, ch, nodes = dims
     lane = iota((ch, cz), 1)
     first, last = lane == 0, lane == cz - 1
+    k = lane % STRIP
+    group = lane // STRIP
+    touching = (k == HALO) | (k == HALO - 1)
 
     def spread(ref, k, x, y):
         return jnp.broadcast_to(ref[k, x, y:y + 1, :], (ch, cz))
 
-    def column(x, _):
+    def column(x):
+        far = reach - max(HALO - x, x - (HALO + cx - 1), 0)
+        low, high = HALO - far, HALO + cy + far
         beyond = src_strip[x]
-        for y in range(HALO - reach, HALO + cy + reach):
-            here = src[x, y]
-            ends = pltpu.roll(beyond, (2 * cz - (y * STRIP + HALO)) % cz, 1)
-            above = jnp.where(last, ends, pltpu.roll(here, cz - 1, 1))
-            below = jnp.where(first, ends, pltpu.roll(here, 1, 1))
+        ends = jnp.zeros_like(beyond)
+        behind, here = src[x, low - 1], src[x, low]
+        for y in range(low, high):
+            ahead = src[x, y + 1]
+            edge = pltpu.roll(beyond, (2 * cz - (y * STRIP + HALO)) % cz, 1)
+            above = jnp.where(last, edge, pltpu.roll(here, cz - 1, 1))
+            below = jnp.where(first, edge, pltpu.roll(here, 1, 1))
             total = r[x, y] - here
             total += spread(c, 0, x, y) * src[x + 1, y]
             total += spread(c, 1, x, y) * src[x - 1, y]
-            total += spread(c, 2, x, y) * src[x, y + 1]
-            total += spread(c, 3, x, y) * src[x, y - 1]
+            total += spread(c, 2, x, y) * ahead
+            total += spread(c, 3, x, y) * behind
             total += spread(c, 4, x, y) * above
             total += spread(c, 5, x, y) * below
             dst[x, y] = here + weight * total
-        return _
-
-    lax.fori_loop(HALO - reach, HALO + cx + reach, column, 0)
-    if reach == 0:
-        return
-
-    k = lane % STRIP
-    group = lane // STRIP
-    touching = (k == HALO) | (k == HALO - 1)
-
-    def strip_column(x, _):
-        here = src_strip[x]
-        ends = jnp.zeros_like(here)
-        for y in range(HALO - reach + 1, HALO + cy + reach - 1):
-            moved = pltpu.roll(src[x, y], (y * STRIP + HALO) % cz, 1)
-            ends = jnp.where(touching & (group == y), moved, ends)
-
+            if far > 0 and low < y < high - 1:
+                moved = pltpu.roll(here, (y * STRIP + HALO) % cz, 1)
+                ends = jnp.where(touching & (group == y), moved, ends)
+            behind, here = here, ahead
+        if far > 0:
+            strip_column(x, beyond, ends)
+
+    def strip_column(x, here, ends):
         def spread_strip(k):
-            return jnp.broadcast_to(c_strip[k, pl.ds(x, 1), :], (ch, cz))
+            return jnp.broadcast_to(c_strip[k, x:x + 1, :], (ch, cz))
 
         above = jnp.where(k == HALO, ends, pltpu.roll(here, 1, 1))
         below = jnp.where(k == HALO - 1, ends, pltpu.roll(here, cz - 1, 1))
@@ -316,9 +314,9 @@
         total += spread_strip(4) * above
         total += spread_strip(5) * below
         dst_strip[x] = here + weight * total
-        return _
-
-    lax.fori_loop(HALO - reach + 1, HALO + cx + reach - 1, strip_column, 0)
+
+    for x in range(HALO - reach, HALO + cx + reach):
+        column(x)
 
 
 def coefficients(dims, kc, kc_strip, c, c_strip):

time: 97.7 us -> 88.2 us (0.903)
  Pallas kernels: 27.4 us -> 17.9 us
    pallas_call x9, Pallas kernels: 27.4 us -> 17.9 us  [kernel_call(): pl.pallas_call(body, out_shape=out_shape, in_specs=specs, out_specs=jax.t...]
  transfers between devices with their start and end apart: 11 -> 11, of which waited for: 6 -> 6; matrix products, arithmetic and copies ran while one was open for 0% -> 0% of each run, Pallas kernels for 2% -> 3%
where the time goes in v2:
time: 88.2 us; the launch traced here: 87.8 us
  starting transfers between devices  26.7 us (30%)
  blocking collectives  25.9 us (29%)
  Pallas kernels  17.9 us (20%)
  waiting for transfers between devices  10.3 us (12%)
  local copies, waits for them, and re-layouts  3.92 us (4%)
  other arithmetic  2.23 us (3%)
    all_to_all x2, blocking collectives, to_all(): return lax.all_to_all(spread, AXES, 0, 0, tiled=True)  25.9 us
    pallas_call x9, Pallas kernels, kernel_call(): pl.pallas_call(body, out_shape=out_shape, in_specs=specs, out_specs=jax.t...  17.9 us
    ppermute x10, starting transfers between devices, exchange(): out.append(lax.ppermute(arrays[which], axis, pairs))  16.4 us
    all_to_all x1, starting transfers between devices, to_all(): return lax.all_to_all(spread, AXES, 0, 0, tiled=True)  10.3 us
    ppermute x10, waiting for transfers between devices, exchange(): out.append(lax.ppermute(arrays[which], axis, pairs))  9.75 us
    unnamed x6, local copies, waits for them, and re-layouts  3.15 us
  transfers between devices with their start and end apart: 11, of which 6 were waited for; matrix products, arithmetic and copies ran while one was open for 0% of the time, Pallas kernels for 3%

profile of v2, /device:TPU:0, one launch (start us, length us, event | category | flops | bytes accessed | tf_op | source)
XLA Modules:
  0.0 87.8 jit_solution(14980694148505894202)
XLA Ops:
  0.6 0.7 convert_bitcast_fusion.1
  1.3 0.8 convert_bitcast_fusion
  2.1 0.7 pad_add_fusion.small.refs_1_
  2.8 0.0 copy-start.2
  2.8 1.0 %copy-done.2 = f32[16,8,8,128]{3,2,1,0:T(8,128)S(1)} copy-done((f32[16,8,8,128]{3,2,1,0:T(8,128)S(1)}, f32[16,8,8,128]{3,2,1,0:T(8,128)}, u32[]{:S(2)}) %copy-start.2) | copy-done | bytes 524312
  3.8 0.7 scatter_first.1
  4.6 0.7 collective-permute-start.1
  5.2 5.9 %collective-permute-start = (bf16[144,128]{1,0:T(8,128)(2,1)S(1)}, bf16[144,128]{1,0:T(8,128)(2,1)S(1)}, u32[]{:S(2)}, u32[]{:S(2)}) collective-permute-start(bf16[144,128]{1,0:T(8,128)(2,1)S(1)} %get-tuple-element.26), channel_id=1, source_target_pairs={{0,1},{1,0},{2,3},{3,2},{4,5},{5,4},{6,7},{7,6},{8,9},{9,8},{10,11... | collective-permute-start | bytes 110600 | tf_op jit(solution)/shard_map/ppermute | solution.py:72
  11.1 0.1 pad_add_fusion.1.place
  11.2 0.0 collective-permute-done.1.refs_3_
  11.2 1.9 %collective-permute-done.refs_2_ = bf16[144,128]{1,0:T(8,128)(2,1)S(1)} collective-permute-done((bf16[144,128]{1,0:T(8,128)(2,1)S(1)}, bf16[144,128]{1,0:T(8,128)(2,1)S(1)}, u32[]{:S(2)}, u32[]{:S(2)}) %collective-permute-start) | collective-permute-done | bytes 36896 | tf_op jit(solution)/shard_map/ppermute | solution.py:72
  13.1 0.6 pack_x.2
  13.7 1.6 %collective-permute-start.2 = (bf16[480,128]{1,0:T(8,128)(2,1)S(1)}, bf16[480,128]{1,0:T(8,128)(2,1)S(1)}, u32[]{:S(2)}, u32[]{:S(2)}) collective-permute-start(bf16[480,128]{1,0:T(8,128)(2,1)S(1)} %get-tuple-element.28), channel_id=1, source_target_pairs={{0,16},{16,0},{1,17},{17,1},{2,18},{18,2},{3,19},{19,3},{4,20},{20... | collective-permute-start | bytes 368648 | tf_op jit(solution)/shard_map/ppermute | solution.py:72
  15.2 3.4 %collective-permute-done.2.refs_3_.refs_0_ = bf16[480,128]{1,0:T(8,128)(2,1)S(1)} collective-permute-done((bf16[480,128]{1,0:T(8,128)(2,1)S(1)}, bf16[480,128]{1,0:T(8,128)(2,1)S(1)}, u32[]{:S(2)}, u32[]{:S(2)}) %collective-permute-start.2) | collective-permute-done | bytes 122912 | tf_op jit(solution)/shard_map/ppermute | solution.py:72
  18.6 0.6 pack_y.2
  19.2 0.1 collective-permute-start.3
  19.3 0.7 collective-permute-start.4
  20.0 0.8 collective-permute-done.3.refs_1_
  20.8 0.0 collective-permute-done.4.refs_2_
  20.8 5.1 %sweeps_first.1 = (f32[1024,128]{1,0:T(8,128)S(1)}, bf16[32,128]{1,0:T(8,128)(2,1)S(1)}, bf16[128,128]{1,0:T(8,128)(2,1)S(1)}, f32[16,16,16,128]{3,2,1,0:T(8,128...) custom-call(s32[3]{0:T(128)S(1)} %pad_add_fusion.1.place, ...), custom_call_target="tpu_custom_call" | custom-call | tf_op jit(solution)/shard_map/sweeps_first/pallas_call | solution.py:45
  25.9 0.0 copy-start
  25.9 0.9 %copy-done = f32[7,16,16,128]{3,2,1,0:T(8,128)} copy-done((f32[7,16,16,128]{3,2,1,0:T(8,128)}, f32[7,16,16,128]{3,2,1,0:T(8,128)S(1)}, u32[]{:S(2)}) %copy-start) | copy-done | bytes 917528
  26.9 0.7 broadcast_in_dim.9
  27.6 10.3 %all-to-all-start = ((bf16[32,32,128]{2,1,0:T(8,128)(2,1)}), bf16[32,32,128]{2,1,0:T(8,128)(2,1)S(1)}, u32[]{:S(2)}, u32[]{:S(2)}) async-start(bf16[32,32,128]{2,1,0:T(8,128)(2,1)} %broadcast_in_dim.9), calls=%async_computation | async-start | bytes 524288 | tf_op jit(solution)/shard_map/all_to_all | solution.py:711
  37.9 0.7 collective-permute-start.6
  38.6 4.5 %collective-permute-start.5 = (bf16[128,128]{1,0:T(8,128)(2,1)S(1)}, bf16[128,128]{1,0:T(8,128)(2,1)S(1)}, u32[]{:S(2)}, u32[]{:S(2)}) collective-permute-start(bf16[128,128]{1,0:T(8,128)(2,1)S(1)} %get-tuple-element.35), channel_id=1, source_target_pairs={{0,1},{1,0},{2,3},{3,2},{4,5},{5,4},{6,7},{7,6},{8,9},{9,8},{10,11... | collective-permute-start | bytes 98312 | tf_op jit(solution)/shard_map/ppermute | solution.py:72
  43.1 0.0 collective-permute-done.6.refs_2_
  43.1 2.3 %collective-permute-done.5.refs_1_ = bf16[128,128]{1,0:T(8,128)(2,1)S(1)} collective-permute-done((bf16[128,128]{1,0:T(8,128)(2,1)S(1)}, bf16[128,128]{1,0:T(8,128)(2,1)S(1)}, u32[]{:S(2)}, u32[]{:S(2)}) %collective-permute-start.5) | collective-permute-done | bytes 32800 | tf_op jit(solution)/shard_map/ppermute | solution.py:72
  45.4 0.6 pack_x.3
  46.0 1.5 %collective-permute-start.7 = (bf16[576,128]{1,0:T(8,128)(2,1)S(1)}, bf16[576,128]{1,0:T(8,128)(2,1)S(1)}, u32[]{:S(2)}, u32[]{:S(2)}) collective-permute-start(bf16[576,128]{1,0:T(8,128)(2,1)S(1)} %get-tuple-element.37), channel_id=1, source_target_pairs={{0,16},{16,0},{1,17},{17,1},{2,18},{18,2},{3,19},{19,3},{4,20},{20... | collective-permute-start | bytes 442376 | tf_op jit(solution)/shard_map/ppermute | solution.py:72
  47.6 0.6 all-to-all-done.recv.blocks
  48.1 1.8 %boundary.1 = (bf16[128,4096]{1,0:T(8,128)(2,1)S(1)}, f32[16,128]{1,0:T(8,128)S(1)}, bf16[16,128]{1,0:T(8,128)(2,1)S(1)}) custom-call(f32[88,128]{1,0:T(8,128)S(1)} %pad_add_fusion.small.refs_1_, bf16[32,32,128]{2,1,0:T(8,128)(2,1)S(1)} %all-to-all-done.recv.blocks), custom_call_target="tpu_custom_call" | custom-call | tf_op jit(solution)/shard_map/boundary/pallas_call | solution.py:45
  50.0 1.4 %collective-permute-done.7.refs_2_.refs_0_ = bf16[576,128]{1,0:T(8,128)(2,1)S(1)} collective-permute-done((bf16[576,128]{1,0:T(8,128)(2,1)S(1)}, bf16[576,128]{1,0:T(8,128)(2,1)S(1)}, u32[]{:S(2)}, u32[]{:S(2)}) %collective-permute-start.7) | collective-permute-done | bytes 147488 | tf_op jit(solution)/shard_map/ppermute | solution.py:72
  51.3 0.6 pack_y.3
  52.0 0.1 collective-permute-start.8
  52.0 0.7 collective-permute-start.9
  52.8 15.8 %all_to_all.15.recv = bf16[32,16,128]{2,1,0:T(8,128)(2,1)S(1)} all-to-all(bf16[32,16,128]{2,1,0:T(8,128)(2,1)S(1)} %broadcast_in_dim.10), channel_id=1, replica_groups=mesh['vol'=2,'row'=4,'col'=4] {'vol','row','col'}, dimensions={0} | all-to-all | bytes 262144 | tf_op jit(solution)/shard_map/all_to_all | solution.py:711
  68.6 0.0 collective-permute-done.8.refs_1_
  68.6 0.0 collective-permute-done.9.refs_2_
  68.6 0.0 copy-start.1
  68.6 1.2 %copy-done.1 = f32[7,16,16,128]{3,2,1,0:T(8,128)S(1)} copy-done((f32[7,16,16,128]{3,2,1,0:T(8,128)S(1)}, f32[7,16,16,128]{3,2,1,0:T(8,128)}, u32[]{:S(2)}) %copy-start.1) | copy-done | bytes 917528
  69.8 6.9 %sweeps_last.1 = (f32[1024,128]{1,0:T(8,128)}, bf16[16,128]{1,0:T(8,128)(2,1)S(1)}) custom-call(s32[3]{0:T(128)S(1)} %pad_add_fusion.1.place, f32[1024,128]{1,0:T(8,128)S(1)} %get-tuple-element.31.refs_0_.main, f32[16,128]{1,0:T(8,128)S(1)} %get-tuple-element.33.sums, f32[88,128]{1,0:T(8,128)S(1)} %pad_add_fusion.small.refs_1_, ...), custom_call_target="tpu_custom_call" | custom-call | tf_op jit(solution)/shard_map/sweeps_last/pallas_call | solution.py:45
  76.7 10.1 %all_to_all.16.recv = bf16[32,16,128]{2,1,0:T(8,128)(2,1)S(1)} all-to-all(bf16[32,16,128]{2,1,0:T(8,128)(2,1)S(1)} %broadcast_in_dim.11), channel_id=1, replica_groups=mesh['vol'=2,'row'=4,'col'=4] {'vol','row','col'}, dimensions={0} | all-to-all | bytes 262144 | tf_op jit(solution)/shard_map/all_to_all | solution.py:711
  86.8 1.0 %flux_last.1 = f32[16,128]{1,0:T(8,128)} custom-call(f32[88,128]{1,0:T(8,128)S(1)} %pad_add_fusion.small.refs_1_, bf16[32,16,128]{2,1,0:T(8,128)(2,1)S(1)} %all_to_all.16.recv, bf16[128,4096]{1,0:T(8,128)(2,1)S(1)} %get-tuple-element.47.tiles), custom_call_target="tpu_custom_call" | custom-call | tf_op jit(solution)/shard_map/flux_last/pallas_call | solution.py:45
  (2 shorter events, 0.0 us)
Async XLA Ops:
  2.8 1.0 %copy-start.2 = (f32[16,8,8,128]{3,2,1,0:T(8,128)S(1)}, f32[16,8,8,128]{3,2,1,0:T(8,128)}, u32[]{:S(2)}) copy-start(f32[16,8,8,128]{3,2,1,0:T(8,128)} %param.6) | copy-start | bytes 1572868
  4.6 6.7 %collective-permute-start.1 = (bf16[144,128]{1,0:T(8,128)(2,1)S(1)}, bf16[144,128]{1,0:T(8,128)(2,1)S(1)}, u32[]{:S(2)}, u32[]{:S(2)}) collective-permute-start(bf16[144,128]{1,0:T(8,128)(2,1)S(1)} %get-tuple-element.26), channel_id=1, source_target_pairs={{1,2},{2,1},{5,6},{6,5},{9,10},{10,9},{13,14},{14,13},{17,18},{18,... | collective-permute-start | bytes 110600 | tf_op jit(solution)/shard_map/ppermute | solution.py:72
  5.2 7.8 %collective-permute-start = (bf16[144,128]{1,0:T(8,128)(2,1)S(1)}, bf16[144,128]{1,0:T(8,128)(2,1)S(1)}, u32[]{:S(2)}, u32[]{:S(2)}) collective-permute-start(bf16[144,128]{1,0:T(8,128)(2,1)S(1)} %get-tuple-element.26), channel_id=1, source_target_pairs={{0,1},{1,0},{2,3},{3,2},{4,5},{5,4},{6,7},{7,6},{8,9},{9,8},{10,11... | collective-permute-start | bytes 110600 | tf_op jit(solution)/shard_map/ppermute | solution.py:72
  13.7 4.9 %collective-permute-start.2 = (bf16[480,128]{1,0:T(8,128)(2,1)S(1)}, bf16[480,128]{1,0:T(8,128)(2,1)S(1)}, u32[]{:S(2)}, u32[]{:S(2)}) collective-permute-start(bf16[480,128]{1,0:T(8,128)(2,1)S(1)} %get-tuple-element.28), channel_id=1, source_target_pairs={{0,16},{16,0},{1,17},{17,1},{2,18},{18,2},{3,19},{19,3},{4,20},{20... | collective-permute-start | bytes 368648 | tf_op jit(solution)/shard_map/ppermute | solution.py:72
  19.2 1.6 %collective-permute-start.3 = (bf16[976,128]{1,0:T(8,128)(2,1)S(1)}, bf16[976,128]{1,0:T(8,128)(2,1)S(1)}, u32[]{:S(2)}, u32[]{:S(2)}) collective-permute-start(bf16[976,128]{1,0:T(8,128)(2,1)S(1)} %get-tuple-element.29), channel_id=1, source_target_pairs={{0,4},{4,0},{8,12},{12,8},{1,5},{5,1},{9,13},{13,9},{2,6},{6,2},{1... | collective-permute-start | bytes 749576 | tf_op jit(solution)/shard_map/ppermute | solution.py:72
  19.3 1.5 %collective-permute-start.4 = (bf16[976,128]{1,0:T(8,128)(2,1)S(1)}, bf16[976,128]{1,0:T(8,128)(2,1)S(1)}, u32[]{:S(2)}, u32[]{:S(2)}) collective-permute-start(bf16[976,128]{1,0:T(8,128)(2,1)S(1)} %get-tuple-element.30), channel_id=1, source_target_pairs={{4,8},{8,4},{5,9},{9,5},{6,10},{10,6},{7,11},{11,7},{20,24},{24,20... | collective-permute-start | bytes 749576 | tf_op jit(solution)/shard_map/ppermute | solution.py:72
  25.9 0.9 %copy-start = (f32[7,16,16,128]{3,2,1,0:T(8,128)}, f32[7,16,16,128]{3,2,1,0:T(8,128)S(1)}, u32[]{:S(2)}) copy-start(f32[7,16,16,128]{3,2,1,0:T(8,128)S(1)} %get-tuple-element.43.refs_5_) | copy-start | bytes 2752516
  27.6 20.5 %all-to-all-start = ((bf16[32,32,128]{2,1,0:T(8,128)(2,1)}), bf16[32,32,128]{2,1,0:T(8,128)(2,1)S(1)}, u32[]{:S(2)}, u32[]{:S(2)}) async-start(bf16[32,32,128]{2,1,0:T(8,128)(2,1)} %broadcast_in_dim.9), calls=%async_computation | async-start | bytes 524288 | tf_op jit(solution)/shard_map/all_to_all | solution.py:711
  37.9 5.2 %collective-permute-start.6 = (bf16[128,128]{1,0:T(8,128)(2,1)S(1)}, bf16[128,128]{1,0:T(8,128)(2,1)S(1)}, u32[]{:S(2)}, u32[]{:S(2)}) collective-permute-start(bf16[128,128]{1,0:T(8,128)(2,1)S(1)} %get-tuple-element.35), channel_id=1, source_target_pairs={{1,2},{2,1},{5,6},{6,5},{9,10},{10,9},{13,14},{14,13},{17,18},{18,... | collective-permute-start | bytes 98312 | tf_op jit(solution)/shard_map/ppermute | solution.py:72
  38.6 6.8 %collective-permute-start.5 = (bf16[128,128]{1,0:T(8,128)(2,1)S(1)}, bf16[128,128]{1,0:T(8,128)(2,1)S(1)}, u32[]{:S(2)}, u32[]{:S(2)}) collective-permute-start(bf16[128,128]{1,0:T(8,128)(2,1)S(1)} %get-tuple-element.35), channel_id=1, source_target_pairs={{0,1},{1,0},{2,3},{3,2},{4,5},{5,4},{6,7},{7,6},{8,9},{9,8},{10,11... | collective-permute-start | bytes 98312 | tf_op jit(solution)/shard_map/ppermute | solution.py:72
  46.0 5.3 %collective-permute-start.7 = (bf16[576,128]{1,0:T(8,128)(2,1)S(1)}, bf16[576,128]{1,0:T(8,128)(2,1)S(1)}, u32[]{:S(2)}, u32[]{:S(2)}) collective-permute-start(bf16[576,128]{1,0:T(8,128)(2,1)S(1)} %get-tuple-element.37), channel_id=1, source_target_pairs={{0,16},{16,0},{1,17},{17,1},{2,18},{18,2},{3,19},{19,3},{4,20},{20... | collective-permute-start | bytes 442376 | tf_op jit(solution)/shard_map/ppermute | solution.py:72
  52.0 16.6 %collective-permute-start.8 = (bf16[1280,128]{1,0:T(8,128)(2,1)S(1)}, bf16[1280,128]{1,0:T(8,128)(2,1)S(1)}, u32[]{:S(2)}, u32[]{:S(2)}) collective-permute-start(bf16[1280,128]{1,0:T(8,128)(2,1)S(1)} %get-tuple-element.39), channel_id=1, source_target_pairs={{0,4},{4,0},{8,12},{12,8},{1,5},{5,1},{9,13},{13,9},{2,6},{6,2},{1... | collective-permute-start | bytes 983048 | tf_op jit(solution)/shard_map/ppermute | solution.py:72
  52.0 16.5 %collective-permute-start.9 = (bf16[1280,128]{1,0:T(8,128)(2,1)S(1)}, bf16[1280,128]{1,0:T(8,128)(2,1)S(1)}, u32[]{:S(2)}, u32[]{:S(2)}) collective-permute-start(bf16[1280,128]{1,0:T(8,128)(2,1)S(1)} %get-tuple-element.40), channel_id=1, source_target_pairs={{4,8},{8,4},{5,9},{9,5},{6,10},{10,6},{7,11},{11,7},{20,24},{24,20... | collective-permute-start | bytes 983048 | tf_op jit(solution)/shard_map/ppermute | solution.py:72
  68.6 1.2 %copy-start.1 = (f32[7,16,16,128]{3,2,1,0:T(8,128)S(1)}, f32[7,16,16,128]{3,2,1,0:T(8,128)}, u32[]{:S(2)}) copy-start(f32[7,16,16,128]{3,2,1,0:T(8,128)} %copy-done) | copy-start | bytes 2752516

commit v3 on v2

--- a/solution.py
+++ b/solution.py
@@ -36,7 +36,7 @@
     return lax.broadcasted_iota(jnp.int32, shape, dim)
 
 
-def kernel_call(body, out_shape, scratch=(), smem=0, operands=(), name=None):
+def kernel_call(body, out_shape, scratch=(), smem=0, operands=(), cost=None, name=None):
     held = [jnp.shape(leaf) + (leaf.dtype,) for leaf in jax.tree.leaves((out_shape, operands))]
     held += [ref.shape + (ref.dtype,) for ref in scratch]
     need = sum(math.prod(entry[:-1]) * jnp.dtype(entry[-1]).itemsize for entry in held)
@@ -49,8 +49,57 @@
         out_specs=jax.tree.map(lambda _: pl.BlockSpec(memory_space=pltpu.VMEM), out_shape),
         scratch_shapes=list(scratch),
         compiler_params=pltpu.CompilerParams(vmem_limit_bytes=need + SPARE),
+        cost_estimate=cost,
         name=name,
     )(*operands)
+
+
+def layers_left(dims, x, reach):
+    cx = dims[0]
+    return reach - max(HALO - x, x - (HALO + cx - 1), 0)
+
+
+@functools.lru_cache
+def held_rows(dims):
+    cx, cy, cz, ch, nodes = dims
+    starts, total = {}, 0
+    for x in range(cx + 2 * HALO):
+        far = layers_left(dims, x, RHS_HALO)
+        if far >= 0:
+            starts[x] = (total, HALO - far, HALO + cy + far)
+            total += cy + 2 * far
+    return starts, total
+
+
+def row_of(dims, x, y):
+    first, y0, y1 = held_rows(dims)[0][x]
+    return first + y - y0
+
+
+@functools.lru_cache(maxsize=None)
+def kept_row(dims, x, y):
+    cx, cy, cz, ch, nodes = dims
+    starts, total = held_rows(dims)
+    if HALO <= x < HALO + cx and HALO <= y < HALO + cy:
+        return True, (x - HALO) * cy + y - HALO
+    before = 0
+    for other in sorted(starts):
+        first, y0, y1 = starts[other]
+        for at in range(y0, y1):
+            if (other, at) == (x, y):
+                return False, before
+            before += not (HALO <= other < HALO + cx and HALO <= at < HALO + cy)
+    raise KeyError(x, y)
+
+
+def x_sizes(dims, width):
+    cx, cy, cz, ch, nodes = dims
+    return width * cy * ch, (width - 1) * ch
+
+
+def y_sizes(dims, width):
+    cx, cy, cz, ch, nodes = dims
+    return [(cx + 2 * (width - d)) * ch for d in range(1, width + 1)], (cx + 2 * (width - 2)) * ch
 
 
 def pick(refs, low, even, rows, size):
@@ -148,17 +197,16 @@
         (codes,) = refs
         codes[...] = jnp.zeros_like(codes)
         codes[:16, :] = strip_out[cx * ch:, :].astype(F32)
-    slab = width * cy * ch
+    slab, edge = x_sizes(dims, width)
     for which in range(nx):
         upward = even_x if which == 0 else 1 - even_x
         x0 = upward * (cx - width)
         send = sends[which]
         send[:slab, :] = main[pl.ds(pl.multiple_of(x0 * (cy * ch), 16), slab), :].astype(BF16)
-        send[slab:slab + width * ch, :] = strip_out[
-            pl.ds(pl.multiple_of(x0 * ch, 16), width * ch), :
-        ]
+        x0 = upward * (cx - width + 1)
+        send[slab:slab + edge, :] = strip_out[pl.ds(pl.multiple_of(x0 * ch, 16), edge), :]
         if with_labels:
-            start = slab + width * ch
+            start = slab + edge
             x0 = upward * (cx - HALO)
             send[start:start + HALO * cy, :] = (
                 small[pl.ds(pl.multiple_of(INCIDENT + ch + x0 * cy, 8), HALO * cy), :]
@@ -176,33 +224,32 @@
     sends, refs = refs[:ny], refs[ny:]
     even_x = 1 - place[0] % 2
     even_y = 1 - place[1] % 2
-    ex = cx + 2 * width
-    slab = width * cy * ch
+    slab, edge = x_sizes(dims, width)
     if with_labels:
         codes, strip_codes, picked = refs
-        fill_codes(dims, small, strip, xrecv, slab + width * ch, even_x, codes, strip_codes)
+        fill_codes(dims, small, strip, xrecv, slab + edge, even_x, codes, strip_codes)
     for which in range(ny):
         send = sends[which]
         upward = even_y if which == 0 else 1 - even_y
-        y0 = upward * (cy - width)
-        size = width * ch
-        for x in range(ex):
-            if width <= x < width + cx:
-                start = pl.multiple_of(((x - width) * cy + y0) * ch, 16)
-                piece = main[pl.ds(start, size), :].astype(BF16)
-            else:
-                low = x < width
-                start = pl.multiple_of(((x if low else x - width - cx) * cy + y0) * ch, 16)
-                piece = pick(xrecv, low, even_x, start, size)
-            send[x * size:(x + 1) * size, :] = piece
-        start = ex * size
-        send[start:start + width * ch, :] = pick(xrecv, True, even_x, slab, width * ch)
-        send[start + width * ch:start + (width + cx) * ch, :] = strip[:cx * ch, :]
-        send[start + (width + cx) * ch:start + ex * ch, :] = pick(
-            xrecv, False, even_x, slab, width * ch
-        )
+        start = 0
+        for d in range(1, width + 1):
+            y = d - 1 + upward * (cy - 2 * d + 1)
+            for x in range(d - width, cx + width - d):
+                if 0 <= x < cx:
+                    at = pl.multiple_of((x * cy + y) * ch, 16)
+                    piece = main[pl.ds(at, ch), :].astype(BF16)
+                else:
+                    at = pl.multiple_of(((x + width if x < 0 else x - cx) * cy + y) * ch, 16)
+                    piece = pick(xrecv, x < 0, even_x, at, ch)
+                send[start:start + ch, :] = piece
+                start += ch
+        side = (width - 2) * ch
+        send[start:start + side, :] = pick(xrecv, True, even_x, slab + edge - side, side)
+        send[start + side:start + side + cx * ch, :] = strip[:cx * ch, :]
+        start += side + cx * ch
+        send[start:start + side, :] = pick(xrecv, False, even_x, slab, side)
+        start += side
         if with_labels:
-            start += ex * ch
             y0 = upward * (cy - HALO)
             tall = cx + 2 * HALO
             for x in range(tall):
@@ -222,34 +269,39 @@
     strip_codes[HALO + cx:, :] = pick(xrecv, False, even_x, start + side, 16).astype(F32)[:HALO]
 
 
-def assemble(dims, width, main, strip, xrecv, yrecv, even_x, even_y, out, out_strip):
-    cx, cy, cz, ch, nodes = dims
-    ex = cx + 2 * width
-    out[HALO:HALO + cx, HALO:HALO + cy] = main[...].reshape(cx, cy, ch, cz)
-    slab = width * cy * ch
-    low = pick(xrecv, True, even_x, 0, slab).astype(F32)
-    out[HALO - width:HALO, HALO:HALO + cy] = low.reshape(width, cy, ch, cz)
-    high = pick(xrecv, False, even_x, 0, slab).astype(F32)
-    out[HALO + cx:HALO + cx + width, HALO:HALO + cy] = high.reshape(width, cy, ch, cz)
-    size = ex * width * ch
-    low = pick(yrecv, True, even_y, 0, size).astype(F32)
-    out[HALO - width:HALO + cx + width, HALO - width:HALO] = low.reshape(ex, width, ch, cz)
-    high = pick(yrecv, False, even_y, 0, size).astype(F32)
-    out[HALO - width:HALO + cx + width, HALO + cy:HALO + cy + width] = high.reshape(
-        ex, width, ch, cz
-    )
+def assemble(dims, width, main, strip, xrecv, yrecv, even_x, even_y, put, out_strip):
+    cx, cy, cz, ch, nodes = dims
+    slab, edge = x_sizes(dims, width)
+    blocks, y_edge = y_sizes(dims, width)
+    column = cy * ch
+    for x in range(cx):
+        put(HALO + x, HALO, main[x * column:(x + 1) * column, :].reshape(cy, ch, cz))
+    for low in (True, False):
+        x0 = HALO - width if low else HALO + cx
+        for i in range(width):
+            got = pick(xrecv, low, even_x, i * column, column).astype(F32)
+            put(x0 + i, HALO, got.reshape(cy, ch, cz))
+        start = 0
+        for d, size in enumerate(blocks, 1):
+            got = pick(yrecv, low, even_y, start, size).astype(F32).reshape(size // ch, 1, ch, cz)
+            for i in range(size // ch):
+                put(HALO + d - width + i, HALO - d if low else HALO + cy + d - 1, got[i])
+            start += size
     own = jnp.concatenate(
         [
-            pick(xrecv, True, even_x, slab, width * ch),
+            pick(xrecv, True, even_x, slab, edge),
             strip[:cx * ch, :],
-            pick(xrecv, False, even_x, slab, width * ch),
+            pick(xrecv, False, even_x, slab, edge),
         ],
         axis=0,
     ).astype(F32)
-    low = pick(yrecv, True, even_y, size, ex * ch).astype(F32)
-    high = pick(yrecv, False, even_y, size, ex * ch).astype(F32)
+    blank = jnp.zeros((ch, cz), F32)
+    low, high = (
+        jnp.concatenate([blank, pick(yrecv, low, even_y, start, y_edge).astype(F32), blank], axis=0)
+        for low in (True, False)
+    )
     full = join_strips(own, low, high, cy)
-    out_strip[HALO - width:HALO + cx + width] = full.reshape(ex, ch, cz)
+    out_strip[HALO - width + 1:HALO + cx + width - 1] = full.reshape(cx + 2 * width - 2, ch, cz)
 
 
 def join_strips(own, low, high, cy):
@@ -263,7 +315,13 @@
     )
 
 
-def sweep(dims, reach, weight, src, src_strip, dst, dst_strip, r, r_strip, c, c_strip):
+def coefficient(dims, state, k, at):
+    cx, cy, cz, ch, nodes = dims
+    at += cx * cy * ch + held_rows(dims)[1] * k
+    return jnp.broadcast_to(state[at:at + 1, :], (ch, cz))
+
+
+def sweep(dims, reach, weight, src, src_strip, dst, dst_strip, r, r_strip, state, c_strip):
     cx, cy, cz, ch, nodes = dims
     lane = iota((ch, cz), 1)
     first, last = lane == 0, lane == cz - 1
@@ -271,11 +329,8 @@
     group = lane // STRIP
     touching = (k == HALO) | (k == HALO - 1)
 
-    def spread(ref, k, x, y):
-        return jnp.broadcast_to(ref[k, x, y:y + 1, :], (ch, cz))
-
     def column(x):
-        far = reach - max(HALO - x, x - (HALO + cx - 1), 0)
+        far = layers_left(dims, x, reach)
         low, high = HALO - far, HALO + cy + far
         beyond = src_strip[x]
         ends = jnp.zeros_like(beyond)
@@ -285,13 +340,14 @@
             edge = pltpu.roll(beyond, (2 * cz - (y * STRIP + HALO)) % cz, 1)
             above = jnp.where(last, edge, pltpu.roll(here, cz - 1, 1))
             below = jnp.where(first, edge, pltpu.roll(here, 1, 1))
-            total = r[x, y] - here
-            total += spread(c, 0, x, y) * src[x + 1, y]
-            total += spread(c, 1, x, y) * src[x - 1, y]
-            total += spread(c, 2, x, y) * ahead
-            total += spread(c, 3, x, y) * behind
-            total += spread(c, 4, x, y) * above
-            total += spread(c, 5, x, y) * below
+            at = row_of(dims, x, y)
+            total = r[at * ch:(at + 1) * ch, :] - here
+            total += coefficient(dims, state, 0, at) * src[x + 1, y]
+            total += coefficient(dims, state, 1, at) * src[x - 1, y]
+            total += coefficient(dims, state, 2, at) * ahead
+            total += coefficient(dims, state, 3, at) * behind
+            total += coefficient(dims, state, 4, at) * above
+            total += coefficient(dims, state, 5, at) * below
             dst[x, y] = here + weight * total
             if far > 0 and low < y < high - 1:
                 moved = pltpu.roll(here, (y * STRIP + HALO) % cz, 1)
@@ -319,7 +375,7 @@
         column(x)
 
 
-def coefficients(dims, kc, kc_strip, c, c_strip):
+def coefficients(dims, kc, kc_strip, state, c_strip):
     cx, cy, cz, ch, nodes = dims
     tx, ty = cx + 2 * HALO, cy + 2 * HALO
     lane = iota((ty, cz), 1)
@@ -328,8 +384,9 @@
     group = lane // STRIP
     k = lane % STRIP
     touching = ((k == HALO) | (k == HALO - 1)) & (group == y)
-    ends = []
-    for x in range(tx):
+    starts, total = held_rows(dims)
+    ends = [jnp.zeros((1, cz), F32)]
+    for x in range(1, tx - 1):
         own = kc[x + 1, 8:8 + ty, :]
         moved = pltpu.roll(own, HALO, 1, stride=STRIP, stride_axis=0)
         ends.append(jnp.sum(jnp.where(touching, moved, 0.0), axis=0, keepdims=True))
@@ -344,8 +401,11 @@
             jnp.where(lane == cz - 1, upper, pltpu.roll(own, cz - 1, 1)),
             jnp.where(lane == 0, lower, pltpu.roll(own, 1, 1)),
         ]
-        finish(own, others, [c.at[i, x] for i in range(7)])
-    ends = jnp.concatenate(ends, axis=0)
+        first, y0, y1 = starts[x]
+        for i, value in enumerate(finish(own, others)):
+            at = cx * cy * ch + total * i + first
+            state[at:at + y1 - y0, :] = value[y0:y1, :]
+    ends = jnp.concatenate(ends + [jnp.zeros((1, cz), F32)], axis=0)
     lane = iota((tx, cz), 1)
     k = lane % STRIP
     others = [
@@ -356,27 +416,26 @@
         jnp.where(k == HALO, ends, pltpu.roll(here, 1, 1)),
         jnp.where(k == HALO - 1, ends, pltpu.roll(here, cz - 1, 1)),
     ]
-    finish(here, others, [c_strip.at[i] for i in range(7)])
-
-
-def finish(own, others, outs):
+    for i, value in enumerate(finish(here, others)):
+        c_strip[i] = value
+
+
+def finish(own, others):
     faces = [0.5 * (own + other) for other in others]
     diag = MASS_TERM + faces[0]
     for face in faces[1:]:
         diag = diag + face
     inverse = jnp.where(own > 0.0, 1.0 / diag, 0.0)
-    for face, out in zip(faces, outs[:6], strict=True):
-        out[...] = face * inverse
-    outs[6][...] = inverse
-
-
-def smooth(dims, start, fields, strips, r, r_strip, c, c_strip):
+    return [face * inverse for face in faces] + [inverse]
+
+
+def smooth(dims, start, fields, strips, r, r_strip, state, c_strip):
     weights = sweep_weights(SWEEPS)
     now = 0
     for number in range(start, SWEEPS):
         sweep(
             dims, SWEEPS - 1 - number, weights[number], fields[now], strips[now],
-            fields[1 - now], strips[1 - now], r, r_strip, c, c_strip,
+            fields[1 - now], strips[1 - now], r, r_strip, state, c_strip,
         )
         now = 1 - now
     return fields[now]
@@ -397,16 +456,17 @@
 def fourth_kernel(dims, regions, nx, ny, place, main, small, strip, *refs):
     cx, cy, cz, ch, nodes = dims
     xrecv, yrecv, refs = refs[:nx], refs[nx:nx + ny], refs[nx + ny:]
-    field_out, block_out, send_out, r, r_strip, c, c_strip, refs = *refs[:7], refs[7:]
-    fa, fb, sa, sb, kc, kc_strip, codes, strip_codes, side_codes = refs
+    field_out, block_out, send_out, state, kept, c_strip, refs = *refs[:6], refs[6:]
+    r, r_strip, fa, fb, sa, sb, kc, kc_strip, codes, strip_codes, side_codes = refs
     even_x = 1 - place[0] % 2
     even_y = 1 - place[1] % 2
     tx, ty = cx + 2 * HALO, cy + 2 * HALO
     width = RHS_HALO
-    ex = cx + 2 * width
+    slab, edge = x_sizes(dims, width)
+    blocks, y_edge = y_sizes(dims, width)
 
     fill_codes(
-        dims, small, strip, xrecv, width * cy * ch + width * ch, even_x, codes, strip_codes
+        dims, small, strip, xrecv, slab + edge, even_x, codes, strip_codes
     )
     kc[...] = jnp.zeros_like(kc)
     kc_strip[...] = jnp.zeros_like(kc_strip)
@@ -419,7 +479,7 @@
         return value
 
     kc[1:1 + tx, 8 + HALO:8 + HALO + cy] = conductivity(codes[...]).reshape(tx, cy, cz)
-    start = ex * width * ch + ex * ch
+    start = sum(blocks) + y_edge
     for low in (True, False):
         got = pick(yrecv, low, even_y, start, tx * HALO).astype(F32)
         side_codes[...] = conductivity(got)
@@ -430,30 +490,36 @@
     low = pick(yrecv, True, even_y, start, 16).astype(F32)
     high = pick(yrecv, False, even_y, start, 16).astype(F32)
     kc_strip[8:8 + tx, :] = conductivity(join_strips(strip_codes[...], low, high, cy))
-    coefficients(dims, kc, kc_strip, c, c_strip)
-
-    r[...] = jnp.zeros_like(r)
+    coefficients(dims, kc, kc_strip, state, c_strip)
+
     r_strip[...] = jnp.zeros_like(r_strip)
-    assemble(dims, width, main, strip, xrecv, yrecv, even_x, even_y, r, r_strip)
     weight = sweep_weights(SWEEPS)[0]
 
-    def column(x, _):
-        for y in range(HALO - width, HALO + cy + width):
-            value = r[x, y] * jnp.broadcast_to(c[6, x, y:y + 1, :], (ch, cz))
-            r[x, y] = value
-            fa[x, y] = weight * value
-        value = r_strip[x] * jnp.broadcast_to(c_strip[6, pl.ds(x, 1), :], (ch, cz))
+    def put(x, y, rows):
+        for i in range(rows.shape[0]):
+            at = row_of(dims, x, y + i)
+            value = rows[i] * coefficient(dims, state, 6, at)
+            r[at * ch:(at + 1) * ch, :] = value
+            fa[x, y + i] = weight * value
+            inside, at = kept_row(dims, x, y + i)
+            if inside:
+                state[at * ch:(at + 1) * ch, :] = value
+            else:
+                kept[at * ch:(at + 1) * ch, :] = rows[i].astype(BF16)
+
+    assemble(dims, width, main, strip, xrecv, yrecv, even_x, even_y, put, r_strip)
+    tx = cx + 2 * HALO
+    kept[kept.shape[0] - tx * ch:, :] = r_strip[...].reshape(tx * ch, cz).astype(BF16)
+    for x in range(HALO - width, HALO + cx + width):
+        value = r_strip[x] * jnp.broadcast_to(c_strip[6, x:x + 1, :], (ch, cz))
         r_strip[x] = value
         sa[x] = weight * value
-        return _
-
-    lax.fori_loop(HALO - width, HALO + cx + width, column, 0)
-    field = smooth(dims, 1, (fa, fb), (sa, sb), r, r_strip, c, c_strip)
+    field = smooth(dims, 1, (fa, fb), (sa, sb), r, r_strip, state, c_strip)
 
     field_out[...] = field[HALO:HALO + cx, HALO:HALO + cy].reshape(cx * cy * ch, cz)
     send_out[...] = strip_rows(lambda x, y: field[HALO + x, HALO + y], cx, cy, cz)
     row, z = node_places(small)
-    block_out[:ch, :] = gather_nodes(dims, field, row, z)
+    traces = gather_nodes(dims, field, row, z)
     rows = []
     for axis in range(3):
         value = small[axis:axis + 1, :]
@@ -462,10 +528,13 @@
             rows.append(part)
             value = value - part
     rows += [row.astype(F32), z.astype(F32), jnp.zeros((5, nodes), F32)]
-    block_out[ch:, :] = jnp.concatenate(rows, axis=0).astype(BF16)
-
-
-def boundary_kernel(dims, count, scale, small, recv, kernel_out, sum_out, half_out):
+    rest = jnp.concatenate(rows, axis=0).astype(BF16)
+    for other in range(block_out.shape[0]):
+        block_out[other, :ch, :] = traces
+        block_out[other, ch:, :] = rest
+
+
+def tile_kernel(dims, count, scale, small, recv, tiles):
     cx, cy, cz, ch, nodes = dims
     own = [jnp.broadcast_to(small[k:k + 1, :], (nodes, nodes)).T for k in range(3)]
 
@@ -477,13 +546,18 @@
             delta = own[k] - jnp.broadcast_to(other, (nodes, nodes))
             squared = delta * delta if squared is None else squared + delta * delta
         tile = (scale * lax.rsqrt(squared + SOFTENING * SOFTENING)).astype(BF16)
-        kernel_out[:, pl.ds(pl.multiple_of(b * nodes, nodes), nodes)] = tile
+        tiles[:, pl.ds(pl.multiple_of(b * nodes, nodes), nodes)] = tile
         return _
 
     lax.fori_loop(0, count, block, 0)
-    total = product(recv, kernel_out, count, dims)
+
+
+def boundary_kernel(dims, count, scale, small, recv, sum_out, half_out, tiles):
+    tile_kernel(dims, count, scale, small, recv, tiles)
+    total = product(recv, tiles, count, dims)
     sum_out[...] = total
-    half_out[...] = total.astype(BF16)
+    for other in range(count):
+        half_out[other] = total.astype(BF16)
 
 
 def product(recv, tiles, count, dims):
@@ -515,17 +589,24 @@
 def fifth_kernel(dims, sizes, nx, ny, place, main, sums, small, recv, blocks, strip, *refs):
     cx, cy, cz, ch, nodes = dims
     xrecv, yrecv, refs = refs[:nx], refs[nx:nx + ny], refs[nx + ny:]
-    r_in, rs_in, c, c_strip, refs = *refs[:4], refs[4:]
+    state, kept, c_strip, refs = *refs[:3], refs[3:]
     field_out, block_out, refs = *refs[:2], refs[2:]
     r, r_strip, fa, fb, sa, sb, left = refs
     even_x = 1 - place[0] % 2
     even_y = 1 - place[1] % 2
     width = RHS_HALO
-    r[...] = r_in[...]
-    r_strip[...] = rs_in[...]
-    fa[...] = jnp.zeros_like(fa)
+    tx = cx + 2 * HALO
+    for x in range(tx):
+        at = kept.shape[0] - (tx - x) * ch
+        r_strip[x] = kept[at:at + ch, :].astype(F32) * jnp.broadcast_to(
+            c_strip[6, x:x + 1, :], (ch, cz)
+        )
     sa[...] = jnp.zeros_like(sa)
-    assemble(dims, HALO, main, strip, xrecv, yrecv, even_x, even_y, fa, sa)
+
+    def put(x, y, rows):
+        fa[x, y:y + rows.shape[0]] = rows
+
+    assemble(dims, HALO, main, strip, xrecv, yrecv, even_x, even_y, put, sa)
 
     def neighbour(dx, dy, dz):
         at = [place[i] + d for i, d in enumerate((dx, dy, dz))]
@@ -545,6 +626,7 @@
     }
     own_row, own_z = node_places(small)
     strip_lane = iota((cz, nodes), 0)
+    starts = held_rows(dims)[0]
     for dx in (-1, 0, 1):
         x0, x1, back_x = spans[dx]
         edge = []
@@ -561,26 +643,30 @@
                 parts = [value]
             hits = (iota((cz, nodes), 0) == z).astype(BF16)
             hits = jnp.concatenate([hits] * len(parts), axis=1)
-            count = (x1 - x0) * (y1 - y0)
-            at = 0
-            for x in range(x0, x1):
-                for y in range(y0, y1):
-                    wanted = (x - HALO + back_x) * cy + (y - HALO + back_y)
-                    here = jnp.broadcast_to(row == wanted, (ch, nodes))
-                    for i, value in enumerate(parts):
-                        left[at:at + ch, i * nodes:(i + 1) * nodes] = jnp.where(
-                            here, value, 0.0
-                        ).astype(BF16)
-                    at += ch
+            cells = [
+                (x, y) for x in range(x0, x1) for y in range(y0, y1)
+                if starts[x][1] <= y < starts[x][2]
+            ]
+            for at, (x, y) in enumerate(cells):
+                wanted = (x - HALO + back_x) * cy + (y - HALO + back_y)
+                here = jnp.broadcast_to(row == wanted, (ch, nodes))
+                for i, value in enumerate(parts):
+                    left[at * ch:(at + 1) * ch, i * nodes:(i + 1) * nodes] = jnp.where(
+                        here, value, 0.0
+                    ).astype(BF16)
             added = lax.dot_general(
-                left[:at, :len(parts) * nodes], hits, NT, preferred_element_type=F32
+                left[:len(cells) * ch, :len(parts) * nodes], hits, NT, preferred_element_type=F32
             )
-            at = 0
-            for x in range(x0, x1):
-                for y in range(y0, y1):
-                    inverse = jnp.broadcast_to(c[6, x, y:y + 1, :], (ch, cz))
-                    r[x, y] += added[at:at + ch] * inverse
-                    at += ch
+            for i, (x, y) in enumerate(cells):
+                at = row_of(dims, x, y)
+                inverse = coefficient(dims, state, 6, at)
+                more = added[i * ch:(i + 1) * ch]
+                inside, old = kept_row(dims, x, y)
+                if inside:
+                    value = state[old * ch:(old + 1) * ch, :] + more * inverse
+                else:
+                    value = (kept[old * ch:(old + 1) * ch, :].astype(F32) + more) * inverse
+                r[at * ch:(at + 1) * ch, :] = value
             for dz in (-1, 1):
                 value, row, z = neighbour(dx, dy, dz)
                 y = row % cy + cy * dy + HALO
@@ -603,11 +689,13 @@
             inverse = jnp.broadcast_to(c_strip[6, x:x + 1, :], (ch, cz))
             r_strip[x] += added[(x - x0) * ch:(x - x0 + 1) * ch] * inverse
 
-    field = smooth(dims, 0, (fa, fb), (sa, sb), r, r_strip, c, c_strip)
+    field = smooth(dims, 0, (fa, fb), (sa, sb), r, r_strip, state, c_strip)
     for x in range(cx):
         for y in range(cy):
             field_out[pl.ds(x * cy + y, ch, stride=cx * cy), :] = field[HALO + x, HALO + y]
-    block_out[...] = gather_nodes(dims, field, own_row, own_z)
+    traces = gather_nodes(dims, field, own_row, own_z)
+    for other in range(block_out.shape[0]):
+        block_out[other] = traces
 
 
 def per_device(source, labels, region_coeff, node_cell, node_pos, incident):
@@ -619,6 +707,7 @@
     nx, ny, nz = (2 if size > 2 else 1 for size in sizes)
     scale = KERNEL_GAIN / math.sqrt(nodes * count)
     tx, ty = cx + 2 * HALO, cy + 2 * HALO
+    held = held_rows(dims)[1]
     place = jnp.stack([lax.axis_index(axis) for axis in AXES]).astype(jnp.int32)
     rows = cx * cy * ch
     flat = source.reshape(ch * cx * cy, cz)
@@ -656,7 +745,7 @@
         strip, *sends = kernel_call(
             functools.partial(second_kernel, dims, width, with_labels, nz, nx),
             (shape((strip_rows_, cz), BF16),)
-            + (shape((width * cy * ch + width * ch + extra, cz), BF16),) * nx,
+            + (shape((sum(x_sizes(dims, width)) + extra, cz), BF16),) * nx,
             [vmem((32, cz), F32)] if with_labels else [],
             smem=1,
             operands=(place, *own, *zrecv),
@@ -664,11 +753,11 @@
         )
         xrecv = exchange(None, "vol", sends)
         xrecv = between[1](xrecv)
-        ex = cx + 2 * width
         extra = tx * HALO + 16 if with_labels else 0
+        blocks, y_edge = y_sizes(dims, width)
         sends = kernel_call(
             functools.partial(third_kernel, dims, width, with_labels, nx, ny),
-            (shape((ex * width * ch + ex * ch + extra, cz), BF16),) * ny,
+            (shape((sum(blocks) + y_edge + extra, cz), BF16),) * ny,
             [vmem((tx * cy, cz), F32), vmem((tx, cz), F32), vmem((tx * HALO, cz), F32)]
             if with_labels else [],
             smem=1,
@@ -679,18 +768,19 @@
         return strip, xrecv, yrecv
 
     strip, xrecv, yrecv = halo(rhs, send, RHS_HALO, True)
-    field, block, send, r, r_strip, c, c_strip = kernel_call(
+    field, block, send, state, kept, c_strip = kernel_call(
         functools.partial(fourth_kernel, dims, region_coeff.shape[0], nx, ny),
         (
             shape((rows, cz), F32),
-            shape((ch + 16, nodes), BF16),
+            shape((count, ch + 16, nodes), BF16),
             shape((cx * ch, cz), BF16),
-            shape((tx, ty, ch, cz), F32),
-            shape((tx, ch, cz), F32),
-            shape((7, tx, ty, cz), F32),
+            shape((rows + 7 * held, cz), F32),
+            shape(((held - cx * cy + tx) * ch, cz), BF16),
             shape((7, tx, cz), F32),
         ),
         [
+            vmem((held * ch, cz), F32),
+            vmem((tx, ch, cz), F32),
             vmem((tx, ty, ch, cz), F32),
             vmem((tx, ty, ch, cz), F32),
             vmem((tx, ch, cz), F32),
@@ -707,17 +797,16 @@
     )
 
     def to_all(value):
-        spread = jnp.broadcast_to(value[None], (count,) + value.shape)
-        return lax.all_to_all(spread, AXES, 0, 0, tiled=True)
+        return lax.all_to_all(value, AXES, 0, 0, tiled=True)
 
     blocks = to_all(block)
-    tiles, sums, half = kernel_call(
+    sums, half = kernel_call(
         functools.partial(boundary_kernel, dims, count, scale),
         (
-            shape((nodes, count * nodes), BF16),
             shape((ch, nodes), F32),
-            shape((ch, nodes), BF16),
+            shape((count, ch, nodes), BF16),
         ),
+        [vmem((nodes, count * nodes), BF16)],
         operands=(small, blocks),
         name="boundary",
     )
@@ -729,9 +818,9 @@
     recv = to_all(half)
     field, block = kernel_call(
         functools.partial(fifth_kernel, dims, sizes, nx, ny),
-        (shape((ch * cx * cy, cz), F32), shape((ch, nodes), BF16)),
+        (shape((ch * cx * cy, cz), F32), shape((count, ch, nodes), BF16)),
         [
-            vmem((tx, ty, ch, cz), F32),
+            vmem((held * ch, cz), F32),
             vmem((tx, ch, cz), F32),
             vmem((tx, ty, ch, cz), F32),
             vmem((tx, ty, ch, cz), F32),
@@ -741,9 +830,17 @@
         ],
         smem=1,
         operands=(
-            place, field, sums, small, recv, blocks, strip, *xrecv, *yrecv, r, r_strip, c, c_strip
+            place, field, sums, small, recv, blocks, strip, *xrecv, *yrecv, state, kept, c_strip
         ),
         name="sweeps_last",
+    )
+    blocks, block = lax.optimization_barrier((blocks, block))
+    tiles = kernel_call(
+        functools.partial(tile_kernel, dims, count, scale),
+        shape((nodes, count * nodes), BF16),
+        operands=(small, blocks),
+        cost=pl.CostEstimate(flops=10**9, bytes_accessed=10**6, transcendentals=10**6),
+        name="tiles_last",
     )
     flux = kernel_call(
         functools.partial(last_kernel, dims, count),

time: 88.2 us -> 83.1 us (0.942)
  blocking collectives: 25.9 us -> 0 us
  waiting for transfers between devices: 10.3 us -> 22.6 us
  starting transfers between devices: 26.7 us -> 35.7 us
  local copies, waits for them, and re-layouts: 3.92 us -> 1.04 us
  Pallas kernels: 17.9 us -> 20.2 us
    all_to_all x2 -> x0, blocking collectives: 25.9 us -> none  [to_all(): return lax.all_to_all(spread, AXES, 0, 0, tiled=True)]
    all_to_all x1 -> x3, waiting for transfers between devices: 0.56 us -> 13.8 us  [to_all(): return lax.all_to_all(value, AXES, 0, 0, tiled=True)]
    all_to_all x1 -> x3, starting transfers between devices: 10.3 us -> 19.1 us  [to_all(): return lax.all_to_all(value, AXES, 0, 0, tiled=True)]
    pallas_call x9 -> x10, Pallas kernels: 17.9 us -> 20.2 us  [kernel_call(): pl.pallas_call(body, out_shape=out_shape, in_specs=specs, out_specs=jax.t...]
    unnamed x6 -> x2, local copies, waits for them, and re-layouts: 3.15 us -> 1.04 us
    ppermute x10, waiting for transfers between devices: 9.75 us -> 8.81 us  [exchange(): out.append(lax.ppermute(arrays[which], axis, pairs))]
  transfers between devices with their start and end apart: 11 -> 13, of which waited for: 6 -> 8; matrix products, arithmetic and copies ran while one was open for 0% -> 0% of each run, Pallas kernels for 3% -> 6%
where the time goes in v3:
time: 83.1 us; the launch traced here: 82.6 us
  starting transfers between devices  35.7 us (43%)
  waiting for transfers between devices  22.6 us (27%)
  Pallas kernels  20.2 us (24%)
  other arithmetic  2.23 us (3%)
  local copies, waits for them, and re-layouts  1.04 us (1%)
    pallas_call x10, Pallas kernels, kernel_call(): pl.pallas_call(body, out_shape=out_shape, in_specs=specs, out_specs=jax.t...  20.2 us
    all_to_all x3, starting transfers between devices, to_all(): return lax.all_to_all(value, AXES, 0, 0, tiled=True)  19.1 us
    ppermute x10, starting transfers between devices, exchange(): out.append(lax.ppermute(arrays[which], axis, pairs))  16.6 us
    all_to_all x3, waiting for transfers between devices, to_all(): return lax.all_to_all(value, AXES, 0, 0, tiled=True)  13.8 us
    ppermute x10, waiting for transfers between devices, exchange(): out.append(lax.ppermute(arrays[which], axis, pairs))  8.81 us
  transfers between devices with their start and end apart: 13, of which 8 were waited for; matrix products, arithmetic and copies ran while one was open for 0% of the time, Pallas kernels for 6%

profile of v3, /device:TPU:0, one launch (start us, length us, event | category | flops | bytes accessed | tf_op | source)
XLA Modules:
  0.0 82.6 jit_solution(3043009243583948263)
XLA Ops:
  0.6 0.7 convert_bitcast_fusion.1
  1.3 0.8 convert_bitcast_fusion
  2.1 0.7 pad_add_fusion.small.refs_1_
  2.8 0.0 copy-start
  2.8 1.0 %copy-done = f32[16,8,8,128]{3,2,1,0:T(8,128)S(1)} copy-done((f32[16,8,8,128]{3,2,1,0:T(8,128)S(1)}, f32[16,8,8,128]{3,2,1,0:T(8,128)}, u32[]{:S(2)}) %copy-start) | copy-done | bytes 524312
  3.8 0.7 scatter_first.1
  4.6 0.7 collective-permute-start.1
  5.2 5.9 %collective-permute-start = (bf16[144,128]{1,0:T(8,128)(2,1)S(1)}, bf16[144,128]{1,0:T(8,128)(2,1)S(1)}, u32[]{:S(2)}, u32[]{:S(2)}) collective-permute-start(bf16[144,128]{1,0:T(8,128)(2,1)S(1)} %get-tuple-element.26), channel_id=1, source_target_pairs={{0,1},{1,0},{2,3},{3,2},{4,5},{5,4},{6,7},{7,6},{8,9},{9,8},{10,11... | collective-permute-start | bytes 110600 | tf_op jit(solution)/shard_map/ppermute | solution.py:121
  11.1 0.1 pad_add_fusion.1.place
  11.2 0.0 collective-permute-done.1.refs_3_
  11.2 1.9 %collective-permute-done.refs_2_ = bf16[144,128]{1,0:T(8,128)(2,1)S(1)} collective-permute-done((bf16[144,128]{1,0:T(8,128)(2,1)S(1)}, bf16[144,128]{1,0:T(8,128)(2,1)S(1)}, u32[]{:S(2)}, u32[]{:S(2)}) %collective-permute-start) | collective-permute-done | bytes 36896 | tf_op jit(solution)/shard_map/ppermute | solution.py:121
  13.1 0.6 pack_x.2
  13.7 1.6 %collective-permute-start.2 = (bf16[464,128]{1,0:T(8,128)(2,1)S(1)}, bf16[464,128]{1,0:T(8,128)(2,1)S(1)}, u32[]{:S(2)}, u32[]{:S(2)}) collective-permute-start(bf16[464,128]{1,0:T(8,128)(2,1)S(1)} %get-tuple-element.28), channel_id=1, source_target_pairs={{0,16},{16,0},{1,17},{17,1},{2,18},{18,2},{3,19},{19,3},{4,20},{20... | collective-permute-start | bytes 356360 | tf_op jit(solution)/shard_map/ppermute | solution.py:121
  15.2 3.3 %collective-permute-done.2.refs_3_.refs_0_ = bf16[464,128]{1,0:T(8,128)(2,1)S(1)} collective-permute-done((bf16[464,128]{1,0:T(8,128)(2,1)S(1)}, bf16[464,128]{1,0:T(8,128)(2,1)S(1)}, u32[]{:S(2)}, u32[]{:S(2)}) %collective-permute-start.2) | collective-permute-done | bytes 118816 | tf_op jit(solution)/shard_map/ppermute | solution.py:121
  18.6 0.6 pack_y.2
  19.2 0.1 collective-permute-start.3
  19.3 0.7 collective-permute-start.4
  19.9 0.7 collective-permute-done.3.refs_1_
  20.7 0.0 collective-permute-done.4.refs_2_
  20.7 5.3 %sweeps_first.1 = (f32[1024,128]{1,0:T(8,128)S(1)}, bf16[32,32,128]{2,1,0:T(8,128)(2,1)}, bf16[128,128]{1,0:T(8,128)(2,1)S(1)}, f32[2228,128]{1,0:T(8,128)S(1)},...) custom-call(s32[3]{0:T(128)S(1)} %pad_add_fusion.1.place, f32[1024,128]{1,0:T(8,128)S(1)} %get-tuple-element.25.refs_0_.main, ...), custom_call_target="tpu_custom_call" | custom-call | tf_op jit(solution)/shard_map/sweeps_first/pallas_call | solution.py:45
  26.0 9.7 %all-to-all-start = ((bf16[32,32,128]{2,1,0:T(8,128)(2,1)}), bf16[32,32,128]{2,1,0:T(8,128)(2,1)S(1)}, u32[]{:S(2)}, u32[]{:S(2)}) async-start(bf16[32,32,128]{2,1,0:T(8,128)(2,1)} %get-tuple-element.32), calls=%async_computation | async-start | bytes 524288 | tf_op jit(solution)/shard_map/all_to_all | solution.py:800
  35.7 0.7 collective-permute-start.6
  36.4 4.5 %collective-permute-start.5 = (bf16[128,128]{1,0:T(8,128)(2,1)S(1)}, bf16[128,128]{1,0:T(8,128)(2,1)S(1)}, u32[]{:S(2)}, u32[]{:S(2)}) collective-permute-start(bf16[128,128]{1,0:T(8,128)(2,1)S(1)} %get-tuple-element.35), channel_id=1, source_target_pairs={{0,1},{1,0},{2,3},{3,2},{4,5},{5,4},{6,7},{7,6},{8,9},{9,8},{10,11... | collective-permute-start | bytes 98312 | tf_op jit(solution)/shard_map/ppermute | solution.py:121
  40.9 0.0 collective-permute-done.6.refs_2_
  40.9 2.3 %collective-permute-done.5.refs_1_ = bf16[128,128]{1,0:T(8,128)(2,1)S(1)} collective-permute-done((bf16[128,128]{1,0:T(8,128)(2,1)S(1)}, bf16[128,128]{1,0:T(8,128)(2,1)S(1)}, u32[]{:S(2)}, u32[]{:S(2)}) %collective-permute-start.5) | collective-permute-done | bytes 32800 | tf_op jit(solution)/shard_map/ppermute | solution.py:121
  43.2 0.6 pack_x.3
  43.8 1.5 %collective-permute-start.7 = (bf16[560,128]{1,0:T(8,128)(2,1)S(1)}, bf16[560,128]{1,0:T(8,128)(2,1)S(1)}, u32[]{:S(2)}, u32[]{:S(2)}) collective-permute-start(bf16[560,128]{1,0:T(8,128)(2,1)S(1)} %get-tuple-element.37), channel_id=1, source_target_pairs={{0,16},{16,0},{1,17},{17,1},{2,18},{18,2},{3,19},{19,3},{4,20},{20... | collective-permute-start | bytes 430088 | tf_op jit(solution)/shard_map/ppermute | solution.py:121
  45.4 0.6 all-to-all-done.recv.blocks
  45.9 2.5 %boundary.1 = (f32[16,128]{1,0:T(8,128)S(1)}, bf16[32,16,128]{2,1,0:T(8,128)(2,1)}) custom-call(f32[88,128]{1,0:T(8,128)S(1)} %pad_add_fusion.small.refs_1_, bf16[32,32,128]{2,1,0:T(8,128)(2,1)S(1)} %all-to-all-done.recv.blocks), custom_call_target="tpu_custom_call" | custom-call | tf_op jit(solution)/shard_map/boundary/pallas_call | solution.py:45
  48.4 3.9 %all-to-all-start.1 = ((bf16[32,16,128]{2,1,0:T(8,128)(2,1)}), bf16[32,16,128]{2,1,0:T(8,128)(2,1)S(1)}, u32[]{:S(2)}, u32[]{:S(2)}) async-start(bf16[32,16,128]{2,1,0:T(8,128)(2,1)} %get-tuple-element.34), calls=%async_computation.1 | async-start | bytes 262144 | tf_op jit(solution)/shard_map/all_to_all | solution.py:800
  52.3 0.0 collective-permute-done.7.refs_2_.refs_0_
  52.3 0.6 pack_y.3
  52.9 0.3 collective-permute-start.8
  53.2 0.7 collective-permute-start.9
  53.9 0.6 collective-permute-done.8.refs_1_
  54.5 0.0 collective-permute-done.9.refs_2_
  54.5 6.3 %all-to-all-done.1.recv = bf16[32,16,128]{2,1,0:T(8,128)(2,1)S(1)} async-done(((bf16[32,16,128]{2,1,0:T(8,128)(2,1)}), bf16[32,16,128]{2,1,0:T(8,128)(2,1)S(1)}, u32[]{:S(2)}, u32[]{:S(2)}) %all-to-all-start.1) | async-done | bytes 131104 | tf_op jit(solution)/shard_map/all_to_all | solution.py:800
  60.8 6.8 %sweeps_last.1 = (f32[1024,128]{1,0:T(8,128)}, bf16[32,16,128]{2,1,0:T(8,128)(2,1)}) custom-call(s32[3]{0:T(128)S(1)} %pad_add_fusion.1.place, f32[1024,128]{1,0:T(8,128)S(1)} %get-tuple-element.31.refs_0_.main, f32[16,128]{1,0:T(8,128)S(1)} %get-tuple-element.33.sums, f32[88,128]{1,0:T(8,128)S(1)} %pad_add_fusion.small.refs_1_, ...), custom_call_target="tpu_custom_call" | custom-call | tf_op jit(solution)/shard_map/sweeps_last/pallas_call | solution.py:45
  67.7 5.5 %all-to-all-start.2 = ((bf16[32,16,128]{2,1,0:T(8,128)(2,1)}), bf16[32,16,128]{2,1,0:T(8,128)(2,1)S(1)}, u32[]{:S(2)}, u32[]{:S(2)}) async-start(bf16[32,16,128]{2,1,0:T(8,128)(2,1)} %get-tuple-element.46), calls=%async_computation.2 | async-start | bytes 262144 | tf_op jit(solution)/shard_map/all_to_all | solution.py:800
  73.2 1.5 %tiles_last.1.tiles = bf16[128,4096]{1,0:T(8,128)(2,1)S(1)} custom-call(f32[88,128]{1,0:T(8,128)S(1)} %pad_add_fusion.small.refs_1_, bf16[32,32,128]{2,1,0:T(8,128)(2,1)S(1)} %all-to-all-done.recv.blocks), custom_call_target="tpu_custom_call" | custom-call | flops 1000000000 | bytes 1000000 | tf_op jit(solution)/shard_map/tiles_last/pallas_call | solution.py:45
  74.6 6.9 %all-to-all-done.2.recv = bf16[32,16,128]{2,1,0:T(8,128)(2,1)S(1)} async-done(((bf16[32,16,128]{2,1,0:T(8,128)(2,1)}), bf16[32,16,128]{2,1,0:T(8,128)(2,1)S(1)}, u32[]{:S(2)}, u32[]{:S(2)}) %all-to-all-start.2) | async-done | bytes 131104 | tf_op jit(solution)/shard_map/all_to_all | solution.py:800
  81.6 1.0 %flux_last.1 = f32[16,128]{1,0:T(8,128)} custom-call(f32[88,128]{1,0:T(8,128)S(1)} %pad_add_fusion.small.refs_1_, bf16[32,16,128]{2,1,0:T(8,128)(2,1)S(1)} %all-to-all-done.2.recv, bf16[128,4096]{1,0:T(8,128)(2,1)S(1)} %tiles_last.1.tiles), custom_call_target="tpu_custom_call" | custom-call | tf_op jit(solution)/shard_map/flux_last/pallas_call | solution.py:45
Async XLA Ops:
  2.8 1.0 %copy-start = (f32[16,8,8,128]{3,2,1,0:T(8,128)S(1)}, f32[16,8,8,128]{3,2,1,0:T(8,128)}, u32[]{:S(2)}) copy-start(f32[16,8,8,128]{3,2,1,0:T(8,128)} %param.6) | copy-start | bytes 1572868
  4.6 6.7 %collective-permute-start.1 = (bf16[144,128]{1,0:T(8,128)(2,1)S(1)}, bf16[144,128]{1,0:T(8,128)(2,1)S(1)}, u32[]{:S(2)}, u32[]{:S(2)}) collective-permute-start(bf16[144,128]{1,0:T(8,128)(2,1)S(1)} %get-tuple-element.26), channel_id=1, source_target_pairs={{1,2},{2,1},{5,6},{6,5},{9,10},{10,9},{13,14},{14,13},{17,18},{18,... | collective-permute-start | bytes 110600 | tf_op jit(solution)/shard_map/ppermute | solution.py:121
  5.2 7.8 %collective-permute-start = (bf16[144,128]{1,0:T(8,128)(2,1)S(1)}, bf16[144,128]{1,0:T(8,128)(2,1)S(1)}, u32[]{:S(2)}, u32[]{:S(2)}) collective-permute-start(bf16[144,128]{1,0:T(8,128)(2,1)S(1)} %get-tuple-element.26), channel_id=1, source_target_pairs={{0,1},{1,0},{2,3},{3,2},{4,5},{5,4},{6,7},{7,6},{8,9},{9,8},{10,11... | collective-permute-start | bytes 110600 | tf_op jit(solution)/shard_map/ppermute | solution.py:121
  13.7 4.9 %collective-permute-start.2 = (bf16[464,128]{1,0:T(8,128)(2,1)S(1)}, bf16[464,128]{1,0:T(8,128)(2,1)S(1)}, u32[]{:S(2)}, u32[]{:S(2)}) collective-permute-start(bf16[464,128]{1,0:T(8,128)(2,1)S(1)} %get-tuple-element.28), channel_id=1, source_target_pairs={{0,16},{16,0},{1,17},{17,1},{2,18},{18,2},{3,19},{19,3},{4,20},{20... | collective-permute-start | bytes 356360 | tf_op jit(solution)/shard_map/ppermute | solution.py:121
  19.2 1.5 %collective-permute-start.3 = (bf16[720,128]{1,0:T(8,128)(2,1)S(1)}, bf16[720,128]{1,0:T(8,128)(2,1)S(1)}, u32[]{:S(2)}, u32[]{:S(2)}) collective-permute-start(bf16[720,128]{1,0:T(8,128)(2,1)S(1)} %get-tuple-element.29), channel_id=1, source_target_pairs={{0,4},{4,0},{8,12},{12,8},{1,5},{5,1},{9,13},{13,9},{2,6},{6,2},{1... | collective-permute-start | bytes 552968 | tf_op jit(solution)/shard_map/ppermute | solution.py:121
  19.3 1.4 %collective-permute-start.4 = (bf16[720,128]{1,0:T(8,128)(2,1)S(1)}, bf16[720,128]{1,0:T(8,128)(2,1)S(1)}, u32[]{:S(2)}, u32[]{:S(2)}) collective-permute-start(bf16[720,128]{1,0:T(8,128)(2,1)S(1)} %get-tuple-element.30), channel_id=1, source_target_pairs={{4,8},{8,4},{5,9},{9,5},{6,10},{10,6},{7,11},{11,7},{20,24},{24,20... | collective-permute-start | bytes 552968 | tf_op jit(solution)/shard_map/ppermute | solution.py:121
  26.0 19.9 %all-to-all-start = ((bf16[32,32,128]{2,1,0:T(8,128)(2,1)}), bf16[32,32,128]{2,1,0:T(8,128)(2,1)S(1)}, u32[]{:S(2)}, u32[]{:S(2)}) async-start(bf16[32,32,128]{2,1,0:T(8,128)(2,1)} %get-tuple-element.32), calls=%async_computation | async-start | bytes 524288 | tf_op jit(solution)/shard_map/all_to_all | solution.py:800
  35.7 5.2 %collective-permute-start.6 = (bf16[128,128]{1,0:T(8,128)(2,1)S(1)}, bf16[128,128]{1,0:T(8,128)(2,1)S(1)}, u32[]{:S(2)}, u32[]{:S(2)}) collective-permute-start(bf16[128,128]{1,0:T(8,128)(2,1)S(1)} %get-tuple-element.35), channel_id=1, source_target_pairs={{1,2},{2,1},{5,6},{6,5},{9,10},{10,9},{13,14},{14,13},{17,18},{18,... | collective-permute-start | bytes 98312 | tf_op jit(solution)/shard_map/ppermute | solution.py:121
  36.4 6.8 %collective-permute-start.5 = (bf16[128,128]{1,0:T(8,128)(2,1)S(1)}, bf16[128,128]{1,0:T(8,128)(2,1)S(1)}, u32[]{:S(2)}, u32[]{:S(2)}) collective-permute-start(bf16[128,128]{1,0:T(8,128)(2,1)S(1)} %get-tuple-element.35), channel_id=1, source_target_pairs={{0,1},{1,0},{2,3},{3,2},{4,5},{5,4},{6,7},{7,6},{8,9},{9,8},{10,11... | collective-permute-start | bytes 98312 | tf_op jit(solution)/shard_map/ppermute | solution.py:121
  43.8 8.5 %collective-permute-start.7 = (bf16[560,128]{1,0:T(8,128)(2,1)S(1)}, bf16[560,128]{1,0:T(8,128)(2,1)S(1)}, u32[]{:S(2)}, u32[]{:S(2)}) collective-permute-start(bf16[560,128]{1,0:T(8,128)(2,1)S(1)} %get-tuple-element.37), channel_id=1, source_target_pairs={{0,16},{16,0},{1,17},{17,1},{2,18},{18,2},{3,19},{19,3},{4,20},{20... | collective-permute-start | bytes 430088 | tf_op jit(solution)/shard_map/ppermute | solution.py:121
  48.4 12.4 %all-to-all-start.1 = ((bf16[32,16,128]{2,1,0:T(8,128)(2,1)}), bf16[32,16,128]{2,1,0:T(8,128)(2,1)S(1)}, u32[]{:S(2)}, u32[]{:S(2)}) async-start(bf16[32,16,128]{2,1,0:T(8,128)(2,1)} %get-tuple-element.34), calls=%async_computation.1 | async-start | bytes 262144 | tf_op jit(solution)/shard_map/all_to_all | solution.py:800
  52.9 1.6 %collective-permute-start.8 = (bf16[896,128]{1,0:T(8,128)(2,1)S(1)}, bf16[896,128]{1,0:T(8,128)(2,1)S(1)}, u32[]{:S(2)}, u32[]{:S(2)}) collective-permute-start(bf16[896,128]{1,0:T(8,128)(2,1)S(1)} %get-tuple-element.39), channel_id=1, source_target_pairs={{0,4},{4,0},{8,12},{12,8},{1,5},{5,1},{9,13},{13,9},{2,6},{6,2},{1... | collective-permute-start | bytes 688136 | tf_op jit(solution)/shard_map/ppermute | solution.py:121
  53.2 1.2 %collective-permute-start.9 = (bf16[896,128]{1,0:T(8,128)(2,1)S(1)}, bf16[896,128]{1,0:T(8,128)(2,1)S(1)}, u32[]{:S(2)}, u32[]{:S(2)}) collective-permute-start(bf16[896,128]{1,0:T(8,128)(2,1)S(1)} %get-tuple-element.40), channel_id=1, source_target_pairs={{4,8},{8,4},{5,9},{9,5},{6,10},{10,6},{7,11},{11,7},{20,24},{24,20... | collective-permute-start | bytes 688136 | tf_op jit(solution)/shard_map/ppermute | solution.py:121
  67.7 13.9 %all-to-all-start.2 = ((bf16[32,16,128]{2,1,0:T(8,128)(2,1)}), bf16[32,16,128]{2,1,0:T(8,128)(2,1)S(1)}, u32[]{:S(2)}, u32[]{:S(2)}) async-start(bf16[32,16,128]{2,1,0:T(8,128)(2,1)} %get-tuple-element.46), calls=%async_computation.2 | async-start | bytes 262144 | tf_op jit(solution)/shard_map/all_to_all | solution.py:800

commit v4 on v3

--- a/solution.py
+++ b/solution.py
@@ -20,7 +20,7 @@
 STRIP = 2 * HALO
 AXES = ("vol", "row", "col")
 F32, BF16 = jnp.float32, jnp.bfloat16
-ROW, LAYER, REGION, INCIDENT = 3, 4, 5, 8
+CELL, REGION, INCIDENT = 3, 4, 8
 SPARE = 4 * 1024 * 1024
 NT = (((1,), (1,)), ((), ()))
 
@@ -141,7 +141,9 @@
 
 
 def node_places(small):
-    return (small[at:at + 1, :].astype(jnp.int32) for at in (ROW, LAYER))
+    cell = small[CELL:CELL + 1, :].astype(jnp.int32)
+    cz = small.shape[1]
+    return cell // cz, cell % cz
 
 
 def first_kernel(dims, source, small, rhs_out, send_out, left):
@@ -168,7 +170,7 @@
 
     send_out[:cx * ch, :] = strip_rows(read, cx, cy, cz)
     base, lane_y = edge_picker(cz, cz)
-    codes = small[INCIDENT + ch:, :].astype(BF16)
+    codes = (small[INCIDENT + ch:, :] + 1.0).astype(BF16)
     strips = jnp.dot(codes, base.astype(BF16), preferred_element_type=F32)
     own = (iota(strips.shape, 0) % cy) == lane_y[:1, :]
     strips = jnp.where(own, strips, 0.0).reshape(cx, cy, cz).sum(axis=1)
@@ -209,7 +211,7 @@
             start = slab + edge
             x0 = upward * (cx - HALO)
             send[start:start + HALO * cy, :] = (
-                small[pl.ds(pl.multiple_of(INCIDENT + ch + x0 * cy, 8), HALO * cy), :]
+                small[pl.ds(pl.multiple_of(INCIDENT + ch + x0 * cy, 8), HALO * cy), :] + 1.0
             ).astype(BF16)
             send[start + HALO * cy:, :] = codes[pl.ds(x0, 16), :].astype(BF16)
 
@@ -262,7 +264,7 @@
     cx, cy, cz, ch, nodes = dims
     side = HALO * cy
     codes[:side, :] = pick(xrecv, True, even_x, start, side).astype(F32)
-    codes[side:side + cx * cy, :] = small[INCIDENT + ch:, :]
+    codes[side:side + cx * cy, :] = small[INCIDENT + ch:, :] + 1.0
     codes[side + cx * cy:, :] = pick(xrecv, False, even_x, start, side).astype(F32)
     strip_codes[:HALO, :] = pick(xrecv, True, even_x, start + side, 16).astype(F32)[:HALO]
     strip_codes[HALO:HALO + cx, :] = strip[cx * ch:cx * ch + 16, :].astype(F32)[:cx]
@@ -523,15 +525,14 @@
     rows = []
     for axis in range(3):
         value = small[axis:axis + 1, :]
-        for _ in range(3):
+        for _ in range(2):
             part = value.astype(BF16).astype(F32)
             rows.append(part)
             value = value - part
-    rows += [row.astype(F32), z.astype(F32), jnp.zeros((5, nodes), F32)]
-    rest = jnp.concatenate(rows, axis=0).astype(BF16)
+    rows += [row.astype(F32), z.astype(F32)]
+    rest = jnp.concatenate([traces.astype(F32)] + rows, axis=0).astype(BF16)
     for other in range(block_out.shape[0]):
-        block_out[other, :ch, :] = traces
-        block_out[other, ch:, :] = rest
+        block_out[other] = rest
 
 
 def tile_kernel(dims, count, scale, small, recv, tiles):
@@ -539,10 +540,10 @@
     own = [jnp.broadcast_to(small[k:k + 1, :], (nodes, nodes)).T for k in range(3)]
 
     def block(b, _):
-        parts = recv[b, ch:ch + 16, :].astype(F32)
+        parts = recv[b].astype(F32)[ch:]
         squared = None
         for k in range(3):
-            other = parts[3 * k:3 * k + 1] + parts[3 * k + 1:3 * k + 2] + parts[3 * k + 2:3 * k + 3]
+            other = parts[2 * k:2 * k + 1] + parts[2 * k + 1:2 * k + 2]
             delta = own[k] - jnp.broadcast_to(other, (nodes, nodes))
             squared = delta * delta if squared is None else squared + delta * delta
         tile = (scale * lax.rsqrt(squared + SOFTENING * SOFTENING)).astype(BF16)
@@ -565,7 +566,7 @@
     group = math.gcd(count, 32)
 
     def part(at):
-        traces = jnp.concatenate([recv[at + i, :ch, :] for i in range(group)], axis=1)
+        traces = jnp.concatenate([recv[at + i][:ch] for i in range(group)], axis=1)
         start = at * nodes
         if not isinstance(at, int):
             start = pl.multiple_of(start, nodes)
@@ -616,10 +617,10 @@
             good = ok if good is None else good & ok
             at[i] = jnp.clip(at[i], 0, size - 1)
         index = (at[0] * sizes[1] + at[1]) * sizes[2] + at[2]
-        info = blocks[index, ch:ch + 16, :].astype(F32)
+        info = blocks[index].astype(F32)[ch:]
         good = jnp.full((1, nodes), good.astype(jnp.int32), jnp.int32) > 0
-        row = jnp.where(good, info[9:10].astype(jnp.int32), -1)
-        return recv[index].astype(F32), row, info[10:11].astype(jnp.int32)
+        row = jnp.where(good, info[6:7].astype(jnp.int32), -1)
+        return recv[index].astype(F32), row, info[7:8].astype(jnp.int32)
 
     spans = {
         -1: (HALO - width, HALO, cx), 0: (HALO, HALO + cx, 0), 1: (HALO + cx, HALO + cx + width, -cx),
@@ -717,17 +718,17 @@
     vmem = pltpu.VMEM
 
     height = INCIDENT + ch + cx * cy
-    small = jnp.zeros((height, cz), F32)
-    for value, row in (
-        (node_pos, 0),
-        ((cells // cz).astype(F32), ROW),
-        ((cells % cz).astype(F32), LAYER),
-        (region_coeff[None], REGION),
-        (incident, INCIDENT),
-        ((marks + 1).astype(F32), INCIDENT + ch),
-    ):
-        sides = ((row, height - row - value.shape[0], 0), (0, cz - value.shape[1], 0))
-        small += lax.pad(value, jnp.float32(0), sides)
+    floats = ((node_pos, 0), (region_coeff[None], REGION), (incident, INCIDENT))
+    whole = ((cells, CELL), (marks, INCIDENT + ch))
+
+    def lay(entries, dtype):
+        total = jnp.zeros((height, cz), dtype)
+        for value, row in entries:
+            sides = ((row, height - row - value.shape[0], 0), (0, cz - value.shape[1], 0))
+            total += lax.pad(value, jnp.zeros((), dtype), sides)
+        return total
+
+    small = lay(floats, F32) + lay(whole, jnp.int32).astype(F32)
     rhs, send = kernel_call(
         functools.partial(first_kernel, dims),
         (shape((rows, cz), F32), shape((cx * ch + 16, cz), BF16)),
@@ -772,7 +773,7 @@
         functools.partial(fourth_kernel, dims, region_coeff.shape[0], nx, ny),
         (
             shape((rows, cz), F32),
-            shape((count, ch + 16, nodes), BF16),
+            shape((count, ch + 8, nodes), BF16),
             shape((cx * ch, cz), BF16),
             shape((rows + 7 * held, cz), F32),
             shape(((held - cx * cy + tx) * ch, cz), BF16),

time: 83.1 us -> 80.2 us (0.965)
  other arithmetic: 2.23 us -> 0.85 us
    convert_element_type x2 -> x0, other arithmetic: 1.43 us -> none  [the longest x1 0.76 us: per_device(): (marks + 1).astype(F32)]
  transfers between devices with their start and end apart: 13 -> 13, of which waited for: 8 -> 7; matrix products, arithmetic and copies ran while one was open for 0% -> 0% of each run, Pallas kernels for 6% -> 6%
where the time goes in v4:
time: 80.2 us; the launch traced here: 79.7 us
  starting transfers between devices  35 us (44%)
  waiting for transfers between devices  21.9 us (27%)
  Pallas kernels  20.2 us (25%)
  local copies, waits for them, and re-layouts  1.04 us (1%)
  other arithmetic  0.85 us (1%)
    pallas_call x10, Pallas kernels, kernel_call(): pl.pallas_call(body, out_shape=out_shape, in_specs=specs, out_specs=jax.t...  20.2 us
    all_to_all x3, starting transfers between devices, to_all(): return lax.all_to_all(value, AXES, 0, 0, tiled=True)  18.4 us
    ppermute x10, starting transfers between devices, exchange(): out.append(lax.ppermute(arrays[which], axis, pairs))  16.6 us
    all_to_all x3, waiting for transfers between devices, to_all(): return lax.all_to_all(value, AXES, 0, 0, tiled=True)  13.3 us
    ppermute x10, waiting for transfers between devices, exchange(): out.append(lax.ppermute(arrays[which], axis, pairs))  8.59 us
  transfers between devices with their start and end apart: 13, of which 7 were waited for; matrix products, arithmetic and copies ran while one was open for 0% of the time, Pallas kernels for 6%

profile of v4, /device:TPU:0, one launch (start us, length us, event | category | flops | bytes accessed | tf_op | source)
XLA Modules:
  0.0 79.7 jit_solution(10267917688299781699)
XLA Ops:
  0.6 0.8 convert_add_fusion.small.refs_1_
  1.4 0.0 copy-start
  1.4 1.0 %copy-done = f32[16,8,8,128]{3,2,1,0:T(8,128)S(1)} copy-done((f32[16,8,8,128]{3,2,1,0:T(8,128)S(1)}, f32[16,8,8,128]{3,2,1,0:T(8,128)}, u32[]{:S(2)}) %copy-start) | copy-done | bytes 524312
  2.5 0.7 scatter_first.1
  3.2 0.7 collective-permute-start.1
  3.9 5.9 %collective-permute-start = (bf16[144,128]{1,0:T(8,128)(2,1)S(1)}, bf16[144,128]{1,0:T(8,128)(2,1)S(1)}, u32[]{:S(2)}, u32[]{:S(2)}) collective-permute-start(bf16[144,128]{1,0:T(8,128)(2,1)S(1)} %get-tuple-element.26), channel_id=1, source_target_pairs={{0,1},{1,0},{2,3},{3,2},{4,5},{5,4},{6,7},{7,6},{8,9},{9,8},{10,11... | collective-permute-start | bytes 110600 | tf_op jit(solution)/shard_map/ppermute | solution.py:121
  9.8 0.1 pad_add_fusion.place
  9.9 0.0 collective-permute-done.1.refs_3_
  9.9 1.9 %collective-permute-done.refs_2_ = bf16[144,128]{1,0:T(8,128)(2,1)S(1)} collective-permute-done((bf16[144,128]{1,0:T(8,128)(2,1)S(1)}, bf16[144,128]{1,0:T(8,128)(2,1)S(1)}, u32[]{:S(2)}, u32[]{:S(2)}) %collective-permute-start) | collective-permute-done | bytes 36896 | tf_op jit(solution)/shard_map/ppermute | solution.py:121
  11.7 0.6 pack_x.2
  12.3 1.6 %collective-permute-start.2 = (bf16[464,128]{1,0:T(8,128)(2,1)S(1)}, bf16[464,128]{1,0:T(8,128)(2,1)S(1)}, u32[]{:S(2)}, u32[]{:S(2)}) collective-permute-start(bf16[464,128]{1,0:T(8,128)(2,1)S(1)} %get-tuple-element.28), channel_id=1, source_target_pairs={{0,16},{16,0},{1,17},{17,1},{2,18},{18,2},{3,19},{19,3},{4,20},{20... | collective-permute-start | bytes 356360 | tf_op jit(solution)/shard_map/ppermute | solution.py:121
  13.9 3.3 %collective-permute-done.2.refs_3_.refs_0_ = bf16[464,128]{1,0:T(8,128)(2,1)S(1)} collective-permute-done((bf16[464,128]{1,0:T(8,128)(2,1)S(1)}, bf16[464,128]{1,0:T(8,128)(2,1)S(1)}, u32[]{:S(2)}, u32[]{:S(2)}) %collective-permute-start.2) | collective-permute-done | bytes 118816 | tf_op jit(solution)/shard_map/ppermute | solution.py:121
  17.2 0.6 pack_y.2
  17.8 0.1 collective-permute-start.3
  17.9 0.7 collective-permute-start.4
  18.6 0.7 collective-permute-done.3.refs_1_
  19.3 0.0 collective-permute-done.4.refs_2_
  19.3 5.3 %sweeps_first.1 = (f32[1024,128]{1,0:T(8,128)S(1)}, bf16[32,24,128]{2,1,0:T(8,128)(2,1)}, bf16[128,128]{1,0:T(8,128)(2,1)S(1)}, f32[2228,128]{1,0:T(8,128)S(1)},...) custom-call(s32[3]{0:T(128)S(1)} %pad_add_fusion.place, f32[1024,128]{1,0:T(8,128)S(1)} %get-tuple-element.25.refs_0_.main, ...), custom_call_target="tpu_custom_call" | custom-call | tf_op jit(solution)/shard_map/sweeps_first/pallas_call | solution.py:45
  24.6 9.7 %all-to-all-start = ((bf16[32,24,128]{2,1,0:T(8,128)(2,1)}), bf16[32,24,128]{2,1,0:T(8,128)(2,1)S(1)}, u32[]{:S(2)}, u32[]{:S(2)}) async-start(bf16[32,24,128]{2,1,0:T(8,128)(2,1)} %get-tuple-element.32), calls=%async_computation | async-start | bytes 393216 | tf_op jit(solution)/shard_map/all_to_all | solution.py:801
  34.3 0.7 collective-permute-start.6
  35.0 4.5 %collective-permute-start.5 = (bf16[128,128]{1,0:T(8,128)(2,1)S(1)}, bf16[128,128]{1,0:T(8,128)(2,1)S(1)}, u32[]{:S(2)}, u32[]{:S(2)}) collective-permute-start(bf16[128,128]{1,0:T(8,128)(2,1)S(1)} %get-tuple-element.35), channel_id=1, source_target_pairs={{0,1},{1,0},{2,3},{3,2},{4,5},{5,4},{6,7},{7,6},{8,9},{9,8},{10,11... | collective-permute-start | bytes 98312 | tf_op jit(solution)/shard_map/ppermute | solution.py:121
  39.5 0.0 collective-permute-done.6.refs_2_
  39.5 2.1 %collective-permute-done.5.refs_1_ = bf16[128,128]{1,0:T(8,128)(2,1)S(1)} collective-permute-done((bf16[128,128]{1,0:T(8,128)(2,1)S(1)}, bf16[128,128]{1,0:T(8,128)(2,1)S(1)}, u32[]{:S(2)}, u32[]{:S(2)}) %collective-permute-start.5) | collective-permute-done | bytes 32800 | tf_op jit(solution)/shard_map/ppermute | solution.py:121
  41.6 0.6 pack_x.3
  42.2 1.5 %collective-permute-start.7 = (bf16[560,128]{1,0:T(8,128)(2,1)S(1)}, bf16[560,128]{1,0:T(8,128)(2,1)S(1)}, u32[]{:S(2)}, u32[]{:S(2)}) collective-permute-start(bf16[560,128]{1,0:T(8,128)(2,1)S(1)} %get-tuple-element.37), channel_id=1, source_target_pairs={{0,16},{16,0},{1,17},{17,1},{2,18},{18,2},{3,19},{19,3},{4,20},{20... | collective-permute-start | bytes 430088 | tf_op jit(solution)/shard_map/ppermute | solution.py:121
  43.8 0.0 all-to-all-done.recv.blocks
  43.8 2.5 %boundary.1 = (f32[16,128]{1,0:T(8,128)S(1)}, bf16[32,16,128]{2,1,0:T(8,128)(2,1)}) custom-call(f32[88,128]{1,0:T(8,128)S(1)} %convert_add_fusion.small.refs_1_, bf16[32,24,128]{2,1,0:T(8,128)(2,1)S(1)} %all-to-all-done.recv.blocks), custom_call_target="tpu_custom_call" | custom-call | tf_op jit(solution)/shard_map/boundary/pallas_call | solution.py:45
  46.3 3.2 %all-to-all-start.1 = ((bf16[32,16,128]{2,1,0:T(8,128)(2,1)}), bf16[32,16,128]{2,1,0:T(8,128)(2,1)S(1)}, u32[]{:S(2)}, u32[]{:S(2)}) async-start(bf16[32,16,128]{2,1,0:T(8,128)(2,1)} %get-tuple-element.34), calls=%async_computation.1 | async-start | bytes 262144 | tf_op jit(solution)/shard_map/all_to_all | solution.py:801
  49.5 0.0 collective-permute-done.7.refs_2_.refs_0_
  49.5 0.6 pack_y.3
  50.1 0.3 collective-permute-start.8
  50.4 0.7 collective-permute-start.9
  51.1 0.6 collective-permute-done.8.refs_1_
  51.7 0.0 collective-permute-done.9.refs_2_
  51.7 6.3 %all-to-all-done.1.recv = bf16[32,16,128]{2,1,0:T(8,128)(2,1)S(1)} async-done(((bf16[32,16,128]{2,1,0:T(8,128)(2,1)}), bf16[32,16,128]{2,1,0:T(8,128)(2,1)S(1)}, u32[]{:S(2)}, u32[]{:S(2)}) %all-to-all-start.1) | async-done | bytes 131104 | tf_op jit(solution)/shard_map/all_to_all | solution.py:801
  58.0 6.8 %sweeps_last.1 = (f32[1024,128]{1,0:T(8,128)}, bf16[32,16,128]{2,1,0:T(8,128)(2,1)}) custom-call(s32[3]{0:T(128)S(1)} %pad_add_fusion.place, f32[1024,128]{1,0:T(8,128)S(1)} %get-tuple-element.31.refs_0_.main, f32[16,128]{1,0:T(8,128)S(1)} %get-tuple-element.33.sums, f32[88,128]{1,0:T(8,128)S(1)} %convert_add_fusion.small.refs_1_, ...), custom_call_target="tpu_custom_call" | custom-call | tf_op jit(solution)/shard_map/sweeps_last/pallas_call | solution.py:45
  64.8 5.5 %all-to-all-start.2 = ((bf16[32,16,128]{2,1,0:T(8,128)(2,1)}), bf16[32,16,128]{2,1,0:T(8,128)(2,1)S(1)}, u32[]{:S(2)}, u32[]{:S(2)}) async-start(bf16[32,16,128]{2,1,0:T(8,128)(2,1)} %get-tuple-element.46), calls=%async_computation.2 | async-start | bytes 262144 | tf_op jit(solution)/shard_map/all_to_all | solution.py:801
  70.3 1.4 %tiles_last.1.tiles = bf16[128,4096]{1,0:T(8,128)(2,1)S(1)} custom-call(f32[88,128]{1,0:T(8,128)S(1)} %convert_add_fusion.small.refs_1_, bf16[32,24,128]{2,1,0:T(8,128)(2,1)S(1)} %all-to-all-done.recv.blocks), custom_call_target="tpu_custom_call" | custom-call | flops 1000000000 | bytes 1000000 | tf_op jit(solution)/shard_map/tiles_last/pallas_call | solution.py:45
  71.8 6.9 %all-to-all-done.2.recv = bf16[32,16,128]{2,1,0:T(8,128)(2,1)S(1)} async-done(((bf16[32,16,128]{2,1,0:T(8,128)(2,1)}), bf16[32,16,128]{2,1,0:T(8,128)(2,1)S(1)}, u32[]{:S(2)}, u32[]{:S(2)}) %all-to-all-start.2) | async-done | bytes 131104 | tf_op jit(solution)/shard_map/all_to_all | solution.py:801
  78.7 1.0 %flux_last.1 = f32[16,128]{1,0:T(8,128)} custom-call(f32[88,128]{1,0:T(8,128)S(1)} %convert_add_fusion.small.refs_1_, bf16[32,16,128]{2,1,0:T(8,128)(2,1)S(1)} %all-to-all-done.2.recv, bf16[128,4096]{1,0:T(8,128)(2,1)S(1)} %tiles_last.1.tiles), custom_call_target="tpu_custom_call" | custom-call | tf_op jit(solution)/shard_map/flux_last/pallas_call | solution.py:45
Async XLA Ops:
  1.4 1.0 %copy-start = (f32[16,8,8,128]{3,2,1,0:T(8,128)S(1)}, f32[16,8,8,128]{3,2,1,0:T(8,128)}, u32[]{:S(2)}) copy-start(f32[16,8,8,128]{3,2,1,0:T(8,128)} %param.6) | copy-start | bytes 1572868
  3.2 6.7 %collective-permute-start.1 = (bf16[144,128]{1,0:T(8,128)(2,1)S(1)}, bf16[144,128]{1,0:T(8,128)(2,1)S(1)}, u32[]{:S(2)}, u32[]{:S(2)}) collective-permute-start(bf16[144,128]{1,0:T(8,128)(2,1)S(1)} %get-tuple-element.26), channel_id=1, source_target_pairs={{1,2},{2,1},{5,6},{6,5},{9,10},{10,9},{13,14},{14,13},{17,18},{18,... | collective-permute-start | bytes 110600 | tf_op jit(solution)/shard_map/ppermute | solution.py:121
  3.9 7.8 %collective-permute-start = (bf16[144,128]{1,0:T(8,128)(2,1)S(1)}, bf16[144,128]{1,0:T(8,128)(2,1)S(1)}, u32[]{:S(2)}, u32[]{:S(2)}) collective-permute-start(bf16[144,128]{1,0:T(8,128)(2,1)S(1)} %get-tuple-element.26), channel_id=1, source_target_pairs={{0,1},{1,0},{2,3},{3,2},{4,5},{5,4},{6,7},{7,6},{8,9},{9,8},{10,11... | collective-permute-start | bytes 110600 | tf_op jit(solution)/shard_map/ppermute | solution.py:121
  12.3 4.9 %collective-permute-start.2 = (bf16[464,128]{1,0:T(8,128)(2,1)S(1)}, bf16[464,128]{1,0:T(8,128)(2,1)S(1)}, u32[]{:S(2)}, u32[]{:S(2)}) collective-permute-start(bf16[464,128]{1,0:T(8,128)(2,1)S(1)} %get-tuple-element.28), channel_id=1, source_target_pairs={{0,16},{16,0},{1,17},{17,1},{2,18},{18,2},{3,19},{19,3},{4,20},{20... | collective-permute-start | bytes 356360 | tf_op jit(solution)/shard_map/ppermute | solution.py:121
  17.8 1.5 %collective-permute-start.3 = (bf16[720,128]{1,0:T(8,128)(2,1)S(1)}, bf16[720,128]{1,0:T(8,128)(2,1)S(1)}, u32[]{:S(2)}, u32[]{:S(2)}) collective-permute-start(bf16[720,128]{1,0:T(8,128)(2,1)S(1)} %get-tuple-element.29), channel_id=1, source_target_pairs={{0,4},{4,0},{8,12},{12,8},{1,5},{5,1},{9,13},{13,9},{2,6},{6,2},{1... | collective-permute-start | bytes 552968 | tf_op jit(solution)/shard_map/ppermute | solution.py:121
  17.9 1.4 %collective-permute-start.4 = (bf16[720,128]{1,0:T(8,128)(2,1)S(1)}, bf16[720,128]{1,0:T(8,128)(2,1)S(1)}, u32[]{:S(2)}, u32[]{:S(2)}) collective-permute-start(bf16[720,128]{1,0:T(8,128)(2,1)S(1)} %get-tuple-element.30), channel_id=1, source_target_pairs={{4,8},{8,4},{5,9},{9,5},{6,10},{10,6},{7,11},{11,7},{20,24},{24,20... | collective-permute-start | bytes 552968 | tf_op jit(solution)/shard_map/ppermute | solution.py:121
  24.6 19.1 %all-to-all-start = ((bf16[32,24,128]{2,1,0:T(8,128)(2,1)}), bf16[32,24,128]{2,1,0:T(8,128)(2,1)S(1)}, u32[]{:S(2)}, u32[]{:S(2)}) async-start(bf16[32,24,128]{2,1,0:T(8,128)(2,1)} %get-tuple-element.32), calls=%async_computation | async-start | bytes 393216 | tf_op jit(solution)/shard_map/all_to_all | solution.py:801
  34.3 5.2 %collective-permute-start.6 = (bf16[128,128]{1,0:T(8,128)(2,1)S(1)}, bf16[128,128]{1,0:T(8,128)(2,1)S(1)}, u32[]{:S(2)}, u32[]{:S(2)}) collective-permute-start(bf16[128,128]{1,0:T(8,128)(2,1)S(1)} %get-tuple-element.35), channel_id=1, source_target_pairs={{1,2},{2,1},{5,6},{6,5},{9,10},{10,9},{13,14},{14,13},{17,18},{18,... | collective-permute-start | bytes 98312 | tf_op jit(solution)/shard_map/ppermute | solution.py:121
  35.0 6.6 %collective-permute-start.5 = (bf16[128,128]{1,0:T(8,128)(2,1)S(1)}, bf16[128,128]{1,0:T(8,128)(2,1)S(1)}, u32[]{:S(2)}, u32[]{:S(2)}) collective-permute-start(bf16[128,128]{1,0:T(8,128)(2,1)S(1)} %get-tuple-element.35), channel_id=1, source_target_pairs={{0,1},{1,0},{2,3},{3,2},{4,5},{5,4},{6,7},{7,6},{8,9},{9,8},{10,11... | collective-permute-start | bytes 98312 | tf_op jit(solution)/shard_map/ppermute | solution.py:121
  42.2 7.3 %collective-permute-start.7 = (bf16[560,128]{1,0:T(8,128)(2,1)S(1)}, bf16[560,128]{1,0:T(8,128)(2,1)S(1)}, u32[]{:S(2)}, u32[]{:S(2)}) collective-permute-start(bf16[560,128]{1,0:T(8,128)(2,1)S(1)} %get-tuple-element.37), channel_id=1, source_target_pairs={{0,16},{16,0},{1,17},{17,1},{2,18},{18,2},{3,19},{19,3},{4,20},{20... | collective-permute-start | bytes 430088 | tf_op jit(solution)/shard_map/ppermute | solution.py:121
  46.3 11.7 %all-to-all-start.1 = ((bf16[32,16,128]{2,1,0:T(8,128)(2,1)}), bf16[32,16,128]{2,1,0:T(8,128)(2,1)S(1)}, u32[]{:S(2)}, u32[]{:S(2)}) async-start(bf16[32,16,128]{2,1,0:T(8,128)(2,1)} %get-tuple-element.34), calls=%async_computation.1 | async-start | bytes 262144 | tf_op jit(solution)/shard_map/all_to_all | solution.py:801
  50.1 1.6 %collective-permute-start.8 = (bf16[896,128]{1,0:T(8,128)(2,1)S(1)}, bf16[896,128]{1,0:T(8,128)(2,1)S(1)}, u32[]{:S(2)}, u32[]{:S(2)}) collective-permute-start(bf16[896,128]{1,0:T(8,128)(2,1)S(1)} %get-tuple-element.39), channel_id=1, source_target_pairs={{0,4},{4,0},{8,12},{12,8},{1,5},{5,1},{9,13},{13,9},{2,6},{6,2},{1... | collective-permute-start | bytes 688136 | tf_op jit(solution)/shard_map/ppermute | solution.py:121
  50.4 1.2 %collective-permute-start.9 = (bf16[896,128]{1,0:T(8,128)(2,1)S(1)}, bf16[896,128]{1,0:T(8,128)(2,1)S(1)}, u32[]{:S(2)}, u32[]{:S(2)}) collective-permute-start(bf16[896,128]{1,0:T(8,128)(2,1)S(1)} %get-tuple-element.40), channel_id=1, source_target_pairs={{4,8},{8,4},{5,9},{9,5},{6,10},{10,6},{7,11},{11,7},{20,24},{24,20... | collective-permute-start | bytes 688136 | tf_op jit(solution)/shard_map/ppermute | solution.py:121
  64.8 13.9 %all-to-all-start.2 = ((bf16[32,16,128]{2,1,0:T(8,128)(2,1)}), bf16[32,16,128]{2,1,0:T(8,128)(2,1)S(1)}, u32[]{:S(2)}, u32[]{:S(2)}) async-start(bf16[32,16,128]{2,1,0:T(8,128)(2,1)} %get-tuple-element.46), calls=%async_computation.2 | async-start | bytes 262144 | tf_op jit(solution)/shard_map/all_to_all | solution.py:801

commit v5 on v4

--- a/solution.py
+++ b/solution.py
@@ -104,10 +104,11 @@
 
 def pick(refs, low, even, rows, size):
     first = refs[0][pl.ds(rows, size), :]
-    second = refs[1][pl.ds(rows, size), :] if len(refs) > 1 else jnp.zeros_like(first)
     flag = jnp.full(first.shape, even, jnp.int32).astype(first.dtype)
     mine, other = (1 - flag, flag) if low else (flag, 1 - flag)
-    return first * mine + second * other
+    if len(refs) == 1:
+        return first * mine
+    return first * mine + refs[1][pl.ds(rows, size), :] * other
 
 
 def exchange(array, axis, arrays=None):
@@ -339,7 +340,12 @@
         behind, here = src[x, low - 1], src[x, low]
         for y in range(low, high):
             ahead = src[x, y + 1]
-            edge = pltpu.roll(beyond, (2 * cz - (y * STRIP + HALO)) % cz, 1)
+            mirror = 2 * HALO + cy - 1 - y
+            shared = far > 0 and low < y < high - 1
+            both = jnp.where(first | last, src[x, mirror], beyond) if shared else beyond
+            edge = pltpu.roll(both, (2 * cz - (y * STRIP + HALO)) % cz, 1)
+            if shared:
+                ends = jnp.where(touching & (group == mirror), edge, ends)
             above = jnp.where(last, edge, pltpu.roll(here, cz - 1, 1))
             below = jnp.where(first, edge, pltpu.roll(here, 1, 1))
             at = row_of(dims, x, y)
@@ -351,9 +357,6 @@
             total += coefficient(dims, state, 4, at) * above
             total += coefficient(dims, state, 5, at) * below
             dst[x, y] = here + weight * total
-            if far > 0 and low < y < high - 1:
-                moved = pltpu.roll(here, (y * STRIP + HALO) % cz, 1)
-                ends = jnp.where(touching & (group == y), moved, ends)
             behind, here = here, ahead
         if far > 0:
             strip_column(x, beyond, ends)

time: 80.2 us -> 79.6 us (level)
  transfers between devices with their start and end apart: 13 -> 13, of which waited for: 7 -> 7; matrix products, arithmetic and copies ran while one was open for 0% -> 0% of each run, Pallas kernels for 6% -> 7%
where the time goes in v5:
time: 79.6 us; the launch traced here: 79.1 us
  starting transfers between devices  35 us (44%)
  waiting for transfers between devices  21.9 us (28%)
  Pallas kernels  19.6 us (25%)
  local copies, waits for them, and re-layouts  1.04 us (1%)
  other arithmetic  0.85 us (1%)
    pallas_call x10, Pallas kernels, kernel_call(): pl.pallas_call(body, out_shape=out_shape, in_specs=specs, out_specs=jax.t...  19.6 us
    all_to_all x3, starting transfers between devices, to_all(): return lax.all_to_all(value, AXES, 0, 0, tiled=True)  18.4 us
    ppermute x10, starting transfers between devices, exchange(): out.append(lax.ppermute(arrays[which], axis, pairs))  16.6 us
    all_to_all x3, waiting for transfers between devices, to_all(): return lax.all_to_all(value, AXES, 0, 0, tiled=True)  13.3 us
    ppermute x10, waiting for transfers between devices, exchange(): out.append(lax.ppermute(arrays[which], axis, pairs))  8.59 us
  transfers between devices with their start and end apart: 13, of which 7 were waited for; matrix products, arithmetic and copies ran while one was open for 0% of the time, Pallas kernels for 7%

profile of v5, /device:TPU:0, one launch (start us, length us, event | category | flops | bytes accessed | tf_op | source)
XLA Modules:
  0.0 79.1 jit_solution(44987346695496971)
XLA Ops:
  0.6 0.8 convert_add_fusion.small.refs_1_
  1.4 0.0 copy-start
  1.4 1.0 %copy-done = f32[16,8,8,128]{3,2,1,0:T(8,128)S(1)} copy-done((f32[16,8,8,128]{3,2,1,0:T(8,128)S(1)}, f32[16,8,8,128]{3,2,1,0:T(8,128)}, u32[]{:S(2)}) %copy-start) | copy-done | bytes 524312
  2.5 0.7 scatter_first.1
  3.2 0.7 collective-permute-start.1
  3.9 5.9 %collective-permute-start = (bf16[144,128]{1,0:T(8,128)(2,1)S(1)}, bf16[144,128]{1,0:T(8,128)(2,1)S(1)}, u32[]{:S(2)}, u32[]{:S(2)}) collective-permute-start(bf16[144,128]{1,0:T(8,128)(2,1)S(1)} %get-tuple-element.26), channel_id=1, source_target_pairs={{0,1},{1,0},{2,3},{3,2},{4,5},{5,4},{6,7},{7,6},{8,9},{9,8},{10,11... | collective-permute-start | bytes 110600 | tf_op jit(solution)/shard_map/ppermute | solution.py:122
  9.8 0.1 pad_add_fusion.place
  9.9 0.0 collective-permute-done.1.refs_3_
  9.9 1.9 %collective-permute-done.refs_2_ = bf16[144,128]{1,0:T(8,128)(2,1)S(1)} collective-permute-done((bf16[144,128]{1,0:T(8,128)(2,1)S(1)}, bf16[144,128]{1,0:T(8,128)(2,1)S(1)}, u32[]{:S(2)}, u32[]{:S(2)}) %collective-permute-start) | collective-permute-done | bytes 36896 | tf_op jit(solution)/shard_map/ppermute | solution.py:122
  11.7 0.6 pack_x.2
  12.3 1.6 %collective-permute-start.2 = (bf16[464,128]{1,0:T(8,128)(2,1)S(1)}, bf16[464,128]{1,0:T(8,128)(2,1)S(1)}, u32[]{:S(2)}, u32[]{:S(2)}) collective-permute-start(bf16[464,128]{1,0:T(8,128)(2,1)S(1)} %get-tuple-element.28), channel_id=1, source_target_pairs={{0,16},{16,0},{1,17},{17,1},{2,18},{18,2},{3,19},{19,3},{4,20},{20... | collective-permute-start | bytes 356360 | tf_op jit(solution)/shard_map/ppermute | solution.py:122
  13.9 3.3 %collective-permute-done.2.refs_3_.refs_0_ = bf16[464,128]{1,0:T(8,128)(2,1)S(1)} collective-permute-done((bf16[464,128]{1,0:T(8,128)(2,1)S(1)}, bf16[464,128]{1,0:T(8,128)(2,1)S(1)}, u32[]{:S(2)}, u32[]{:S(2)}) %collective-permute-start.2) | collective-permute-done | bytes 118816 | tf_op jit(solution)/shard_map/ppermute | solution.py:122
  17.2 0.6 pack_y.2
  17.8 0.1 collective-permute-start.3
  17.9 0.7 collective-permute-start.4
  18.6 0.7 collective-permute-done.3.refs_1_
  19.3 0.0 collective-permute-done.4.refs_2_
  19.3 5.0 %sweeps_first.1 = (f32[1024,128]{1,0:T(8,128)S(1)}, bf16[32,24,128]{2,1,0:T(8,128)(2,1)}, bf16[128,128]{1,0:T(8,128)(2,1)S(1)}, f32[2228,128]{1,0:T(8,128)S(1)},...) custom-call(s32[3]{0:T(128)S(1)} %pad_add_fusion.place, f32[1024,128]{1,0:T(8,128)S(1)} %get-tuple-element.25.refs_0_.main, ...), custom_call_target="tpu_custom_call" | custom-call | tf_op jit(solution)/shard_map/sweeps_first/pallas_call | solution.py:45
  24.3 9.7 %all-to-all-start = ((bf16[32,24,128]{2,1,0:T(8,128)(2,1)}), bf16[32,24,128]{2,1,0:T(8,128)(2,1)S(1)}, u32[]{:S(2)}, u32[]{:S(2)}) async-start(bf16[32,24,128]{2,1,0:T(8,128)(2,1)} %get-tuple-element.32), calls=%async_computation | async-start | bytes 393216 | tf_op jit(solution)/shard_map/all_to_all | solution.py:804
  34.0 0.7 collective-permute-start.6
  34.7 4.5 %collective-permute-start.5 = (bf16[128,128]{1,0:T(8,128)(2,1)S(1)}, bf16[128,128]{1,0:T(8,128)(2,1)S(1)}, u32[]{:S(2)}, u32[]{:S(2)}) collective-permute-start(bf16[128,128]{1,0:T(8,128)(2,1)S(1)} %get-tuple-element.35), channel_id=1, source_target_pairs={{0,1},{1,0},{2,3},{3,2},{4,5},{5,4},{6,7},{7,6},{8,9},{9,8},{10,11... | collective-permute-start | bytes 98312 | tf_op jit(solution)/shard_map/ppermute | solution.py:122
  39.2 0.0 collective-permute-done.6.refs_2_
  39.3 2.1 %collective-permute-done.5.refs_1_ = bf16[128,128]{1,0:T(8,128)(2,1)S(1)} collective-permute-done((bf16[128,128]{1,0:T(8,128)(2,1)S(1)}, bf16[128,128]{1,0:T(8,128)(2,1)S(1)}, u32[]{:S(2)}, u32[]{:S(2)}) %collective-permute-start.5) | collective-permute-done | bytes 32800 | tf_op jit(solution)/shard_map/ppermute | solution.py:122
  41.3 0.6 pack_x.3
  41.9 1.5 %collective-permute-start.7 = (bf16[560,128]{1,0:T(8,128)(2,1)S(1)}, bf16[560,128]{1,0:T(8,128)(2,1)S(1)}, u32[]{:S(2)}, u32[]{:S(2)}) collective-permute-start(bf16[560,128]{1,0:T(8,128)(2,1)S(1)} %get-tuple-element.37), channel_id=1, source_target_pairs={{0,16},{16,0},{1,17},{17,1},{2,18},{18,2},{3,19},{19,3},{4,20},{20... | collective-permute-start | bytes 430088 | tf_op jit(solution)/shard_map/ppermute | solution.py:122
  43.5 0.0 all-to-all-done.recv.blocks
  43.5 2.5 %boundary.1 = (f32[16,128]{1,0:T(8,128)S(1)}, bf16[32,16,128]{2,1,0:T(8,128)(2,1)}) custom-call(f32[88,128]{1,0:T(8,128)S(1)} %convert_add_fusion.small.refs_1_, bf16[32,24,128]{2,1,0:T(8,128)(2,1)S(1)} %all-to-all-done.recv.blocks), custom_call_target="tpu_custom_call" | custom-call | tf_op jit(solution)/shard_map/boundary/pallas_call | solution.py:45
  46.0 3.2 %all-to-all-start.1 = ((bf16[32,16,128]{2,1,0:T(8,128)(2,1)}), bf16[32,16,128]{2,1,0:T(8,128)(2,1)S(1)}, u32[]{:S(2)}, u32[]{:S(2)}) async-start(bf16[32,16,128]{2,1,0:T(8,128)(2,1)} %get-tuple-element.34), calls=%async_computation.1 | async-start | bytes 262144 | tf_op jit(solution)/shard_map/all_to_all | solution.py:804
  49.2 0.0 collective-permute-done.7.refs_2_.refs_0_
  49.2 0.6 pack_y.3
  49.8 0.3 collective-permute-start.8
  50.1 0.7 collective-permute-start.9
  50.8 0.6 collective-permute-done.8.refs_1_
  51.4 0.0 collective-permute-done.9.refs_2_
  51.4 6.3 %all-to-all-done.1.recv = bf16[32,16,128]{2,1,0:T(8,128)(2,1)S(1)} async-done(((bf16[32,16,128]{2,1,0:T(8,128)(2,1)}), bf16[32,16,128]{2,1,0:T(8,128)(2,1)S(1)}, u32[]{:S(2)}, u32[]{:S(2)}) %all-to-all-start.1) | async-done | bytes 131104 | tf_op jit(solution)/shard_map/all_to_all | solution.py:804
  57.7 6.5 %sweeps_last.1 = (f32[1024,128]{1,0:T(8,128)}, bf16[32,16,128]{2,1,0:T(8,128)(2,1)}) custom-call(s32[3]{0:T(128)S(1)} %pad_add_fusion.place, f32[1024,128]{1,0:T(8,128)S(1)} %get-tuple-element.31.refs_0_.main, f32[16,128]{1,0:T(8,128)S(1)} %get-tuple-element.33.sums, f32[88,128]{1,0:T(8,128)S(1)} %convert_add_fusion.small.refs_1_, ...), custom_call_target="tpu_custom_call" | custom-call | tf_op jit(solution)/shard_map/sweeps_last/pallas_call | solution.py:45
  64.2 5.5 %all-to-all-start.2 = ((bf16[32,16,128]{2,1,0:T(8,128)(2,1)}), bf16[32,16,128]{2,1,0:T(8,128)(2,1)S(1)}, u32[]{:S(2)}, u32[]{:S(2)}) async-start(bf16[32,16,128]{2,1,0:T(8,128)(2,1)} %get-tuple-element.46), calls=%async_computation.2 | async-start | bytes 262144 | tf_op jit(solution)/shard_map/all_to_all | solution.py:804
  69.7 1.4 %tiles_last.1.tiles = bf16[128,4096]{1,0:T(8,128)(2,1)S(1)} custom-call(f32[88,128]{1,0:T(8,128)S(1)} %convert_add_fusion.small.refs_1_, bf16[32,24,128]{2,1,0:T(8,128)(2,1)S(1)} %all-to-all-done.recv.blocks), custom_call_target="tpu_custom_call" | custom-call | flops 1000000000 | bytes 1000000 | tf_op jit(solution)/shard_map/tiles_last/pallas_call | solution.py:45
  71.2 6.9 %all-to-all-done.2.recv = bf16[32,16,128]{2,1,0:T(8,128)(2,1)S(1)} async-done(((bf16[32,16,128]{2,1,0:T(8,128)(2,1)}), bf16[32,16,128]{2,1,0:T(8,128)(2,1)S(1)}, u32[]{:S(2)}, u32[]{:S(2)}) %all-to-all-start.2) | async-done | bytes 131104 | tf_op jit(solution)/shard_map/all_to_all | solution.py:804
  78.1 1.0 %flux_last.1 = f32[16,128]{1,0:T(8,128)} custom-call(f32[88,128]{1,0:T(8,128)S(1)} %convert_add_fusion.small.refs_1_, bf16[32,16,128]{2,1,0:T(8,128)(2,1)S(1)} %all-to-all-done.2.recv, bf16[128,4096]{1,0:T(8,128)(2,1)S(1)} %tiles_last.1.tiles), custom_call_target="tpu_custom_call" | custom-call | tf_op jit(solution)/shard_map/flux_last/pallas_call | solution.py:45
Async XLA Ops:
  1.4 1.0 %copy-start = (f32[16,8,8,128]{3,2,1,0:T(8,128)S(1)}, f32[16,8,8,128]{3,2,1,0:T(8,128)}, u32[]{:S(2)}) copy-start(f32[16,8,8,128]{3,2,1,0:T(8,128)} %param.6) | copy-start | bytes 1572868
  3.2 6.7 %collective-permute-start.1 = (bf16[144,128]{1,0:T(8,128)(2,1)S(1)}, bf16[144,128]{1,0:T(8,128)(2,1)S(1)}, u32[]{:S(2)}, u32[]{:S(2)}) collective-permute-start(bf16[144,128]{1,0:T(8,128)(2,1)S(1)} %get-tuple-element.26), channel_id=1, source_target_pairs={{1,2},{2,1},{5,6},{6,5},{9,10},{10,9},{13,14},{14,13},{17,18},{18,... | collective-permute-start | bytes 110600 | tf_op jit(solution)/shard_map/ppermute | solution.py:122
  3.9 7.8 %collective-permute-start = (bf16[144,128]{1,0:T(8,128)(2,1)S(1)}, bf16[144,128]{1,0:T(8,128)(2,1)S(1)}, u32[]{:S(2)}, u32[]{:S(2)}) collective-permute-start(bf16[144,128]{1,0:T(8,128)(2,1)S(1)} %get-tuple-element.26), channel_id=1, source_target_pairs={{0,1},{1,0},{2,3},{3,2},{4,5},{5,4},{6,7},{7,6},{8,9},{9,8},{10,11... | collective-permute-start | bytes 110600 | tf_op jit(solution)/shard_map/ppermute | solution.py:122
  12.3 4.9 %collective-permute-start.2 = (bf16[464,128]{1,0:T(8,128)(2,1)S(1)}, bf16[464,128]{1,0:T(8,128)(2,1)S(1)}, u32[]{:S(2)}, u32[]{:S(2)}) collective-permute-start(bf16[464,128]{1,0:T(8,128)(2,1)S(1)} %get-tuple-element.28), channel_id=1, source_target_pairs={{0,16},{16,0},{1,17},{17,1},{2,18},{18,2},{3,19},{19,3},{4,20},{20... | collective-permute-start | bytes 356360 | tf_op jit(solution)/shard_map/ppermute | solution.py:122
  17.8 1.5 %collective-permute-start.3 = (bf16[720,128]{1,0:T(8,128)(2,1)S(1)}, bf16[720,128]{1,0:T(8,128)(2,1)S(1)}, u32[]{:S(2)}, u32[]{:S(2)}) collective-permute-start(bf16[720,128]{1,0:T(8,128)(2,1)S(1)} %get-tuple-element.29), channel_id=1, source_target_pairs={{0,4},{4,0},{8,12},{12,8},{1,5},{5,1},{9,13},{13,9},{2,6},{6,2},{1... | collective-permute-start | bytes 552968 | tf_op jit(solution)/shard_map/ppermute | solution.py:122
  17.9 1.4 %collective-permute-start.4 = (bf16[720,128]{1,0:T(8,128)(2,1)S(1)}, bf16[720,128]{1,0:T(8,128)(2,1)S(1)}, u32[]{:S(2)}, u32[]{:S(2)}) collective-permute-start(bf16[720,128]{1,0:T(8,128)(2,1)S(1)} %get-tuple-element.30), channel_id=1, source_target_pairs={{4,8},{8,4},{5,9},{9,5},{6,10},{10,6},{7,11},{11,7},{20,24},{24,20... | collective-permute-start | bytes 552968 | tf_op jit(solution)/shard_map/ppermute | solution.py:122
  24.3 19.1 %all-to-all-start = ((bf16[32,24,128]{2,1,0:T(8,128)(2,1)}), bf16[32,24,128]{2,1,0:T(8,128)(2,1)S(1)}, u32[]{:S(2)}, u32[]{:S(2)}) async-start(bf16[32,24,128]{2,1,0:T(8,128)(2,1)} %get-tuple-element.32), calls=%async_computation | async-start | bytes 393216 | tf_op jit(solution)/shard_map/all_to_all | solution.py:804
  34.0 5.2 %collective-permute-start.6 = (bf16[128,128]{1,0:T(8,128)(2,1)S(1)}, bf16[128,128]{1,0:T(8,128)(2,1)S(1)}, u32[]{:S(2)}, u32[]{:S(2)}) collective-permute-start(bf16[128,128]{1,0:T(8,128)(2,1)S(1)} %get-tuple-element.35), channel_id=1, source_target_pairs={{1,2},{2,1},{5,6},{6,5},{9,10},{10,9},{13,14},{14,13},{17,18},{18,... | collective-permute-start | bytes 98312 | tf_op jit(solution)/shard_map/ppermute | solution.py:122
  34.7 6.6 %collective-permute-start.5 = (bf16[128,128]{1,0:T(8,128)(2,1)S(1)}, bf16[128,128]{1,0:T(8,128)(2,1)S(1)}, u32[]{:S(2)}, u32[]{:S(2)}) collective-permute-start(bf16[128,128]{1,0:T(8,128)(2,1)S(1)} %get-tuple-element.35), channel_id=1, source_target_pairs={{0,1},{1,0},{2,3},{3,2},{4,5},{5,4},{6,7},{7,6},{8,9},{9,8},{10,11... | collective-permute-start | bytes 98312 | tf_op jit(solution)/shard_map/ppermute | solution.py:122
  41.9 7.3 %collective-permute-start.7 = (bf16[560,128]{1,0:T(8,128)(2,1)S(1)}, bf16[560,128]{1,0:T(8,128)(2,1)S(1)}, u32[]{:S(2)}, u32[]{:S(2)}) collective-permute-start(bf16[560,128]{1,0:T(8,128)(2,1)S(1)} %get-tuple-element.37), channel_id=1, source_target_pairs={{0,16},{16,0},{1,17},{17,1},{2,18},{18,2},{3,19},{19,3},{4,20},{20... | collective-permute-start | bytes 430088 | tf_op jit(solution)/shard_map/ppermute | solution.py:122
  46.0 11.7 %all-to-all-start.1 = ((bf16[32,16,128]{2,1,0:T(8,128)(2,1)}), bf16[32,16,128]{2,1,0:T(8,128)(2,1)S(1)}, u32[]{:S(2)}, u32[]{:S(2)}) async-start(bf16[32,16,128]{2,1,0:T(8,128)(2,1)} %get-tuple-element.34), calls=%async_computation.1 | async-start | bytes 262144 | tf_op jit(solution)/shard_map/all_to_all | solution.py:804
  49.8 1.6 %collective-permute-start.8 = (bf16[896,128]{1,0:T(8,128)(2,1)S(1)}, bf16[896,128]{1,0:T(8,128)(2,1)S(1)}, u32[]{:S(2)}, u32[]{:S(2)}) collective-permute-start(bf16[896,128]{1,0:T(8,128)(2,1)S(1)} %get-tuple-element.39), channel_id=1, source_target_pairs={{0,4},{4,0},{8,12},{12,8},{1,5},{5,1},{9,13},{13,9},{2,6},{6,2},{1... | collective-permute-start | bytes 688136 | tf_op jit(solution)/shard_map/ppermute | solution.py:122
  50.1 1.2 %collective-permute-start.9 = (bf16[896,128]{1,0:T(8,128)(2,1)S(1)}, bf16[896,128]{1,0:T(8,128)(2,1)S(1)}, u32[]{:S(2)}, u32[]{:S(2)}) collective-permute-start(bf16[896,128]{1,0:T(8,128)(2,1)S(1)} %get-tuple-element.40), channel_id=1, source_target_pairs={{4,8},{8,4},{5,9},{9,5},{6,10},{10,6},{7,11},{11,7},{20,24},{24,20... | collective-permute-start | bytes 688136 | tf_op jit(solution)/shard_map/ppermute | solution.py:122
  64.2 13.9 %all-to-all-start.2 = ((bf16[32,16,128]{2,1,0:T(8,128)(2,1)}), bf16[32,16,128]{2,1,0:T(8,128)(2,1)S(1)}, u32[]{:S(2)}, u32[]{:S(2)}) async-start(bf16[32,16,128]{2,1,0:T(8,128)(2,1)} %get-tuple-element.46), calls=%async_computation.2 | async-start | bytes 262144 | tf_op jit(solution)/shard_map/all_to_all | solution.py:804

commit v6 on v5

--- a/solution.py
+++ b/solution.py
@@ -553,7 +553,7 @@
         tiles[:, pl.ds(pl.multiple_of(b * nodes, nodes), nodes)] = tile
         return _
 
-    lax.fori_loop(0, count, block, 0)
+    lax.fori_loop(0, count, block, 0, unroll=math.gcd(count, 4))
 
 
 def boundary_kernel(dims, count, scale, small, recv, sum_out, half_out, tiles):

time: 79.6 us -> 79.3 us (level)
  transfers between devices with their start and end apart: 13 -> 13, of which waited for: 7 -> 7; matrix products, arithmetic and copies ran while one was open for 0% -> 0% of each run, Pallas kernels for 7% -> 6%
where the time goes in v6:
time: 79.3 us; the launch traced here: 78.8 us
  starting transfers between devices  35 us (44%)
  waiting for transfers between devices  22.2 us (28%)
  Pallas kernels  18.9 us (24%)
  local copies, waits for them, and re-layouts  1.04 us (1%)
  other arithmetic  0.85 us (1%)
    pallas_call x10, Pallas kernels, kernel_call(): pl.pallas_call(body, out_shape=out_shape, in_specs=specs, out_specs=jax.t...  18.9 us
    all_to_all x3, starting transfers between devices, to_all(): return lax.all_to_all(value, AXES, 0, 0, tiled=True)  18.4 us
    ppermute x10, starting transfers between devices, exchange(): out.append(lax.ppermute(arrays[which], axis, pairs))  16.6 us
    all_to_all x3, waiting for transfers between devices, to_all(): return lax.all_to_all(value, AXES, 0, 0, tiled=True)  13.6 us
    ppermute x10, waiting for transfers between devices, exchange(): out.append(lax.ppermute(arrays[which], axis, pairs))  8.59 us
  transfers between devices with their start and end apart: 13, of which 7 were waited for; matrix products, arithmetic and copies ran while one was open for 0% of the time, Pallas kernels for 6%

profile of v6, /device:TPU:0, one launch (start us, length us, event | category | flops | bytes accessed | tf_op | source)
XLA Modules:
  0.0 78.8 jit_solution(7062051380580232549)
XLA Ops:
  0.6 0.8 convert_add_fusion.small.refs_1_
  1.4 0.0 copy-start
  1.4 1.0 %copy-done = f32[16,8,8,128]{3,2,1,0:T(8,128)S(1)} copy-done((f32[16,8,8,128]{3,2,1,0:T(8,128)S(1)}, f32[16,8,8,128]{3,2,1,0:T(8,128)}, u32[]{:S(2)}) %copy-start) | copy-done | bytes 524312
  2.5 0.7 scatter_first.1
  3.2 0.7 collective-permute-start.1
  3.9 5.9 %collective-permute-start = (bf16[144,128]{1,0:T(8,128)(2,1)S(1)}, bf16[144,128]{1,0:T(8,128)(2,1)S(1)}, u32[]{:S(2)}, u32[]{:S(2)}) collective-permute-start(bf16[144,128]{1,0:T(8,128)(2,1)S(1)} %get-tuple-element.26), channel_id=1, source_target_pairs={{0,1},{1,0},{2,3},{3,2},{4,5},{5,4},{6,7},{7,6},{8,9},{9,8},{10,11... | collective-permute-start | bytes 110600 | tf_op jit(solution)/shard_map/ppermute | solution.py:122
  9.8 0.1 pad_add_fusion.place
  9.9 0.0 collective-permute-done.1.refs_3_
  9.9 1.9 %collective-permute-done.refs_2_ = bf16[144,128]{1,0:T(8,128)(2,1)S(1)} collective-permute-done((bf16[144,128]{1,0:T(8,128)(2,1)S(1)}, bf16[144,128]{1,0:T(8,128)(2,1)S(1)}, u32[]{:S(2)}, u32[]{:S(2)}) %collective-permute-start) | collective-permute-done | bytes 36896 | tf_op jit(solution)/shard_map/ppermute | solution.py:122
  11.7 0.6 pack_x.2
  12.3 1.6 %collective-permute-start.2 = (bf16[464,128]{1,0:T(8,128)(2,1)S(1)}, bf16[464,128]{1,0:T(8,128)(2,1)S(1)}, u32[]{:S(2)}, u32[]{:S(2)}) collective-permute-start(bf16[464,128]{1,0:T(8,128)(2,1)S(1)} %get-tuple-element.28), channel_id=1, source_target_pairs={{0,16},{16,0},{1,17},{17,1},{2,18},{18,2},{3,19},{19,3},{4,20},{20... | collective-permute-start | bytes 356360 | tf_op jit(solution)/shard_map/ppermute | solution.py:122
  13.9 3.3 %collective-permute-done.2.refs_3_.refs_0_ = bf16[464,128]{1,0:T(8,128)(2,1)S(1)} collective-permute-done((bf16[464,128]{1,0:T(8,128)(2,1)S(1)}, bf16[464,128]{1,0:T(8,128)(2,1)S(1)}, u32[]{:S(2)}, u32[]{:S(2)}) %collective-permute-start.2) | collective-permute-done | bytes 118816 | tf_op jit(solution)/shard_map/ppermute | solution.py:122
  17.2 0.6 pack_y.2
  17.8 0.1 collective-permute-start.3
  17.9 0.7 collective-permute-start.4
  18.6 0.7 collective-permute-done.3.refs_1_
  19.3 0.0 collective-permute-done.4.refs_2_
  19.3 5.0 %sweeps_first.1 = (f32[1024,128]{1,0:T(8,128)S(1)}, bf16[32,24,128]{2,1,0:T(8,128)(2,1)}, bf16[128,128]{1,0:T(8,128)(2,1)S(1)}, f32[2228,128]{1,0:T(8,128)S(1)},...) custom-call(s32[3]{0:T(128)S(1)} %pad_add_fusion.place, f32[1024,128]{1,0:T(8,128)S(1)} %get-tuple-element.25.refs_0_.main, ...), custom_call_target="tpu_custom_call" | custom-call | tf_op jit(solution)/shard_map/sweeps_first/pallas_call | solution.py:45
  24.3 9.7 %all-to-all-start = ((bf16[32,24,128]{2,1,0:T(8,128)(2,1)}), bf16[32,24,128]{2,1,0:T(8,128)(2,1)S(1)}, u32[]{:S(2)}, u32[]{:S(2)}) async-start(bf16[32,24,128]{2,1,0:T(8,128)(2,1)} %get-tuple-element.32), calls=%async_computation | async-start | bytes 393216 | tf_op jit(solution)/shard_map/all_to_all | solution.py:804
  34.0 0.7 collective-permute-start.6
  34.7 4.5 %collective-permute-start.5 = (bf16[128,128]{1,0:T(8,128)(2,1)S(1)}, bf16[128,128]{1,0:T(8,128)(2,1)S(1)}, u32[]{:S(2)}, u32[]{:S(2)}) collective-permute-start(bf16[128,128]{1,0:T(8,128)(2,1)S(1)} %get-tuple-element.35), channel_id=1, source_target_pairs={{0,1},{1,0},{2,3},{3,2},{4,5},{5,4},{6,7},{7,6},{8,9},{9,8},{10,11... | collective-permute-start | bytes 98312 | tf_op jit(solution)/shard_map/ppermute | solution.py:122
  39.2 0.0 collective-permute-done.6.refs_2_
  39.3 2.1 %collective-permute-done.5.refs_1_ = bf16[128,128]{1,0:T(8,128)(2,1)S(1)} collective-permute-done((bf16[128,128]{1,0:T(8,128)(2,1)S(1)}, bf16[128,128]{1,0:T(8,128)(2,1)S(1)}, u32[]{:S(2)}, u32[]{:S(2)}) %collective-permute-start.5) | collective-permute-done | bytes 32800 | tf_op jit(solution)/shard_map/ppermute | solution.py:122
  41.3 0.6 pack_x.3
  41.9 1.5 %collective-permute-start.7 = (bf16[560,128]{1,0:T(8,128)(2,1)S(1)}, bf16[560,128]{1,0:T(8,128)(2,1)S(1)}, u32[]{:S(2)}, u32[]{:S(2)}) collective-permute-start(bf16[560,128]{1,0:T(8,128)(2,1)S(1)} %get-tuple-element.37), channel_id=1, source_target_pairs={{0,16},{16,0},{1,17},{17,1},{2,18},{18,2},{3,19},{19,3},{4,20},{20... | collective-permute-start | bytes 430088 | tf_op jit(solution)/shard_map/ppermute | solution.py:122
  43.5 0.0 all-to-all-done.recv.blocks
  43.5 2.2 %boundary.1 = (f32[16,128]{1,0:T(8,128)S(1)}, bf16[32,16,128]{2,1,0:T(8,128)(2,1)}) custom-call(f32[88,128]{1,0:T(8,128)S(1)} %convert_add_fusion.small.refs_1_, bf16[32,24,128]{2,1,0:T(8,128)(2,1)S(1)} %all-to-all-done.recv.blocks), custom_call_target="tpu_custom_call" | custom-call | tf_op jit(solution)/shard_map/boundary/pallas_call | solution.py:45
  45.6 3.2 %all-to-all-start.1 = ((bf16[32,16,128]{2,1,0:T(8,128)(2,1)}), bf16[32,16,128]{2,1,0:T(8,128)(2,1)S(1)}, u32[]{:S(2)}, u32[]{:S(2)}) async-start(bf16[32,16,128]{2,1,0:T(8,128)(2,1)} %get-tuple-element.34), calls=%async_computation.1 | async-start | bytes 262144 | tf_op jit(solution)/shard_map/all_to_all | solution.py:804
  48.9 0.0 collective-permute-done.7.refs_2_.refs_0_
  48.9 0.6 pack_y.3
  49.5 0.3 collective-permute-start.8
  49.8 0.7 collective-permute-start.9
  50.5 0.6 collective-permute-done.8.refs_1_
  51.1 0.0 collective-permute-done.9.refs_2_
  51.1 6.3 %all-to-all-done.1.recv = bf16[32,16,128]{2,1,0:T(8,128)(2,1)S(1)} async-done(((bf16[32,16,128]{2,1,0:T(8,128)(2,1)}), bf16[32,16,128]{2,1,0:T(8,128)(2,1)S(1)}, u32[]{:S(2)}, u32[]{:S(2)}) %all-to-all-start.1) | async-done | bytes 131104 | tf_op jit(solution)/shard_map/all_to_all | solution.py:804
  57.4 6.5 %sweeps_last.1 = (f32[1024,128]{1,0:T(8,128)}, bf16[32,16,128]{2,1,0:T(8,128)(2,1)}) custom-call(s32[3]{0:T(128)S(1)} %pad_add_fusion.place, f32[1024,128]{1,0:T(8,128)S(1)} %get-tuple-element.31.refs_0_.main, f32[16,128]{1,0:T(8,128)S(1)} %get-tuple-element.33.sums, f32[88,128]{1,0:T(8,128)S(1)} %convert_add_fusion.small.refs_1_, ...), custom_call_target="tpu_custom_call" | custom-call | tf_op jit(solution)/shard_map/sweeps_last/pallas_call | solution.py:45
  63.9 5.5 %all-to-all-start.2 = ((bf16[32,16,128]{2,1,0:T(8,128)(2,1)}), bf16[32,16,128]{2,1,0:T(8,128)(2,1)S(1)}, u32[]{:S(2)}, u32[]{:S(2)}) async-start(bf16[32,16,128]{2,1,0:T(8,128)(2,1)} %get-tuple-element.46), calls=%async_computation.2 | async-start | bytes 262144 | tf_op jit(solution)/shard_map/all_to_all | solution.py:804
  69.4 1.1 %tiles_last.1.tiles = bf16[128,4096]{1,0:T(8,128)(2,1)S(1)} custom-call(f32[88,128]{1,0:T(8,128)S(1)} %convert_add_fusion.small.refs_1_, bf16[32,24,128]{2,1,0:T(8,128)(2,1)S(1)} %all-to-all-done.recv.blocks), custom_call_target="tpu_custom_call" | custom-call | flops 1000000000 | bytes 1000000 | tf_op jit(solution)/shard_map/tiles_last/pallas_call | solution.py:45
  70.5 7.3 %all-to-all-done.2.recv = bf16[32,16,128]{2,1,0:T(8,128)(2,1)S(1)} async-done(((bf16[32,16,128]{2,1,0:T(8,128)(2,1)}), bf16[32,16,128]{2,1,0:T(8,128)(2,1)S(1)}, u32[]{:S(2)}, u32[]{:S(2)}) %all-to-all-start.2) | async-done | bytes 131104 | tf_op jit(solution)/shard_map/all_to_all | solution.py:804
  77.8 1.0 %flux_last.1 = f32[16,128]{1,0:T(8,128)} custom-call(f32[88,128]{1,0:T(8,128)S(1)} %convert_add_fusion.small.refs_1_, bf16[32,16,128]{2,1,0:T(8,128)(2,1)S(1)} %all-to-all-done.2.recv, bf16[128,4096]{1,0:T(8,128)(2,1)S(1)} %tiles_last.1.tiles), custom_call_target="tpu_custom_call" | custom-call | tf_op jit(solution)/shard_map/flux_last/pallas_call | solution.py:45
Async XLA Ops:
  1.4 1.0 %copy-start = (f32[16,8,8,128]{3,2,1,0:T(8,128)S(1)}, f32[16,8,8,128]{3,2,1,0:T(8,128)}, u32[]{:S(2)}) copy-start(f32[16,8,8,128]{3,2,1,0:T(8,128)} %param.6) | copy-start | bytes 1572868
  3.2 6.7 %collective-permute-start.1 = (bf16[144,128]{1,0:T(8,128)(2,1)S(1)}, bf16[144,128]{1,0:T(8,128)(2,1)S(1)}, u32[]{:S(2)}, u32[]{:S(2)}) collective-permute-start(bf16[144,128]{1,0:T(8,128)(2,1)S(1)} %get-tuple-element.26), channel_id=1, source_target_pairs={{1,2},{2,1},{5,6},{6,5},{9,10},{10,9},{13,14},{14,13},{17,18},{18,... | collective-permute-start | bytes 110600 | tf_op jit(solution)/shard_map/ppermute | solution.py:122
  3.9 7.8 %collective-permute-start = (bf16[144,128]{1,0:T(8,128)(2,1)S(1)}, bf16[144,128]{1,0:T(8,128)(2,1)S(1)}, u32[]{:S(2)}, u32[]{:S(2)}) collective-permute-start(bf16[144,128]{1,0:T(8,128)(2,1)S(1)} %get-tuple-element.26), channel_id=1, source_target_pairs={{0,1},{1,0},{2,3},{3,2},{4,5},{5,4},{6,7},{7,6},{8,9},{9,8},{10,11... | collective-permute-start | bytes 110600 | tf_op jit(solution)/shard_map/ppermute | solution.py:122
  12.3 4.9 %collective-permute-start.2 = (bf16[464,128]{1,0:T(8,128)(2,1)S(1)}, bf16[464,128]{1,0:T(8,128)(2,1)S(1)}, u32[]{:S(2)}, u32[]{:S(2)}) collective-permute-start(bf16[464,128]{1,0:T(8,128)(2,1)S(1)} %get-tuple-element.28), channel_id=1, source_target_pairs={{0,16},{16,0},{1,17},{17,1},{2,18},{18,2},{3,19},{19,3},{4,20},{20... | collective-permute-start | bytes 356360 | tf_op jit(solution)/shard_map/ppermute | solution.py:122
  17.8 1.5 %collective-permute-start.3 = (bf16[720,128]{1,0:T(8,128)(2,1)S(1)}, bf16[720,128]{1,0:T(8,128)(2,1)S(1)}, u32[]{:S(2)}, u32[]{:S(2)}) collective-permute-start(bf16[720,128]{1,0:T(8,128)(2,1)S(1)} %get-tuple-element.29), channel_id=1, source_target_pairs={{0,4},{4,0},{8,12},{12,8},{1,5},{5,1},{9,13},{13,9},{2,6},{6,2},{1... | collective-permute-start | bytes 552968 | tf_op jit(solution)/shard_map/ppermute | solution.py:122
  17.9 1.4 %collective-permute-start.4 = (bf16[720,128]{1,0:T(8,128)(2,1)S(1)}, bf16[720,128]{1,0:T(8,128)(2,1)S(1)}, u32[]{:S(2)}, u32[]{:S(2)}) collective-permute-start(bf16[720,128]{1,0:T(8,128)(2,1)S(1)} %get-tuple-element.30), channel_id=1, source_target_pairs={{4,8},{8,4},{5,9},{9,5},{6,10},{10,6},{7,11},{11,7},{20,24},{24,20... | collective-permute-start | bytes 552968 | tf_op jit(solution)/shard_map/ppermute | solution.py:122
  24.3 19.1 %all-to-all-start = ((bf16[32,24,128]{2,1,0:T(8,128)(2,1)}), bf16[32,24,128]{2,1,0:T(8,128)(2,1)S(1)}, u32[]{:S(2)}, u32[]{:S(2)}) async-start(bf16[32,24,128]{2,1,0:T(8,128)(2,1)} %get-tuple-element.32), calls=%async_computation | async-start | bytes 393216 | tf_op jit(solution)/shard_map/all_to_all | solution.py:804
  34.0 5.2 %collective-permute-start.6 = (bf16[128,128]{1,0:T(8,128)(2,1)S(1)}, bf16[128,128]{1,0:T(8,128)(2,1)S(1)}, u32[]{:S(2)}, u32[]{:S(2)}) collective-permute-start(bf16[128,128]{1,0:T(8,128)(2,1)S(1)} %get-tuple-element.35), channel_id=1, source_target_pairs={{1,2},{2,1},{5,6},{6,5},{9,10},{10,9},{13,14},{14,13},{17,18},{18,... | collective-permute-start | bytes 98312 | tf_op jit(solution)/shard_map/ppermute | solution.py:122
  34.7 6.6 %collective-permute-start.5 = (bf16[128,128]{1,0:T(8,128)(2,1)S(1)}, bf16[128,128]{1,0:T(8,128)(2,1)S(1)}, u32[]{:S(2)}, u32[]{:S(2)}) collective-permute-start(bf16[128,128]{1,0:T(8,128)(2,1)S(1)} %get-tuple-element.35), channel_id=1, source_target_pairs={{0,1},{1,0},{2,3},{3,2},{4,5},{5,4},{6,7},{7,6},{8,9},{9,8},{10,11... | collective-permute-start | bytes 98312 | tf_op jit(solution)/shard_map/ppermute | solution.py:122
  41.9 7.0 %collective-permute-start.7 = (bf16[560,128]{1,0:T(8,128)(2,1)S(1)}, bf16[560,128]{1,0:T(8,128)(2,1)S(1)}, u32[]{:S(2)}, u32[]{:S(2)}) collective-permute-start(bf16[560,128]{1,0:T(8,128)(2,1)S(1)} %get-tuple-element.37), channel_id=1, source_target_pairs={{0,16},{16,0},{1,17},{17,1},{2,18},{18,2},{3,19},{19,3},{4,20},{20... | collective-permute-start | bytes 430088 | tf_op jit(solution)/shard_map/ppermute | solution.py:122
  45.6 11.7 %all-to-all-start.1 = ((bf16[32,16,128]{2,1,0:T(8,128)(2,1)}), bf16[32,16,128]{2,1,0:T(8,128)(2,1)S(1)}, u32[]{:S(2)}, u32[]{:S(2)}) async-start(bf16[32,16,128]{2,1,0:T(8,128)(2,1)} %get-tuple-element.34), calls=%async_computation.1 | async-start | bytes 262144 | tf_op jit(solution)/shard_map/all_to_all | solution.py:804
  49.5 1.6 %collective-permute-start.8 = (bf16[896,128]{1,0:T(8,128)(2,1)S(1)}, bf16[896,128]{1,0:T(8,128)(2,1)S(1)}, u32[]{:S(2)}, u32[]{:S(2)}) collective-permute-start(bf16[896,128]{1,0:T(8,128)(2,1)S(1)} %get-tuple-element.39), channel_id=1, source_target_pairs={{0,4},{4,0},{8,12},{12,8},{1,5},{5,1},{9,13},{13,9},{2,6},{6,2},{1... | collective-permute-start | bytes 688136 | tf_op jit(solution)/shard_map/ppermute | solution.py:122
  49.8 1.2 %collective-permute-start.9 = (bf16[896,128]{1,0:T(8,128)(2,1)S(1)}, bf16[896,128]{1,0:T(8,128)(2,1)S(1)}, u32[]{:S(2)}, u32[]{:S(2)}) collective-permute-start(bf16[896,128]{1,0:T(8,128)(2,1)S(1)} %get-tuple-element.40), channel_id=1, source_target_pairs={{4,8},{8,4},{5,9},{9,5},{6,10},{10,6},{7,11},{11,7},{20,24},{24,20... | collective-permute-start | bytes 688136 | tf_op jit(solution)/shard_map/ppermute | solution.py:122
  63.9 13.9 %all-to-all-start.2 = ((bf16[32,16,128]{2,1,0:T(8,128)(2,1)}), bf16[32,16,128]{2,1,0:T(8,128)(2,1)S(1)}, u32[]{:S(2)}, u32[]{:S(2)}) async-start(bf16[32,16,128]{2,1,0:T(8,128)(2,1)} %get-tuple-element.46), calls=%async_computation.2 | async-start | bytes 262144 | tf_op jit(solution)/shard_map/all_to_all | solution.py:804
